TPU v7x, 256 devices: a whole 4x4x8 slice. The times are simulated.
256 devices in a mesh: leaf: 64 (over x, z, core), blk: 4 (over y).
Axes of the slice: x: 4, y: 4, z: 8, core: 2. Of those that a mesh axis runs over, the one named last changes fastest.
Arguments:
- sources: bfloat16 [128, 1048576], P(None, ('leaf', 'blk')), may hold values from -6 to 6
- near_blocks: bfloat16 [8192, 6, 128, 128], P(('leaf', 'blk')), may hold values from -0.21875 to 0.21875
- near_cols: int32 [8192, 6], P(('leaf', 'blk')), may hold values from 0 to 8191, as said below
- basis: bfloat16 [8192, 64, 128], P(('leaf', 'blk')), may hold values from -0.046875 to 0.046875
- transfer: bfloat16 [126, 64, 64], replicated, may hold values from -0.75 to 0.75
- coupling: bfloat16 [126, 64, 64], replicated, may hold values from -0.75 to 0.75
Outputs:
- potential: float32 [128, 1048576], P(None, ('leaf', 'blk'))
Inputs may be any that keep to these rules, and one draw needn't show every extreme that they name: `near_cols`: for cluster c the entries are c, min(c + 4, 8191), max(c - 4, 0), then entries within 4 clusters of c, clipped to the grid of clusters.
All inputs are finite; a program needn't handle non-finite values.
Results may differ from a plain program's by a relative error of at most 0.0012.
Values may be sent and summed in bfloat16 or wider, within the bound.
No kernel may reach another device: no remote copies, remote signals or barrier semaphores. Data moves between devices by JAX's collectives and lax.ppermute only.
A program may use at most 128 MiB of HBM per device.

v0:
```python
import jax
import jax.numpy as jnp
from jax import lax
from jax.sharding import PartitionSpec as P

REACH = 4


highest = lax.Precision.HIGHEST


def padded(cells, sides, width):
    for axis, dim in sides:
        count = lax.axis_size(axis)
        ends = count - 1
        head = lax.slice_in_dim(cells, 0, width, axis=dim)
        tail = lax.slice_in_dim(cells, cells.shape[dim] - width, cells.shape[dim], axis=dim)
        cells = jnp.concatenate(
            [
                lax.ppermute(tail, axis, [(i, (i + 1) % count) for i in range(ends)]),
                cells,
                lax.ppermute(head, axis, [((i + 1) % count, i) for i in range(ends)]),
            ],
            axis=dim,
        )
    return cells


def from_partner(value, axis, distance):
    mask = 2**distance
    pairs = [(source, source ^ mask) for source in range(lax.axis_size(axis))]
    return lax.ppermute(value, axis, pairs)


def pick_matrix(table, table_row):
    return lax.dynamic_index_in_dim(table, table_row, 0, keepdims=False).astype(jnp.float32)


def body(sources, near_blocks, near_cols, basis, transfer, coupling):
    rhs_count = sources.shape[0]
    own_clusters = near_blocks.shape[0]
    near_count = near_blocks.shape[1]
    panel_size = near_blocks.shape[2]
    leaf_count = lax.axis_size("leaf")
    levels = leaf_count.bit_length() - 1
    leaf_index = lax.axis_index("leaf")
    extended = padded(sources, ((("leaf", "blk"), 1),), REACH * panel_size)
    by_cluster = jnp.transpose(
        extended.reshape(rhs_count, own_clusters + 2 * REACH, panel_size), (1, 0, 2)
    )
    own_sources = by_cluster[REACH : REACH + own_clusters]
    partial_value = jnp.einsum(
        "crp,ckp->rk", own_sources, basis, preferred_element_type=jnp.float32
    )
    moment = lax.psum(partial_value, "blk")
    first_cluster = lax.axis_index(("leaf", "blk")) * own_clusters
    local_columns = near_cols - (first_cluster - REACH)
    near = jnp.zeros((own_clusters, rhs_count, panel_size), jnp.float32)
    for slot in range(near_count):
        picked = jnp.take(by_cluster, local_columns[:, slot], axis=0)
        near = near + jnp.einsum(
            "crp,cpq->crq", picked, near_blocks[:, slot], preferred_element_type=jnp.float32
        )
    siblings = []
    current = moment
    for level in range(levels):
        sibling_moment = from_partner(current, "leaf", level)
        siblings.append(sibling_moment)
        if level + 1 < levels:
            node_count = leaf_count >> level
            node_index = leaf_index >> level
            mine = pick_matrix(transfer, node_count - 2 + node_index)
            theirs = pick_matrix(transfer, node_count - 2 + (node_index ^ 1))
            current = jnp.dot(current, mine, precision=highest) + jnp.dot(
                sibling_moment, theirs, precision=highest
            )
    local_terms = []
    for level in range(levels):
        node_count = leaf_count >> level
        couple = pick_matrix(coupling, node_count - 2 + (leaf_index >> level))
        local_terms.append(jnp.dot(siblings[level], couple, precision=highest))
    descended = local_terms[levels - 1]
    for level in range(levels - 2, -1, -1):
        node_count = leaf_count >> level
        up_matrix = pick_matrix(transfer, node_count - 2 + (leaf_index >> level))
        descended = local_terms[level] + jnp.dot(descended, up_matrix.T, precision=highest)
    leaf_local = descended.astype(jnp.bfloat16)
    far = jnp.einsum("rk,ckp->crp", leaf_local, basis, preferred_element_type=jnp.float32)
    total = near + far
    return jnp.transpose(total, (1, 0, 2)).reshape(rhs_count, own_clusters * panel_size)


def solution(mesh):
    return jax.shard_map(
        body,
        mesh=mesh,
        in_specs=(
            P(None, ("leaf", "blk")),
            P(("leaf", "blk"), None, None, None),
            P(("leaf", "blk"), None),
            P(("leaf", "blk"), None, None),
            P(),
            P(),
        ),
        out_specs=P(None, ("leaf", "blk")),
        check_vma=False,
    )
```

profile of v0, /device:TPU:6, one launch (start us, length us, event | category | flops | bytes accessed | tf_op | source)
XLA Modules:
  0.0 127.6 jit_solution(17000539796109426428)
XLA Ops:
  0.0 1.7 %copy.14 = bf16[128,4096]{0,1:T(8,128)(2,1)S(1)} copy(bf16[128,4096]{1,0:T(8,128)(2,1)} %param.8) | data formatting | bytes 2097152 | tf_op args[0]
  1.8 3.5 %collective-permute-start = (bf16[128,512]{0,1:T(8,128)(2,1)S(1)}, bf16[128,512]{0,1:T(8,128)(2,1)S(1)}, u32[]{:S(2)}, u32[]{:S(2)}) collective-permute-start(bf16[128,512]{0,1:T(8,128)(2,1)S(1)} %get-tuple-element.34), channel_id=1, source_target_pairs={{0,1},{1,2},{2,3},{3,4},{4,5},{5,6},{6,7},{7,8},{8,9},{9,10},{10,1... | collective-permute-start | bytes 393224 | tf_op jit(solution)/shard_map/ppermute | solution.py:20
  5.3 8.4 %collective-permute-start.1 = (bf16[128,512]{0,1:T(8,128)(2,1)S(1)}, bf16[128,512]{0,1:T(8,128)(2,1)S(1)}, u32[]{:S(2)}, u32[]{:S(2)}) collective-permute-start(bf16[128,512]{0,1:T(8,128)(2,1)S(1)} %get-tuple-element.35), channel_id=1, source_target_pairs={{1,0},{2,1},{3,2},{4,3},{5,4},{6,5},{7,6},{8,7},{9,8},{10,9},{11,1... | collective-permute-start | bytes 393224 | tf_op jit(solution)/shard_map/ppermute | solution.py:22
  13.8 4.6 %constant_dynamic-slice_fusion.15 = (bf16[1,64,64]{0,2,1:T(8,128)(2,1)}, bf16[1,64,64]{0,2,1:T(8,128)(2,1)}, bf16[1,64,64]{0,2,1:T(8,128)(2,1)}, bf16[1,64,64]{0...) fusion(bf16[126,64,64]{0,2,1:T(8,128)(2,1)S(1)} %copy-done.2, s32[]{:T(128)S(6)} %select_n.51, ...), kind=kLoop, calls=%fused_computation.109 | loop fusion | bytes 98328 | tf_op jit(solution)/shard_map/jit(dynamic_index_in_dim)/dynamic_slice | solution.py:36
  18.4 7.1 %constant_dynamic-slice_fusion.1 = (bf16[1,64,64]{0,2,1:T(8,128)(2,1)S(1)}, bf16[1,64,64]{0,2,1:T(8,128)(2,1)}, bf16[1,64,64]{0,2,1:T(8,128)(2,1)}, bf16[1,64,64...) fusion(bf16[126,64,64]{0,2,1:T(8,128)(2,1)S(1)} %copy-done.1, ...), kind=kLoop, calls=%fused_computation.95 | loop fusion | bytes 163880 | tf_op jit(solution)/shard_map/jit(dynamic_index_in_dim)/dynamic_slice | solution.py:36
  25.6 1.7 %copy.48 = bf16[1,64,64]{2,1,0:T(8,128)(2,1)S(1)} copy(bf16[1,64,64]{0,2,1:T(8,128)(2,1)} %get-tuple-element.33) | data formatting | bytes 16384
  27.3 1.7 %copy.49 = bf16[1,64,64]{2,1,0:T(8,128)(2,1)S(1)} copy(bf16[1,64,64]{0,2,1:T(8,128)(2,1)} %get-tuple-element.32) | data formatting | bytes 16384
  28.9 1.7 %copy.51 = bf16[1,64,64]{2,1,0:T(8,128)(2,1)S(1)} copy(bf16[1,64,64]{0,2,1:T(8,128)(2,1)} %get-tuple-element.31) | data formatting | bytes 16384
  30.6 1.7 %copy.52 = bf16[1,64,64]{2,1,0:T(8,128)(2,1)S(1)} copy(bf16[1,64,64]{0,2,1:T(8,128)(2,1)} %get-tuple-element.30) | data formatting | bytes 16384
  32.3 1.7 %copy.54 = bf16[1,64,64]{2,1,0:T(8,128)(2,1)S(1)} copy(bf16[1,64,64]{0,2,1:T(8,128)(2,1)} %get-tuple-element.29) | data formatting | bytes 16384
  34.0 1.7 %copy.55 = bf16[1,64,64]{2,1,0:T(8,128)(2,1)S(1)} copy(bf16[1,64,64]{0,2,1:T(8,128)(2,1)} %get-tuple-element.28) | data formatting | bytes 16384
  35.7 1.7 %copy.57 = bf16[1,64,64]{2,1,0:T(8,128)(2,1)S(1)} copy(bf16[1,64,64]{0,2,1:T(8,128)(2,1)} %get-tuple-element.27) | data formatting | bytes 16384
  37.3 1.7 %copy.58 = bf16[1,64,64]{2,1,0:T(8,128)(2,1)S(1)} copy(bf16[1,64,64]{0,2,1:T(8,128)(2,1)} %get-tuple-element.26) | data formatting | bytes 16384
  39.0 1.7 %copy.60 = bf16[1,64,64]{2,1,0:T(8,128)(2,1)S(1)} copy(bf16[1,64,64]{0,2,1:T(8,128)(2,1)} %get-tuple-element.25) | data formatting | bytes 16384
  40.7 0.5 copy.61
  41.2 1.7 %copy.62 = bf16[1,64,64]{2,1,0:T(8,128)(2,1)S(1)} copy(bf16[1,64,64]{0,2,1:T(8,128)(2,1)} %get-tuple-element.23) | data formatting | bytes 16384
  42.9 1.8 %copy.59 = bf16[1,64,64]{2,1,0:T(8,128)(2,1)S(1)} copy(bf16[1,64,64]{0,2,1:T(8,128)(2,1)} %get-tuple-element.19) | data formatting | bytes 16384
  44.6 1.7 %copy.56 = bf16[1,64,64]{2,1,0:T(8,128)(2,1)S(1)} copy(bf16[1,64,64]{0,2,1:T(8,128)(2,1)} %get-tuple-element.20) | data formatting | bytes 16384
  46.3 1.7 %copy.53 = bf16[1,64,64]{2,1,0:T(8,128)(2,1)S(1)} copy(bf16[1,64,64]{0,2,1:T(8,128)(2,1)} %get-tuple-element.21) | data formatting | bytes 16384
  48.0 1.7 %copy.50 = bf16[1,64,64]{2,1,0:T(8,128)(2,1)S(1)} copy(bf16[1,64,64]{0,2,1:T(8,128)(2,1)} %get-tuple-element.22) | data formatting | bytes 16384
  49.7 0.5 copy.47
  50.2 1.1 pad_maximum_fusion
  51.3 1.8 %copy.17 = bf16[128,40,128]{2,0,1:T(8,128)(2,1)S(1)} copy(bf16[128,40,128]{0,2,1:T(8,128)(2,1)} %bitcast.143) | data formatting | bytes 2621440 | tf_op jit(solution)/shard_map/reshape | solution.py:49
  53.1 0.5 convolution_bitcast_fusion
  53.6 14.4 %psum.7 = f32[128,64]{0,1:T(8,128)S(1)} all-reduce(f32[128,64]{0,1:T(8,128)S(1)} %convolution_bitcast_fusion), channel_id=1, replica_groups=mesh['leaf'=64,'blk'=4] {'blk'}, use_global_device_ids=true, to_apply=%region_0.2 | all-reduce | flops 8192 | bytes 65536 | tf_op jit(solution)/shard_map/psum | solution.py:55
  68.0 0.3 collective-permute-start.2
  68.3 1.7 %gather_fusion.4 = bf16[32,128,128]{2,1,0:T(8,128)(2,1)} fusion(bf16[40,128,128]{2,1,0:T(8,128)(2,1)S(1)} %bitcast.136, s32[1024]{0:T(1024)S(1)} %get-tuple-element.46), kind=kCustom, calls=%fused_computation.4.clone | custom fusion | bytes 2097280 | tf_op jit(solution)/shard_map/jit(_take)/gather | solution.py:60
  70.0 1.7 %gather_fusion.3 = bf16[32,128,128]{2,1,0:T(8,128)(2,1)} fusion(bf16[40,128,128]{2,1,0:T(8,128)(2,1)S(1)} %bitcast.137, s32[1024]{0:T(1024)S(1)} %get-tuple-element.47), kind=kCustom, calls=%fused_computation.3.clone | custom fusion | bytes 2097280 | tf_op jit(solution)/shard_map/jit(_take)/gather | solution.py:60
  71.6 0.7 gather_fusion.2
  72.4 1.7 %gather_fusion.1 = bf16[32,128,128]{2,1,0:T(8,128)(2,1)} fusion(bf16[40,128,128]{2,1,0:T(8,128)(2,1)S(1)} %bitcast.139, s32[1024]{0:T(1024)S(1)} %get-tuple-element.49), kind=kCustom, calls=%fused_computation.1.clone | custom fusion | bytes 2097280 | tf_op jit(solution)/shard_map/jit(_take)/gather | solution.py:60
  74.0 3.9 %fusion.3 = f32[32,128,128]{1,2,0:T(8,128)} fusion(bf16[32,128,128]{2,1,0:T(8,128)(2,1)} %gather_fusion.4, bf16[32,6,128,128]{3,2,1,0:T(8,128)(2,1)} %param.9, pred[32]{0:T(512)(128)(4,1)S(1)} %get-tuple-element.36), kind=kOutput, calls=%fused_computation.22 | convolution fusion | flops 134742016 | bytes 4194336 | tf_op jit(solution)/shard_map/crp,cpq->crq/dot_general | solution.py:61
  77.9 3.5 %fusion.5 = f32[32,128,128]{1,2,0:T(8,128)} fusion(bf16[32,128,128]{2,1,0:T(8,128)(2,1)S(1)} %copy-done.6, bf16[32,6,128,128]{3,2,1,0:T(8,128)(2,1)} %param.9, pred[32]{0:T(512)(128)(4,1)S(1)} %get-tuple-element.38), kind=kOutput, calls=%fused_computation.24 | convolution fusion | flops 134742016 | bytes 4194336 | tf_op jit(solution)/shard_map/crp,cpq->crq/dot_general | solution.py:61
  81.4 3.5 %fusion.7 = f32[32,128,128]{1,2,0:T(8,128)} fusion(bf16[32,128,128]{2,1,0:T(8,128)(2,1)S(1)} %gather_fusion.2, bf16[32,6,128,128]{3,2,1,0:T(8,128)(2,1)} %param.9, pred[32]{0:T(512)(128)(4,1)S(1)} %get-tuple-element.40), kind=kOutput, calls=%fused_computation.26 | convolution fusion | flops 134742016 | bytes 4194336 | tf_op jit(solution)/shard_map/crp,cpq->crq/dot_general | solution.py:61
  84.9 3.5 %fusion.9 = f32[32,128,128]{1,2,0:T(8,128)} fusion(bf16[32,128,128]{2,1,0:T(8,128)(2,1)S(1)} %copy-done.5, bf16[32,6,128,128]{3,2,1,0:T(8,128)(2,1)} %param.9, pred[32]{0:T(512)(128)(4,1)S(1)} %get-tuple-element.42), kind=kOutput, calls=%fused_computation.28 | convolution fusion | flops 134742016 | bytes 4194336 | tf_op jit(solution)/shard_map/crp,cpq->crq/dot_general | solution.py:61
  88.6 0.7 gather_fusion
  89.9 3.7 %collective-permute-done.3 = f32[128,64]{0,1:T(8,128)S(1)} collective-permute-done((f32[128,64]{0,1:T(8,128)S(1)}, f32[128,64]{0,1:T(8,128)S(1)}, u32[]{:S(2)}, u32[]{:S(2)}) %collective-permute-start.3) | collective-permute-done | bytes 32800 | tf_op jit(solution)/shard_map/ppermute | solution.py:32
  93.8 0.3 collective-permute-start.4
  94.3 4.4 %collective-permute-done.4 = f32[128,64]{0,1:T(8,128)S(1)} collective-permute-done((f32[128,64]{0,1:T(8,128)S(1)}, f32[128,64]{0,1:T(8,128)S(1)}, u32[]{:S(2)}, u32[]{:S(2)}) %collective-permute-start.4) | collective-permute-done | bytes 32800 | tf_op jit(solution)/shard_map/ppermute | solution.py:32
  98.9 4.3 %collective-permute-start.5 = (f32[128,64]{0,1:T(8,128)S(1)}, f32[128,64]{0,1:T(8,128)S(1)}, u32[]{:S(2)}, u32[]{:S(2)}) collective-permute-start(f32[128,64]{0,1:T(8,128)S(1)} %convolution_add_fusion.6), channel_id=1, source_target_pairs={{0,32},{4,36},{8,40},{12,44},{16,48},{20,52},{24,56},{28,60},{32,0... | collective-permute-start | bytes 98312 | tf_op jit(solution)/shard_map/ppermute | solution.py:32
  103.4 3.6 %collective-permute-done.5 = f32[128,64]{0,1:T(8,128)S(1)} collective-permute-done((f32[128,64]{0,1:T(8,128)S(1)}, f32[128,64]{0,1:T(8,128)S(1)}, u32[]{:S(2)}, u32[]{:S(2)}) %collective-permute-start.5) | collective-permute-done | bytes 32800 | tf_op jit(solution)/shard_map/ppermute | solution.py:32
  107.2 0.8 collective-permute-start.6
  108.3 3.0 %collective-permute-done.6 = f32[128,64]{0,1:T(8,128)S(1)} collective-permute-done((f32[128,64]{0,1:T(8,128)S(1)}, f32[128,64]{0,1:T(8,128)S(1)}, u32[]{:S(2)}, u32[]{:S(2)}) %collective-permute-start.6) | collective-permute-done | bytes 32800 | tf_op jit(solution)/shard_map/ppermute | solution.py:32
  111.5 1.3 %collective-permute-start.7 = (f32[128,64]{1,0:T(8,128)S(1)}, f32[128,64]{1,0:T(8,128)S(1)}, u32[]{:S(2)}, u32[]{:S(2)}) collective-permute-start(f32[128,64]{1,0:T(8,128)S(1)} %convolution_add_fusion), channel_id=1, source_target_pairs={{0,128},{4,132},{8,136},{12,140},{16,144},{20,148},{24,152},{28,15... | collective-permute-start | bytes 98312 | tf_op jit(solution)/shard_map/ppermute | solution.py:32
  112.8 3.5 %fusion.11 = f32[32,128,128]{1,2,0:T(8,128)} fusion(bf16[32,128,128]{2,1,0:T(8,128)(2,1)S(1)} %gather_fusion, bf16[32,6,128,128]{3,2,1,0:T(8,128)(2,1)} %param.9, pred[32]{0:T(512)(128)(4,1)S(1)} %get-tuple-element.44), kind=kOutput, calls=%fused_computation.30 | convolution fusion | flops 134742016 | bytes 4194336 | tf_op jit(solution)/shard_map/crp,cpq->crq/dot_general | solution.py:61
  116.3 1.8 %gather_fusion.5 = bf16[32,128,128]{2,1,0:T(8,128)(2,1)} fusion(bf16[40,128,128]{2,1,0:T(8,128)(2,1)S(1)} %bitcast.141, s32[1024]{0:T(1024)S(1)} %pad_clamp_fusion), kind=kCustom, calls=%fused_computation.5.clone | custom fusion | bytes 2097280 | tf_op jit(solution)/shard_map/jit(_take)/gather | solution.py:60
  120.4 0.5 fusion.77
  121.0 4.7 %bitcast_add_fusion = f32[128,32,128]{0,2,1:T(8,128)S(1)} fusion(f32[128,32,128]{0,2,1:T(8,128)S(1)} %fusion.77, f32[32,128,128]{1,2,0:T(8,128)S(1)} %copy-done.3, f32[32,128,128]{1,2,0:T(8,128)S(1)} %copy-done.4, f32[32,128,128]{1,2,0:T(8,128)} %fusion.7, f32[32,128,128]{1,2,0:T(8,128)} %fusion.11, f32[32,128,128]{1,2,0:T(8,128)} %fusion.9, ...), kind=kOutput, calls=%fused_computation.6 | convolution fusion | flops 137887744 | bytes 16777248 | tf_op jit(solution)/shard_map/crp,cpq->crq/dot_general | solution.py:61
  125.8 1.8 %copy.40 = f32[128,4096]{1,0:T(8,128)} copy(f32[128,4096]{0,1:T(8,128)S(1)} %bitcast.142) | data formatting | bytes 4194304 | tf_op jit(solution)/shard_map/reshape | solution.py:90
  (51 shorter events, 4.6 us)
Async XLA Ops:
  0.0 53.1 %copy-start = (bf16[32,64,128]{2,1,0:T(8,128)(2,1)S(1)}, bf16[32,64,128]{2,1,0:T(8,128)(2,1)}, u32[]{:S(2)}) copy-start(bf16[32,64,128]{2,1,0:T(8,128)(2,1)} %param.11) | copy-start | bytes 1572868
  0.0 13.7 %copy-start.8 = (s32[32,6]{0,1:T(8,128)S(1)}, s32[32,6]{0,1:T(8,128)}, u32[]{:S(2)}) copy-start(s32[32,6]{0,1:T(8,128)} %param.10) | copy-start | bytes 2308
  0.0 13.8 %copy-start.2 = (bf16[126,64,64]{0,2,1:T(8,128)(2,1)S(1)}, bf16[126,64,64]{0,2,1:T(8,128)(2,1)}, u32[]{:S(2)}) copy-start(bf16[126,64,64]{0,2,1:T(8,128)(2,1)} %param.13) | copy-start | bytes 3096580
  1.8 48.4 %collective-permute-start = (bf16[128,512]{0,1:T(8,128)(2,1)S(1)}, bf16[128,512]{0,1:T(8,128)(2,1)S(1)}, u32[]{:S(2)}, u32[]{:S(2)}) collective-permute-start(bf16[128,512]{0,1:T(8,128)(2,1)S(1)} %get-tuple-element.34), channel_id=1, source_target_pairs={{0,1},{1,2},{2,3},{3,4},{4,5},{5,6},{6,7},{7,8},{8,9},{9,10},{10,1... | collective-permute-start | bytes 393224 | tf_op jit(solution)/shard_map/ppermute | solution.py:20
  5.3 44.9 %collective-permute-start.1 = (bf16[128,512]{0,1:T(8,128)(2,1)S(1)}, bf16[128,512]{0,1:T(8,128)(2,1)S(1)}, u32[]{:S(2)}, u32[]{:S(2)}) collective-permute-start(bf16[128,512]{0,1:T(8,128)(2,1)S(1)} %get-tuple-element.35), channel_id=1, source_target_pairs={{1,0},{2,1},{3,2},{4,3},{5,4},{6,5},{7,6},{8,7},{9,8},{10,9},{11,1... | collective-permute-start | bytes 393224 | tf_op jit(solution)/shard_map/ppermute | solution.py:22
  13.8 4.7 %copy-start.1 = (bf16[126,64,64]{0,2,1:T(8,128)(2,1)S(1)}, bf16[126,64,64]{0,2,1:T(8,128)(2,1)}, u32[]{:S(2)}) copy-start(bf16[126,64,64]{0,2,1:T(8,128)(2,1)} %param.12) | copy-start | bytes 3096580
  42.9 6.8 %copy-start.7 = (bf16[1,64,64]{0,2,1:T(8,128)(2,1)S(1)}, bf16[1,64,64]{0,2,1:T(8,128)(2,1)}, u32[]{:S(2)}) copy-start(bf16[1,64,64]{0,2,1:T(8,128)(2,1)} %get-tuple-element.18) | copy-start | bytes 24580
  68.0 21.3 %collective-permute-start.2 = (f32[128,64]{0,1:T(8,128)S(1)}, f32[128,64]{0,1:T(8,128)S(1)}, u32[]{:S(2)}, u32[]{:S(2)}) collective-permute-start(f32[128,64]{0,1:T(8,128)S(1)} %psum.7), channel_id=1, source_target_pairs={{0,4},{4,0},{8,12},{12,8},{16,20},{20,16},{24,28},{28,24},{32,36},... | collective-permute-start | bytes 98312 | tf_op jit(solution)/shard_map/ppermute | solution.py:32
  74.0 3.9 %copy-start.6 = (bf16[32,128,128]{2,1,0:T(8,128)(2,1)S(1)}, bf16[32,128,128]{2,1,0:T(8,128)(2,1)}, u32[]{:S(2)}) copy-start(bf16[32,128,128]{2,1,0:T(8,128)(2,1)} %gather_fusion.3) | copy-start | bytes 3145732
  81.4 3.5 %copy-start.5 = (bf16[32,128,128]{2,1,0:T(8,128)(2,1)S(1)}, bf16[32,128,128]{2,1,0:T(8,128)(2,1)}, u32[]{:S(2)}) copy-start(bf16[32,128,128]{2,1,0:T(8,128)(2,1)} %gather_fusion.1) | copy-start | bytes 3145732
  89.6 4.0 %collective-permute-start.3 = (f32[128,64]{0,1:T(8,128)S(1)}, f32[128,64]{0,1:T(8,128)S(1)}, u32[]{:S(2)}, u32[]{:S(2)}) collective-permute-start(f32[128,64]{0,1:T(8,128)S(1)} %convolution_add_fusion.8), channel_id=1, source_target_pairs={{0,8},{4,12},{8,0},{12,4},{16,24},{20,28},{24,16},{28,20},{32,40},... | collective-permute-start | bytes 98312 | tf_op jit(solution)/shard_map/ppermute | solution.py:32
  93.8 4.9 %collective-permute-start.4 = (f32[128,64]{0,1:T(8,128)S(1)}, f32[128,64]{0,1:T(8,128)S(1)}, u32[]{:S(2)}, u32[]{:S(2)}) collective-permute-start(f32[128,64]{0,1:T(8,128)S(1)} %convolution_add_fusion.7), channel_id=1, source_target_pairs={{0,16},{4,20},{8,24},{12,28},{16,0},{20,4},{24,8},{28,12},{32,48},... | collective-permute-start | bytes 98312 | tf_op jit(solution)/shard_map/ppermute | solution.py:32
  98.9 8.1 %collective-permute-start.5 = (f32[128,64]{0,1:T(8,128)S(1)}, f32[128,64]{0,1:T(8,128)S(1)}, u32[]{:S(2)}, u32[]{:S(2)}) collective-permute-start(f32[128,64]{0,1:T(8,128)S(1)} %convolution_add_fusion.6), channel_id=1, source_target_pairs={{0,32},{4,36},{8,40},{12,44},{16,48},{20,52},{24,56},{28,60},{32,0... | collective-permute-start | bytes 98312 | tf_op jit(solution)/shard_map/ppermute | solution.py:32
  107.2 4.0 %collective-permute-start.6 = (f32[128,64]{0,1:T(8,128)S(1)}, f32[128,64]{0,1:T(8,128)S(1)}, u32[]{:S(2)}, u32[]{:S(2)}) collective-permute-start(f32[128,64]{0,1:T(8,128)S(1)} %convolution_add_fusion.5), channel_id=1, source_target_pairs={{0,64},{4,68},{8,72},{12,76},{16,80},{20,84},{24,88},{28,92},{32,9... | collective-permute-start | bytes 98312 | tf_op jit(solution)/shard_map/ppermute | solution.py:32
  111.5 6.6 %collective-permute-start.7 = (f32[128,64]{1,0:T(8,128)S(1)}, f32[128,64]{1,0:T(8,128)S(1)}, u32[]{:S(2)}, u32[]{:S(2)}) collective-permute-start(f32[128,64]{1,0:T(8,128)S(1)} %convolution_add_fusion), channel_id=1, source_target_pairs={{0,128},{4,132},{8,136},{12,140},{16,144},{20,148},{24,152},{28,15... | collective-permute-start | bytes 98312 | tf_op jit(solution)/shard_map/ppermute | solution.py:32
  118.1 2.9 %copy-start.4 = (f32[32,128,128]{1,2,0:T(8,128)S(1)}, f32[32,128,128]{1,2,0:T(8,128)}, u32[]{:S(2)}) copy-start(f32[32,128,128]{1,2,0:T(8,128)} %fusion.5) | copy-start | bytes 6291460
  118.2 2.8 %copy-start.3 = (f32[32,128,128]{1,2,0:T(8,128)S(1)}, f32[32,128,128]{1,2,0:T(8,128)}, u32[]{:S(2)}) copy-start(f32[32,128,128]{1,2,0:T(8,128)} %fusion.3) | copy-start | bytes 6291460
where the time goes:
time: 129 us; the launch traced here: 128 us
  local copies, waits for them, and re-layouts  49.9 us (39%)
  matrix products  28 us (22%)
  starting transfers between devices  18.9 us (15%)
  waiting for transfers between devices  14.6 us (11%)
  blocking collectives  14.4 us (11%)
    unnamed x35, local copies, waits for them, and re-layouts  26.3 us
    dot_general x6, matrix products, body(): jnp.einsum('crp,cpq->crq', picked, near_blocks[:, slot], preferred_elemen...  22.5 us
    ppermute x6, waiting for transfers between devices, from_partner(): return lax.ppermute(value, axis, pairs)  14.6 us
    psum x1, blocking collectives, body(): moment = lax.psum(partial_value, 'blk')  14.4 us
    dynamic_slice x2, local copies, waits for them, and re-layouts, pick_matrix(): lax.dynamic_index_in_dim(table, table_row, 0, keepdims=False)  11.8 us
    ppermute x1, starting transfers between devices, padded(): lax.ppermute(head, axis, [((i + 1) % count, i) for i in range(ends)])  8.36 us
    gather x6, local copies, waits for them, and re-layouts, body(): picked = jnp.take(by_cluster, local_columns[:, slot], axis=0)  8.24 us
    ppermute x6, starting transfers between devices, from_partner(): return lax.ppermute(value, axis, pairs)  7.1 us
  transfers between devices with their start and end apart: 8, of which 4 were waited for; matrix products, arithmetic and copies ran while one was open for 50% of the time, Pallas kernels for 0%

commit v1 on v0

v1 whole, which is shorter than its diff:
```python
import functools

import jax
import jax.numpy as jnp
from jax import lax
from jax.experimental import pallas as pl
from jax.experimental.pallas import tpu as pltpu
from jax.sharding import PartitionSpec as P

REACH = 4

highest = lax.Precision.HIGHEST
AXES = ("leaf", "blk")
NT = (((1,), (1,)), ((), ()))
TN = (((0,), (0,)), ((), ()))
NN = (((1,), (0,)), ((), ()))


def xor_permute(value, axis, mask):
    pairs = [(source, source ^ mask) for source in range(lax.axis_size(axis))]
    return lax.ppermute(value, axis, pairs)


def neighbour_clusters(sources, width):
    count = lax.axis_size(AXES)
    head = sources[:, :width]
    tail = sources[:, sources.shape[1] - width :]
    left = lax.ppermute(tail, AXES, [(i, i + 1) for i in range(count - 1)])
    right = lax.ppermute(head, AXES, [(i + 1, i) for i in range(count - 1)])
    return left, right


def moment_kernel(sources_ref, basis_ref, moment_ref):
    @pl.when(pl.program_id(0) == 0)
    def _():
        moment_ref[...] = jnp.zeros_like(moment_ref)

    clusters, _, panel = basis_ref.shape
    flat = jnp.concatenate([basis_ref[c] for c in range(clusters)], axis=1)
    moment_ref[...] += lax.dot_general(
        flat, sources_ref[...], NT, preferred_element_type=jnp.float32
    )


def moments(sources, basis, steps=4):
    rhs, panels = sources.shape
    clusters, rank, panel = basis.shape
    return pl.pallas_call(
        moment_kernel,
        grid=(steps,),
        in_specs=[
            pl.BlockSpec((rhs, panels // steps), lambda i: (0, i)),
            pl.BlockSpec((clusters // steps, rank, panel), lambda i: (i, 0, 0)),
        ],
        out_specs=pl.BlockSpec((rank, rhs), lambda i: (0, 0)),
        out_shape=jax.ShapeDtypeStruct((rank, rhs), jnp.float32),
        cost_estimate=pl.CostEstimate(
            flops=2 * rhs * panels * rank, bytes_accessed=2 * panels * (rhs + rank), transcendentals=0
        ),
        name="moments",
    )(sources, basis)


def tree_kernel(levels, rows_ref, transfer_ref, coupling_ref, up_ref, down_ref, mats, sems):
    copies = []
    for level in range(levels):
        row = rows_ref[level]
        pair = rows_ref[levels + level]
        copies.append(pltpu.make_async_copy(coupling_ref.at[row], mats.at[3 * level], sems.at[3 * level]))
        if level + 1 < levels:
            copies.append(pltpu.make_async_copy(transfer_ref.at[row], mats.at[3 * level + 1], sems.at[3 * level + 1]))
            copies.append(pltpu.make_async_copy(transfer_ref.at[pair], mats.at[3 * level + 2], sems.at[3 * level + 2]))
    for copy in copies:
        copy.start()
    for copy in copies:
        copy.wait()
    chain = None
    for level in range(levels):
        couple = mats[3 * level].astype(jnp.float32)
        if chain is None:
            down_ref[level] = couple.T
        else:
            down_ref[level] = lax.dot_general(
                chain, couple, NT, precision=highest, preferred_element_type=jnp.float32
            )
        if level + 1 < levels:
            mine = mats[3 * level + 1].astype(jnp.float32)
            theirs = mats[3 * level + 2].astype(jnp.float32)
            up_ref[2 * level] = mine.T
            up_ref[2 * level + 1] = theirs.T
            if chain is None:
                chain = mine
            else:
                chain = lax.dot_general(
                    chain, mine, NN, precision=highest, preferred_element_type=jnp.float32
                )


def tree_matrices(transfer, coupling, rows, levels):
    rank = transfer.shape[1]
    any_spec = pl.BlockSpec(memory_space=pl.ANY)
    return pl.pallas_call(
        functools.partial(tree_kernel, levels),
        in_specs=[pl.BlockSpec(memory_space=pltpu.SMEM), any_spec, any_spec],
        out_specs=[pl.BlockSpec(memory_space=pltpu.VMEM)] * 2,
        out_shape=[
            jax.ShapeDtypeStruct((2 * (levels - 1), rank, rank), jnp.float32),
            jax.ShapeDtypeStruct((levels, rank, rank), jnp.float32),
        ],
        scratch_shapes=[
            pltpu.VMEM((3 * levels, rank, rank), jnp.bfloat16),
            pltpu.SemaphoreType.DMA((3 * levels,)),
        ],
        cost_estimate=pl.CostEstimate(
            flops=2 * 6 * 2 * levels * rank**3, bytes_accessed=3 * levels * rank * rank * 4, transcendentals=0
        ),
        name="tree_matrices",
    )(rows, transfer, coupling)


def near_kernel(per_step, columns_ref, sources_ref, left_ref, right_ref, blocks_ref, near_ref, extended):
    step = pl.program_id(0)
    width = left_ref.shape[1]
    panels = sources_ref.shape[1]
    near_count = blocks_ref.shape[1]
    panel = blocks_ref.shape[2]

    @pl.when(step == 0)
    def _():
        extended[:, :width] = left_ref[...]
        extended[:, width : width + panels] = sources_ref[...]
        extended[:, width + panels :] = right_ref[...]

    for c in range(per_step):
        picked = []
        for slot in range(near_count):
            column = columns_ref[(step * per_step + c) * near_count + slot]
            picked.append(extended[:, pl.ds(pl.multiple_of(column * panel, panel), panel)])
        near_ref[:, c * panel : (c + 1) * panel] = jnp.dot(
            jnp.concatenate(picked, axis=1),
            blocks_ref[c].reshape(near_count * panel, panel),
            preferred_element_type=jnp.float32,
        )


def near_field(columns, sources, left, right, blocks, per_step=4):
    rhs, panels = sources.shape
    clusters, near_count, panel, _ = blocks.shape
    width = left.shape[1]
    whole = lambda i, columns: (0, 0)
    return pl.pallas_call(
        functools.partial(near_kernel, per_step),
        grid_spec=pltpu.PrefetchScalarGridSpec(
            num_scalar_prefetch=1,
            grid=(clusters // per_step,),
            in_specs=[
                pl.BlockSpec((rhs, panels), whole),
                pl.BlockSpec((rhs, width), whole),
                pl.BlockSpec((rhs, width), whole),
                pl.BlockSpec((per_step, near_count, panel, panel), lambda i, columns: (i, 0, 0, 0)),
            ],
            out_specs=pl.BlockSpec((rhs, per_step * panel), lambda i, columns: (0, i)),
            scratch_shapes=[pltpu.VMEM((rhs, panels + 2 * width), sources.dtype)],
        ),
        out_shape=jax.ShapeDtypeStruct((rhs, panels), jnp.float32),
        compiler_params=pltpu.CompilerParams(vmem_limit_bytes=24 * 1024 * 1024),
        cost_estimate=pl.CostEstimate(
            flops=2 * rhs * panels * near_count * panel,
            bytes_accessed=2 * panels * near_count * panel + 6 * rhs * panels,
            transcendentals=0,
        ),
        name="near_field",
    )(columns, sources, left, right, blocks)


def far_kernel(partial_ref, last_ref, matrix_ref, near_ref, basis_ref, out_ref, leaf_local):
    @pl.when(pl.program_id(0) == 0)
    def _():
        descended = partial_ref[...] + lax.dot_general(
            matrix_ref[0], last_ref[...], NN, precision=highest, preferred_element_type=jnp.float32
        )
        leaf_local[...] = descended.T.astype(leaf_local.dtype)

    clusters, _, panel = basis_ref.shape
    for c in range(clusters):
        columns = slice(c * panel, (c + 1) * panel)
        out_ref[:, columns] = near_ref[:, columns] + jnp.dot(
            leaf_local[...], basis_ref[c], preferred_element_type=jnp.float32
        )


def add_far(partial, last, matrices, near, basis, steps=4):
    rhs, panels = near.shape
    clusters, rank, panel = basis.shape
    levels = matrices.shape[0]
    whole = lambda i: (0, 0)
    return pl.pallas_call(
        far_kernel,
        grid=(steps,),
        in_specs=[
            pl.BlockSpec((rank, rhs), whole),
            pl.BlockSpec((rank, rhs), whole),
            pl.BlockSpec((1, rank, rank), lambda i: (levels - 1, 0, 0)),
            pl.BlockSpec((rhs, panels // steps), lambda i: (0, i)),
            pl.BlockSpec((clusters // steps, rank, panel), lambda i: (i, 0, 0)),
        ],
        out_specs=pl.BlockSpec((rhs, panels // steps), lambda i: (0, i)),
        out_shape=jax.ShapeDtypeStruct((rhs, panels), jnp.float32),
        scratch_shapes=[pltpu.VMEM((rhs, rank), jnp.bfloat16)],
        cost_estimate=pl.CostEstimate(
            flops=2 * rhs * panels * rank, bytes_accessed=8 * rhs * panels + 2 * rank * panels, transcendentals=0
        ),
        name="add_far",
    )(partial, last, matrices, near, basis)


def matmul(left, right):
    return jnp.dot(left, right, precision=highest, preferred_element_type=jnp.float32)


def body(sources, near_blocks, near_cols, basis, transfer, coupling):
    own_clusters = near_blocks.shape[0]
    panel_size = near_blocks.shape[2]
    leaf_count = lax.axis_size("leaf")
    blk_count = lax.axis_size("blk")
    levels = leaf_count.bit_length() - 1
    leaf_index = lax.axis_index("leaf")

    left, right = neighbour_clusters(sources, REACH * panel_size)
    moment = moments(sources, basis)

    level_index = jnp.arange(levels, dtype=jnp.int32)
    node = jnp.right_shift(leaf_index, level_index)
    first_row = jnp.right_shift(leaf_count, level_index) - 2
    rows = jnp.concatenate([first_row + node, first_row + (node ^ 1)]).astype(jnp.int32)
    up, down = tree_matrices(transfer, coupling, rows, levels)

    first_cluster = lax.axis_index(AXES) * own_clusters
    columns = (near_cols - (first_cluster - REACH)).reshape(-1)
    near = near_field(columns, sources, left, right, near_blocks)

    current = moment
    for bit in range(blk_count.bit_length() - 1):
        current = current + xor_permute(current, "blk", 2 ** (bit + 1) - 1)

    masks = [1, 2, 4, 12, 16, 48]
    collected = jnp.zeros_like(moment)
    for level in range(levels):
        sibling = xor_permute(current, "leaf", masks[level])
        if level + 1 < levels:
            current = matmul(up[2 * level], current) + matmul(up[2 * level + 1], sibling)
            collected = collected + matmul(down[level], sibling)
    return add_far(collected, sibling, down, near, basis)


def solution(mesh):
    return jax.shard_map(
        body,
        mesh=mesh,
        in_specs=(
            P(None, ("leaf", "blk")),
            P(("leaf", "blk"), None, None, None),
            P(("leaf", "blk"), None),
            P(("leaf", "blk"), None, None),
            P(),
            P(),
        ),
        out_specs=P(None, ("leaf", "blk")),
        check_vma=False,
    )
```

time: 129 us -> 75.5 us (0.59)
  local copies, waits for them, and re-layouts: 49.9 us -> 13.9 us
  matrix products: 28 us -> 7.57 us
  Pallas kernels: 0 us -> 15.2 us
  blocking collectives: 14.4 us -> 0 us
  waiting for transfers between devices: 14.6 us -> 16.3 us
    dot_general x29 -> x15, matrix products: 28 us -> 7.57 us  [matmul(): jnp.dot(left, right, precision=highest, preferred_element_type=jnp.float32)]
    pallas_call x0 -> x4, Pallas kernels: none -> 15.2 us  [the longest x1 4.43 us: add_far(): pl.pallas_call(far_kernel, grid=(steps,), in_specs=[pl.BlockSpec((rank, r...]
    psum x1 -> x0, blocking collectives: 14.4 us -> none  [body(): moment = lax.psum(partial_value, 'blk')]
    unnamed x35 -> x20, local copies, waits for them, and re-layouts: 26.3 us -> 12.8 us
    dynamic_slice x2 -> x0, local copies, waits for them, and re-layouts: 11.8 us -> none  [pick_matrix(): lax.dynamic_index_in_dim(table, table_row, 0, keepdims=False)]
    gather x6 -> x0, local copies, waits for them, and re-layouts: 8.24 us -> none  [body(): picked = jnp.take(by_cluster, local_columns[:, slot], axis=0)]
    reshape x2 -> x1, local copies, waits for them, and re-layouts: 3.58 us -> 0.1 us  [body(): columns = (near_cols - (first_cluster - REACH)).reshape(-1)]
    ppermute x8 -> x10, waiting for transfers between devices: 14.6 us -> 16.3 us  [the longest x8 16.3 us: xor_permute(): return lax.ppermute(value, axis, pairs)]
  transfers between devices with their start and end apart: 8 -> 10, of which waited for: 4 -> 5; matrix products, arithmetic and copies ran while one was open for 50% -> 24% of each run, Pallas kernels for 0% -> 10%
where the time goes in v1:
time: 75.5 us; the launch traced here: 74.6 us
  starting transfers between devices  20 us (26%)
  waiting for transfers between devices  16.3 us (22%)
  Pallas kernels  15.2 us (20%)
  local copies, waits for them, and re-layouts  13.9 us (18%)
  matrix products  7.57 us (10%)
  other arithmetic  1.44 us (2%)
    ppermute x8, waiting for transfers between devices, xor_permute(): return lax.ppermute(value, axis, pairs)  16.3 us
    unnamed x20, local copies, waits for them, and re-layouts  12.8 us
    ppermute x8, starting transfers between devices, xor_permute(): return lax.ppermute(value, axis, pairs)  9.24 us
    ppermute x1, starting transfers between devices, neighbour_clusters(): right = lax.ppermute(head, AXES, [(i + 1, i) for i in range(count - 1)])  8.37 us
    dot_general x15, matrix products, matmul(): jnp.dot(left, right, precision=highest, preferred_element_type=jnp.float32)  7.57 us
    pallas_call x1, Pallas kernels, add_far(): pl.pallas_call(far_kernel, grid=(steps,), in_specs=[pl.BlockSpec((rank, r...  4.43 us
    pallas_call x1, Pallas kernels, near_field(): pl.pallas_call(functools.partial(near_kernel, per_step), grid_spec=pltpu....  3.86 us
    pallas_call x1, Pallas kernels, tree_matrices(): pl.pallas_call(functools.partial(tree_kernel, levels), in_specs=[pl.Block...  3.53 us
  transfers between devices with their start and end apart: 10, of which 5 were waited for; matrix products, arithmetic and copies ran while one was open for 24% of the time, Pallas kernels for 10%

profile of v1, /device:TPU:6, one launch (start us, length us, event | category | flops | bytes accessed | tf_op | source)
XLA Modules:
  0.0 74.6 jit_solution(14002704391736037312)
XLA Ops:
  0.0 3.4 %moments.1 = f32[64,128]{1,0:T(8,128)} custom-call(bf16[128,4096]{1,0:T(8,128)(2,1)} %sources_ref.3, bf16[32,64,128]{2,1,0:T(8,128)(2,1)} %basis_ref.3), custom_call_target="tpu_custom_call" | custom-call | flops 67108864 | bytes 1572864 | tf_op jit(solution)/shard_map/moments/pallas_call | solution.py:48
  3.4 1.6 %collective-permute-start = (f32[64,128]{1,0:T(8,128)}, f32[64,128]{1,0:T(8,128)S(1)}, u32[]{:S(2)}, u32[]{:S(2)}) collective-permute-start(f32[64,128]{1,0:T(8,128)} %moments.1), channel_id=1, source_target_pairs={{0,1},{1,0},{2,3},{3,2},{4,5},{5,4},{6,7},{7,6},{8,9},{9,8},{10,11... | collective-permute-start | bytes 98312 | tf_op jit(solution)/shard_map/ppermute | solution.py:21
  5.0 1.0 %fusion.43 = (bf16[128,512]{1,0:T(8,128)(2,1)S(1)}, bf16[128,512]{1,0:T(8,128)(2,1)S(1)}) fusion(bf16[128,4096]{1,0:T(8,128)(2,1)} %sources_ref.3), kind=kLoop, calls=%fused_computation.54 | loop fusion | bytes 524288 | tf_op jit(solution)/shard_map/slice | solution.py:26
  6.0 2.4 %collective-permute-start.8 = (bf16[128,512]{1,0:T(8,128)(2,1)S(1)}, bf16[128,512]{1,0:T(8,128)(2,1)S(1)}, u32[]{:S(2)}, u32[]{:S(2)}) collective-permute-start(bf16[128,512]{1,0:T(8,128)(2,1)S(1)} %get-tuple-element.10), channel_id=1, source_target_pairs={{0,1},{1,2},{2,3},{3,4},{4,5},{5,6},{6,7},{7,8},{8,9},{9,10},{10,1... | collective-permute-start | bytes 393224 | tf_op jit(solution)/shard_map/ppermute | solution.py:28
  8.3 8.4 %collective-permute-start.9 = (bf16[128,512]{1,0:T(8,128)(2,1)S(1)}, bf16[128,512]{1,0:T(8,128)(2,1)S(1)}, u32[]{:S(2)}, u32[]{:S(2)}) collective-permute-start(bf16[128,512]{1,0:T(8,128)(2,1)S(1)} %get-tuple-element.9), channel_id=1, source_target_pairs={{1,0},{2,1},{3,2},{4,3},{5,4},{6,5},{7,6},{8,7},{9,8},{10,9},{11,1... | collective-permute-start | bytes 393224 | tf_op jit(solution)/shard_map/ppermute | solution.py:29
  16.7 0.0 collective-permute-done
  16.7 0.8 %add.46 = f32[64,128]{1,0:T(8,128)S(1)} add(f32[64,128]{1,0:T(8,128)} %moments.1, f32[64,128]{1,0:T(8,128)S(1)} %collective-permute-done) | non-fusion elementwise | flops 8192 | bytes 98304 | tf_op jit(solution)/shard_map/add | solution.py:244
  17.5 0.0 collective-permute-start.1
  17.5 5.1 %collective-permute-done.1 = f32[64,128]{1,0:T(8,128)S(1)} collective-permute-done((f32[64,128]{1,0:T(8,128)S(1)}, f32[64,128]{1,0:T(8,128)S(1)}, u32[]{:S(2)}, u32[]{:S(2)}) %collective-permute-start.1) | collective-permute-done | bytes 32800 | tf_op jit(solution)/shard_map/ppermute | solution.py:21
  22.6 0.0 collective-permute-start.2
  22.6 0.7 pad_add_fusion.rows_ref
  23.3 4.1 %copy.10.coupling_ref = bf16[126,64,64]{2,1,0:T(8,128)(2,1)} copy(bf16[126,64,64]{0,2,1:T(8,128)(2,1)S(1)} %copy-done.3) | data formatting | bytes 2064384 | tf_op args[5]
  27.4 4.0 %copy.9.transfer_ref = bf16[126,64,64]{2,1,0:T(8,128)(2,1)} copy(bf16[126,64,64]{0,2,1:T(8,128)(2,1)S(1)} %copy-done.4) | data formatting | bytes 2064384 | tf_op args[4]
  31.3 0.1 copy.11
  31.4 0.1 reshape.3.columns_ref
  31.5 0.0 copy-start.2
  31.5 3.5 %tree_matrices.1 = (f32[10,64,64]{2,1,0:T(8,128)}, f32[6,64,64]{2,1,0:T(8,128)}) custom-call(s32[12]{0:T(128)} %pad_add_fusion.rows_ref, bf16[126,64,64]{2,1,0:T(8,128)(2,1)} %copy.9.transfer_ref, bf16[126,64,64]{2,1,0:T(8,128)(2,1)} %copy.10.coupling_ref), custom_call_target="tpu_custom_call" | custom-call | flops 37748736 | bytes 294912 | tf_op jit(solution)/shard_map/tree_matrices/pallas_call | solution.py:102
  35.1 0.9 %fusion.21 = f32[64,128]{1,0:T(8,128)S(1)} fusion(f32[64,128]{1,0:T(8,128)S(1)} %collective-permute-done.2, f32[10,64,64]{2,1,0:T(8,128)} %get-tuple-element.8), kind=kOutput, calls=%fused_computation.27 | convolution fusion | flops 6291456 | bytes 98304 | tf_op jit(solution)/shard_map/dot_general | solution.py:218
  36.0 0.9 %convolution_add_fusion.4 = f32[64,128]{1,0:T(8,128)S(1)} fusion(f32[64,128]{1,0:T(8,128)S(1)} %fusion.21, f32[64,128]{1,0:T(8,128)S(1)} %add.47, f32[10,64,64]{2,1,0:T(8,128)} %get-tuple-element.8), kind=kOutput, calls=%fused_computation.4 | convolution fusion | flops 6299648 | bytes 131072 | tf_op jit(solution)/shard_map/dot_general | solution.py:218
  36.9 0.1 collective-permute-start.3
  37.0 0.9 %fusion.17 = f32[64,128]{1,0:T(8,128)S(1)} fusion(f32[64,128]{1,0:T(8,128)S(1)} %convolution_add_fusion.4, f32[10,64,64]{2,1,0:T(8,128)} %get-tuple-element.8), kind=kOutput, calls=%fused_computation.23 | convolution fusion | flops 6291456 | bytes 98304 | tf_op jit(solution)/shard_map/dot_general | solution.py:218
  38.0 3.0 %collective-permute-done.3 = f32[64,128]{1,0:T(8,128)S(1)} collective-permute-done((f32[64,128]{1,0:T(8,128)S(1)}, f32[64,128]{1,0:T(8,128)S(1)}, u32[]{:S(2)}, u32[]{:S(2)}) %collective-permute-start.3) | collective-permute-done | bytes 32800 | tf_op jit(solution)/shard_map/ppermute | solution.py:21
  40.9 0.9 %convolution_add_fusion.3 = f32[64,128]{1,0:T(8,128)S(1)} fusion(f32[64,128]{1,0:T(8,128)S(1)} %fusion.17, f32[64,128]{1,0:T(8,128)S(1)} %collective-permute-done.3, f32[10,64,64]{2,1,0:T(8,128)} %get-tuple-element.8), kind=kOutput, calls=%fused_computation.3 | convolution fusion | flops 6299648 | bytes 131072 | tf_op jit(solution)/shard_map/dot_general | solution.py:218
  41.9 0.4 collective-permute-start.4
  42.2 0.9 %fusion.12 = f32[64,128]{1,0:T(8,128)S(1)} fusion(f32[64,128]{1,0:T(8,128)S(1)} %convolution_add_fusion.3, f32[10,64,64]{2,1,0:T(8,128)} %get-tuple-element.8), kind=kOutput, calls=%fused_computation.18 | convolution fusion | flops 6291456 | bytes 98304 | tf_op jit(solution)/shard_map/dot_general | solution.py:218
  43.1 0.9 %fusion.24 = f32[64,128]{1,0:T(8,128)S(1)} fusion(f32[64,128]{1,0:T(8,128)S(1)} %collective-permute-done.3, f32[6,64,64]{2,1,0:T(8,128)} %get-tuple-element.7.matrix_ref), kind=kOutput, calls=%fused_computation.30 | convolution fusion | flops 6291456 | bytes 98304 | tf_op jit(solution)/shard_map/dot_general | solution.py:218
  44.1 0.0 collective-permute-done.8.left_ref
  44.1 0.0 copy-start.1
  44.1 2.8 %copy-done.1 = bf16[32,6,128,128]{3,2,1,0:T(8,128)(2,1)S(1)} copy-done((bf16[32,6,128,128]{3,2,1,0:T(8,128)(2,1)S(1)}, bf16[32,6,128,128]{3,2,1,0:T(8,128)(2,1)}, u32[]{:S(2)}) %copy-start.1) | copy-done | bytes 6291480
  46.9 3.9 %near_field.1.near_ref = f32[128,4096]{1,0:T(8,128)S(1)} custom-call(s32[192]{0:T(256)S(1)} %reshape.3.columns_ref, bf16[128,4096]{1,0:T(8,128)(2,1)S(1)} %copy-done.2, bf16[128,512]{1,0:T(8,128)(2,1)S(1)} %collective-permute-done.8.left_ref, bf16[128,512]{1,0:T(8,128)(2,1)S(1)} %collective-permute-done.9.right_ref, bf16[32,6,128,128]{3,2,1,0:T(8,128)(2,1)S(1)} %copy-done.1), custom_call_target="tpu_custom_call" | custom-call | flops 805306368 | bytes 9437184 | tf_op jit(solution)/shard_map/near_field/pallas_call | solution.py:151
  50.8 1.3 %copy-done = f32[128,4096]{1,0:T(8,128)} copy-done((f32[128,4096]{1,0:T(8,128)}, f32[128,4096]{1,0:T(8,128)S(1)}, u32[]{:S(2)}) %copy-start) | copy-done | bytes 2097176
  52.1 0.2 convolution_add_fusion.2
  52.3 5.7 %collective-permute-start.5 = (f32[64,128]{1,0:T(8,128)S(1)}, f32[64,128]{1,0:T(8,128)S(1)}, u32[]{:S(2)}, u32[]{:S(2)}) collective-permute-start(f32[64,128]{1,0:T(8,128)S(1)} %convolution_add_fusion.2), channel_id=1, source_target_pairs={{0,48},{4,52},{8,56},{12,60},{16,32},{20,36},{24,40},{28,44},{32,1... | collective-permute-start | bytes 98312 | tf_op jit(solution)/shard_map/ppermute | solution.py:21
  58.0 0.2 fusion.7
  58.2 0.2 fusion.19
  58.3 1.5 %collective-permute-done.5 = f32[64,128]{1,0:T(8,128)S(1)} collective-permute-done((f32[64,128]{1,0:T(8,128)S(1)}, f32[64,128]{1,0:T(8,128)S(1)}, u32[]{:S(2)}, u32[]{:S(2)}) %collective-permute-start.5) | collective-permute-done | bytes 32800 | tf_op jit(solution)/shard_map/ppermute | solution.py:21
  59.9 0.2 convolution_add_fusion.1
  60.1 0.2 fusion.4
  60.2 0.9 %collective-permute-start.6 = (f32[64,128]{1,0:T(8,128)S(1)}, f32[64,128]{1,0:T(8,128)S(1)}, u32[]{:S(2)}, u32[]{:S(2)}) collective-permute-start(f32[64,128]{1,0:T(8,128)S(1)} %convolution_add_fusion.1), channel_id=1, source_target_pairs={{0,64},{4,68},{8,72},{12,76},{16,80},{20,84},{24,88},{28,92},{32,9... | collective-permute-start | bytes 98312 | tf_op jit(solution)/shard_map/ppermute | solution.py:21
  61.1 0.2 fusion.14
  61.3 2.9 %collective-permute-done.6 = f32[64,128]{1,0:T(8,128)S(1)} collective-permute-done((f32[64,128]{1,0:T(8,128)S(1)}, f32[64,128]{1,0:T(8,128)S(1)}, u32[]{:S(2)}, u32[]{:S(2)}) %collective-permute-start.6) | collective-permute-done | bytes 32800 | tf_op jit(solution)/shard_map/ppermute | solution.py:21
  64.2 0.2 convolution_add_fusion
  64.4 0.6 collective-permute-start.7
  65.0 0.2 fusion.9
  65.1 0.8 %fusion.2.partial_ref = f32[64,128]{1,0:T(8,128)} fusion(f32[64,128]{1,0:T(8,128)S(1)} %fusion.9, f32[64,128]{1,0:T(8,128)S(1)} %fusion.14, f32[64,128]{1,0:T(8,128)S(1)} %fusion.19, f32[64,128]{1,0:T(8,128)S(1)} %fusion.24, f32[64,128]{1,0:T(8,128)S(1)} %collective-permute-done.2, f32[6,64,64]{2,1,0:T(8,128)S(1)} %copy-done.5), kind=kOutput, calls=%fused_computation.8 | convolution fusion | flops 6324224 | bytes 229376 | tf_op jit(solution)/shard_map/dot_general | solution.py:218
  65.9 3.7 %collective-permute-done.7.last_ref = f32[64,128]{1,0:T(8,128)S(1)} collective-permute-done((f32[64,128]{1,0:T(8,128)S(1)}, f32[64,128]{1,0:T(8,128)S(1)}, u32[]{:S(2)}, u32[]{:S(2)}) %collective-permute-start.7) | collective-permute-done | bytes 32800 | tf_op jit(solution)/shard_map/ppermute | solution.py:21
  69.6 0.6 copy-done.7
  70.2 4.4 %add_far.1 = f32[128,4096]{1,0:T(8,128)} custom-call(f32[64,128]{1,0:T(8,128)} %fusion.2.partial_ref, f32[64,128]{1,0:T(8,128)} %copy-done.7, f32[6,64,64]{2,1,0:T(8,128)} %get-tuple-element.7.matrix_ref, f32[128,4096]{1,0:T(8,128)} %copy-done, bf16[32,64,128]{2,1,0:T(8,128)(2,1)} %basis_ref.3), custom_call_target="tpu_custom_call" | custom-call | flops 67108864 | bytes 4718592 | tf_op jit(solution)/shard_map/add_far/pallas_call | solution.py:197
  (19 shorter events, 0.0 us)
Async XLA Ops:
  0.0 16.7 %copy-start.8 = (s32[32,6]{0,1:T(8,128)S(1)}, s32[32,6]{0,1:T(8,128)}, u32[]{:S(2)}) copy-start(s32[32,6]{0,1:T(8,128)} %param.8) | copy-start | bytes 2308
  0.0 23.3 %copy-start.3 = (bf16[126,64,64]{0,2,1:T(8,128)(2,1)S(1)}, bf16[126,64,64]{0,2,1:T(8,128)(2,1)}, u32[]{:S(2)}) copy-start(bf16[126,64,64]{0,2,1:T(8,128)(2,1)} %param.11) | copy-start | bytes 3096580
  3.4 24.0 %copy-start.4 = (bf16[126,64,64]{0,2,1:T(8,128)(2,1)S(1)}, bf16[126,64,64]{0,2,1:T(8,128)(2,1)}, u32[]{:S(2)}) copy-start(bf16[126,64,64]{0,2,1:T(8,128)(2,1)} %param.10) | copy-start | bytes 3096580
  3.4 13.3 %collective-permute-start = (f32[64,128]{1,0:T(8,128)}, f32[64,128]{1,0:T(8,128)S(1)}, u32[]{:S(2)}, u32[]{:S(2)}) collective-permute-start(f32[64,128]{1,0:T(8,128)} %moments.1), channel_id=1, source_target_pairs={{0,1},{1,0},{2,3},{3,2},{4,5},{5,4},{6,7},{7,6},{8,9},{9,8},{10,11... | collective-permute-start | bytes 98312 | tf_op jit(solution)/shard_map/ppermute | solution.py:21
  6.0 38.1 %collective-permute-start.8 = (bf16[128,512]{1,0:T(8,128)(2,1)S(1)}, bf16[128,512]{1,0:T(8,128)(2,1)S(1)}, u32[]{:S(2)}, u32[]{:S(2)}) collective-permute-start(bf16[128,512]{1,0:T(8,128)(2,1)S(1)} %get-tuple-element.10), channel_id=1, source_target_pairs={{0,1},{1,2},{2,3},{3,4},{4,5},{5,6},{6,7},{7,8},{8,9},{9,10},{10,1... | collective-permute-start | bytes 393224 | tf_op jit(solution)/shard_map/ppermute | solution.py:28
  8.3 35.8 %collective-permute-start.9 = (bf16[128,512]{1,0:T(8,128)(2,1)S(1)}, bf16[128,512]{1,0:T(8,128)(2,1)S(1)}, u32[]{:S(2)}, u32[]{:S(2)}) collective-permute-start(bf16[128,512]{1,0:T(8,128)(2,1)S(1)} %get-tuple-element.9), channel_id=1, source_target_pairs={{1,0},{2,1},{3,2},{4,3},{5,4},{6,5},{7,6},{8,7},{9,8},{10,9},{11,1... | collective-permute-start | bytes 393224 | tf_op jit(solution)/shard_map/ppermute | solution.py:29
  17.5 5.1 %collective-permute-start.1 = (f32[64,128]{1,0:T(8,128)S(1)}, f32[64,128]{1,0:T(8,128)S(1)}, u32[]{:S(2)}, u32[]{:S(2)}) collective-permute-start(f32[64,128]{1,0:T(8,128)S(1)} %add.46), channel_id=1, source_target_pairs={{0,3},{1,2},{2,1},{3,0},{4,7},{5,6},{6,5},{7,4},{8,11},{9,10},{10,... | collective-permute-start | bytes 98312 | tf_op jit(solution)/shard_map/ppermute | solution.py:21
  22.6 12.4 %collective-permute-start.2 = (f32[64,128]{1,0:T(8,128)S(1)}, f32[64,128]{1,0:T(8,128)S(1)}, u32[]{:S(2)}, u32[]{:S(2)}) collective-permute-start(f32[64,128]{1,0:T(8,128)S(1)} %add.47), channel_id=1, source_target_pairs={{0,4},{4,0},{8,12},{12,8},{16,20},{20,16},{24,28},{28,24},{32,36},... | collective-permute-start | bytes 98312 | tf_op jit(solution)/shard_map/ppermute | solution.py:21
  31.5 12.6 %copy-start.2 = (bf16[128,4096]{1,0:T(8,128)(2,1)S(1)}, bf16[128,4096]{1,0:T(8,128)(2,1)}, u32[]{:S(2)}) copy-start(bf16[128,4096]{1,0:T(8,128)(2,1)} %sources_ref.3) | copy-start | bytes 3145732
  36.9 4.0 %collective-permute-start.3 = (f32[64,128]{1,0:T(8,128)S(1)}, f32[64,128]{1,0:T(8,128)S(1)}, u32[]{:S(2)}, u32[]{:S(2)}) collective-permute-start(f32[64,128]{1,0:T(8,128)S(1)} %convolution_add_fusion.4), channel_id=1, source_target_pairs={{0,8},{4,12},{8,0},{12,4},{16,24},{20,28},{24,16},{28,20},{32,40},... | collective-permute-start | bytes 98312 | tf_op jit(solution)/shard_map/ppermute | solution.py:21
  41.9 10.2 %collective-permute-start.4 = (f32[64,128]{1,0:T(8,128)S(1)}, f32[64,128]{1,0:T(8,128)S(1)}, u32[]{:S(2)}, u32[]{:S(2)}) collective-permute-start(f32[64,128]{1,0:T(8,128)S(1)} %convolution_add_fusion.3), channel_id=1, source_target_pairs={{0,16},{4,20},{8,24},{12,28},{16,0},{20,4},{24,8},{28,12},{32,48},... | collective-permute-start | bytes 98312 | tf_op jit(solution)/shard_map/ppermute | solution.py:21
  44.1 2.8 %copy-start.1 = (bf16[32,6,128,128]{3,2,1,0:T(8,128)(2,1)S(1)}, bf16[32,6,128,128]{3,2,1,0:T(8,128)(2,1)}, u32[]{:S(2)}) copy-start(bf16[32,6,128,128]{3,2,1,0:T(8,128)(2,1)} %blocks_ref.1) | copy-start | bytes 18874372
  46.9 5.2 %copy-start.6 = (f32[10,64,64]{2,1,0:T(8,128)S(1)}, f32[10,64,64]{2,1,0:T(8,128)}, u32[]{:S(2)}) copy-start(f32[10,64,64]{2,1,0:T(8,128)} %get-tuple-element.8) | copy-start | bytes 491524
  46.9 11.3 %copy-start.5 = (f32[6,64,64]{2,1,0:T(8,128)S(1)}, f32[6,64,64]{2,1,0:T(8,128)}, u32[]{:S(2)}) copy-start(f32[6,64,64]{2,1,0:T(8,128)} %get-tuple-element.7.matrix_ref) | copy-start | bytes 294916
  50.8 1.3 %copy-start = (f32[128,4096]{1,0:T(8,128)}, f32[128,4096]{1,0:T(8,128)S(1)}, u32[]{:S(2)}) copy-start(f32[128,4096]{1,0:T(8,128)S(1)} %near_field.1.near_ref) | copy-start | bytes 6291460
  52.3 7.6 %collective-permute-start.5 = (f32[64,128]{1,0:T(8,128)S(1)}, f32[64,128]{1,0:T(8,128)S(1)}, u32[]{:S(2)}, u32[]{:S(2)}) collective-permute-start(f32[64,128]{1,0:T(8,128)S(1)} %convolution_add_fusion.2), channel_id=1, source_target_pairs={{0,48},{4,52},{8,56},{12,60},{16,32},{20,36},{24,40},{28,44},{32,1... | collective-permute-start | bytes 98312 | tf_op jit(solution)/shard_map/ppermute | solution.py:21
  60.2 4.0 %collective-permute-start.6 = (f32[64,128]{1,0:T(8,128)S(1)}, f32[64,128]{1,0:T(8,128)S(1)}, u32[]{:S(2)}, u32[]{:S(2)}) collective-permute-start(f32[64,128]{1,0:T(8,128)S(1)} %convolution_add_fusion.1), channel_id=1, source_target_pairs={{0,64},{4,68},{8,72},{12,76},{16,80},{20,84},{24,88},{28,92},{32,9... | collective-permute-start | bytes 98312 | tf_op jit(solution)/shard_map/ppermute | solution.py:21
  64.4 5.2 %collective-permute-start.7 = (f32[64,128]{1,0:T(8,128)S(1)}, f32[64,128]{1,0:T(8,128)S(1)}, u32[]{:S(2)}, u32[]{:S(2)}) collective-permute-start(f32[64,128]{1,0:T(8,128)S(1)} %convolution_add_fusion), channel_id=1, source_target_pairs={{0,192},{4,196},{8,200},{12,204},{16,208},{20,212},{24,216},{28,22... | collective-permute-start | bytes 98312 | tf_op jit(solution)/shard_map/ppermute | solution.py:21
  69.6 0.6 copy-start.7

commit v2 on v0

v2 whole, which is shorter than its diff:
```python
import functools

import jax
import jax.numpy as jnp
from jax import lax
from jax.experimental import pallas as pl
from jax.experimental.pallas import tpu as pltpu
from jax.sharding import PartitionSpec as P

REACH = 4
HALVES = 2
QUARTERS = 4
VMEM_BYTES = 16 * 1024 * 1024
NEAR_VMEM_BYTES = 16 * 1024 * 1024
MOMENT_VMEM_BYTES = 54784 * 1024

highest = lax.Precision.HIGHEST
AXES = ("leaf", "blk")
NT = (((1,), (1,)), ((), ()))
TN = (((0,), (0,)), ((), ()))


def xor_permute(value, axis, mask):
    pairs = [(source, source ^ mask) for source in range(lax.axis_size(axis))]
    return lax.ppermute(value, axis, pairs)


def inner_exchange(value):
    count = lax.axis_size(AXES)
    return lax.ppermute(value, AXES, [(i, i ^ 1) for i in range(count)])


def outer_exchange(value):
    count = lax.axis_size(AXES)
    pairs = [(i, i + 1) for i in range(1, count - 1, 2)]
    return lax.ppermute(value, AXES, pairs + [(b, a) for a, b in pairs])


def moment_kernel(odd_ref, sources_hbm, basis_hbm, moment_ref, inner_ref, outer_ref, sources, basis, sems):
    chunks = sources.shape[0]
    clusters = basis.shape[0] // chunks
    panels = sources.shape[2]
    width = inner_ref.shape[1]
    copies = []
    for k in range(chunks):
        own = slice(k * clusters, (k + 1) * clusters)
        copies.append(
            (
                pltpu.make_async_copy(
                    sources_hbm.at[:, k * panels : (k + 1) * panels], sources.at[k], sems.at[2 * k]
                ),
                pltpu.make_async_copy(basis_hbm.at[own], basis.at[own], sems.at[2 * k + 1]),
            )
        )
        for copy in copies[-1]:
            copy.start()
    total = jnp.zeros(moment_ref.shape, jnp.float32)
    for k in range(chunks):
        for copy in copies[k]:
            copy.wait()
        flat = jnp.concatenate([basis[k * clusters + c] for c in range(clusters)], axis=1)
        total += lax.dot_general(flat, sources[k], NT, preferred_element_type=jnp.float32)
    moment_ref[...] = total
    odd = odd_ref[0]

    @pl.when(odd == 0)
    def _():
        inner_ref[...] = sources[chunks - 1, :, panels - width :]
        outer_ref[...] = sources[0, :, :width]

    @pl.when(odd != 0)
    def _():
        inner_ref[...] = sources[0, :, :width]
        outer_ref[...] = sources[chunks - 1, :, panels - width :]


def moments(odd, sources, basis, width, chunks=4):
    rhs, panels = sources.shape
    clusters, rank, panel = basis.shape
    vmem = pl.BlockSpec(memory_space=pltpu.VMEM)
    hbm = pl.BlockSpec(memory_space=pltpu.HBM)
    return pl.pallas_call(
        moment_kernel,
        in_specs=[pl.BlockSpec(memory_space=pltpu.SMEM), hbm, hbm],
        out_specs=[vmem] * 3,
        out_shape=[
            jax.ShapeDtypeStruct((rank, rhs), jnp.float32),
            jax.ShapeDtypeStruct((rhs, width), sources.dtype),
            jax.ShapeDtypeStruct((rhs, width), sources.dtype),
        ],
        scratch_shapes=[
            pltpu.VMEM((chunks, rhs, panels // chunks), sources.dtype),
            pltpu.VMEM((clusters, rank, panel), basis.dtype),
            pltpu.SemaphoreType.DMA((2 * chunks,)),
        ],
        compiler_params=pltpu.CompilerParams(vmem_limit_bytes=MOMENT_VMEM_BYTES),
        cost_estimate=pl.CostEstimate(
            flops=2 * rhs * panels * rank, bytes_accessed=2 * panels * (rhs + rank), transcendentals=0
        ),
        name="moments",
    )(odd, sources, basis)


def near_products(columns_ref, panels_ref, near_ref, blocks_ref, first, base):
    quarter_clusters, near_count, panel, _ = blocks_ref.shape
    for c in range(quarter_clusters):
        picked = []
        for slot in range(near_count):
            column = columns_ref[slot, first + c] - base
            picked.append(panels_ref[:, pl.ds(pl.multiple_of(column * panel, panel), panel)])
        near_ref[:, c * panel : (c + 1) * panel] = jnp.dot(
            jnp.concatenate(picked, axis=1),
            blocks_ref[c].reshape(near_count * panel, panel),
            preferred_element_type=jnp.float32,
        )


def middle_kernel(first, place_ref, columns_ref, sources_ref, blocks_ref, near_ref):
    near_products(columns_ref, sources_ref, near_ref, blocks_ref, first, place_ref[1])


def edge_kernel(first, place_ref, columns_ref, sources_ref, inner_ref, outer_ref, blocks_ref, near_ref, window):
    width = inner_ref.shape[1]
    panels = sources_ref.shape[1]
    panel = blocks_ref.shape[2]
    reach = window.shape[1] - width
    is_left = first == 0
    halo = slice(0, width) if is_left else slice(reach, reach + width)
    own = slice(width, width + reach) if is_left else slice(0, reach)
    source = slice(0, reach) if is_left else slice(panels - reach, panels)
    base = place_ref[1] - width // panel if is_left else place_ref[1] + (panels - reach) // panel
    window[:, own] = sources_ref[:, source]
    from_inner = place_ref[0] == (1 if is_left else 0)

    @pl.when(from_inner)
    def _():
        window[:, halo] = inner_ref[...]

    @pl.when(jnp.logical_not(from_inner))
    def _():
        window[:, halo] = outer_ref[...]

    near_products(columns_ref, window, near_ref, blocks_ref, first, base)


def near_quarter(place, columns, sources, beside, blocks, index, name):
    rhs, panels = sources.shape
    clusters, near_count, panel, _ = blocks.shape
    quarter = clusters // QUARTERS
    smem = pl.BlockSpec(memory_space=pltpu.SMEM)
    vmem = pl.BlockSpec(memory_space=pltpu.VMEM)
    kernel = functools.partial(edge_kernel if beside else middle_kernel, index * quarter)
    scratch = []
    if beside:
        scratch = [pltpu.VMEM((rhs, panels // QUARTERS + 2 * beside[0].shape[1]), sources.dtype)]
    return pl.pallas_call(
        kernel,
        in_specs=[smem, smem] + [vmem] * (2 + len(beside)),
        out_specs=vmem,
        out_shape=jax.ShapeDtypeStruct((rhs, panels // QUARTERS), jnp.float32),
        scratch_shapes=scratch,
        compiler_params=pltpu.CompilerParams(vmem_limit_bytes=NEAR_VMEM_BYTES),
        cost_estimate=pl.CostEstimate(
            flops=2 * rhs * panels * near_count * panel // QUARTERS,
            bytes_accessed=(2 * panels * near_count * panel + 6 * rhs * panels) // QUARTERS,
            transcendentals=0,
        ),
        name=name,
    )(place, columns, sources, *beside, blocks[index * quarter : (index + 1) * quarter])


def far_kernel(
    partial_ref, last_ref, matrix_ref, left_ref, early_ref, late_ref, right_ref, basis_ref, out_ref, leaf_local
):
    step = pl.program_id(0)

    @pl.when(step == 0)
    def _():
        descended = partial_ref[...] + lax.dot_general(
            matrix_ref[...], last_ref[...], TN, precision=highest, preferred_element_type=jnp.float32
        )
        leaf_local[...] = descended.T.astype(leaf_local.dtype)

    clusters, _, panel = basis_ref.shape
    width = left_ref.shape[1]
    flat = jnp.concatenate([basis_ref[c] for c in range(clusters)], axis=1)
    far = jnp.dot(leaf_local[...], flat, preferred_element_type=jnp.float32)

    def put(low, high):
        out_ref[:, :width] = low[...] + far[:, :width]
        out_ref[:, width:] = high[...] + far[:, width:]

    pl.when(step == 0)(lambda: put(left_ref, early_ref))
    pl.when(step != 0)(lambda: put(late_ref, right_ref))


def add_far(partial, last, matrix, left, early, late, right, basis):
    rhs, quarter = left.shape
    clusters, rank, panel = basis.shape
    half_panels = clusters * panel // HALVES
    whole = lambda i: (0, 0)
    return pl.pallas_call(
        far_kernel,
        grid=(HALVES,),
        in_specs=[
            pl.BlockSpec((rank, rhs), whole),
            pl.BlockSpec((rank, rhs), whole),
            pl.BlockSpec((rank, rank), whole),
            *[pl.BlockSpec((rhs, quarter), whole)] * 4,
            pl.BlockSpec((clusters // HALVES, rank, panel), lambda i: (i, 0, 0)),
        ],
        out_specs=pl.BlockSpec((rhs, half_panels), lambda i: (0, i)),
        out_shape=jax.ShapeDtypeStruct((rhs, HALVES * half_panels), jnp.float32),
        scratch_shapes=[pltpu.VMEM((rhs, rank), jnp.bfloat16)],
        compiler_params=pltpu.CompilerParams(vmem_limit_bytes=VMEM_BYTES),
        cost_estimate=pl.CostEstimate(
            flops=4 * rhs * half_panels * rank,
            bytes_accessed=16 * rhs * half_panels + 4 * rank * half_panels,
            transcendentals=0,
        ),
        name="add_far",
    )(partial, last, matrix, left, early, late, right, basis)


def matmul(left, right):
    return jnp.dot(left, right, precision=highest, preferred_element_type=jnp.float32)


def matmul_tn(left, right):
    return lax.dot_general(left, right, TN, precision=highest, preferred_element_type=jnp.float32)


def pick_rows(table, rows):
    one_hot = (rows[:, None] == jnp.arange(table.shape[0], dtype=rows.dtype)[None, :]).astype(table.dtype)
    return jnp.einsum("nkj,sn->skj", table, one_hot, preferred_element_type=jnp.float32)


def together(*values):
    return lax.optimization_barrier(values)


def body(sources, near_blocks, near_cols, basis, transfer, coupling):
    own_clusters = near_blocks.shape[0]
    panel_size = near_blocks.shape[2]
    leaf_count = lax.axis_size("leaf")
    levels = leaf_count.bit_length() - 1
    leaf_index = lax.axis_index("leaf")
    device = lax.axis_index(AXES)
    odd = jnp.bitwise_and(device, 1).astype(jnp.int32)
    odd_flag = odd.reshape(1)
    first_cluster = device * own_clusters

    def place(side, first_column):
        return jnp.stack([side, first_column]).astype(jnp.int32)

    here = place(odd, first_cluster)
    columns = near_cols.T

    level_index = jnp.arange(levels, dtype=jnp.int32)
    node = jnp.right_shift(leaf_index, level_index)
    first_row = jnp.right_shift(leaf_count, level_index) - 2
    mine_rows = (first_row + node).astype(jnp.int32)
    their_rows = (first_row + (node ^ 1)).astype(jnp.int32)

    moment, inner_send, outer_send = moments(odd_flag, sources, basis, REACH * panel_size)

    inner_clusters = inner_exchange(inner_send)
    other = xor_permute(moment, "blk", 1)
    moves = pick_rows(transfer, jnp.concatenate([mine_rows[: levels - 1], their_rows[: levels - 1]]))
    other, moves = together(other, moves)
    current = moment + other

    current, coupling = together(current, coupling)
    other = xor_permute(current, "blk", 3)
    couples = pick_rows(coupling, mine_rows)
    other, couples, inner_clusters = together(other, couples, inner_clusters)
    current = current + other

    siblings = []
    down = [couples[0]]
    chain = moves[0].T
    for level, mask in enumerate([1, 2, 4, 12, 16, 48]):
        if level == 1:
            current, early_sources, early_blocks = together(current, sources, near_blocks)
        elif level == 3:
            current, late_sources, late_blocks = together(current, sources, near_blocks)
        elif level == 2:
            current, outer_send = together(current, outer_send)
        elif level == 4:
            current, left_sources, left_blocks = together(current, sources, near_blocks)
        elif level == 5:
            current, right_sources, right_blocks = together(current, sources, near_blocks)
        sibling = xor_permute(current, "leaf", mask)
        if level == 1:
            early = near_quarter(here, columns, early_sources, (), early_blocks, 1, "near_early")
            sibling, early = together(sibling, early)
        elif level == 3:
            late = near_quarter(here, columns, late_sources, (), late_blocks, 2, "near_late")
            sibling, late, outer_clusters = together(sibling, late, outer_clusters)
        elif level == 2:
            outer_clusters = outer_exchange(outer_send)
        elif level == 4:
            beside = (inner_clusters, outer_clusters)
            left = near_quarter(here, columns, left_sources, beside, left_blocks, 0, "near_left")
            sibling, left = together(sibling, left)
        elif level == 5:
            beside = (inner_clusters, outer_clusters)
            right = near_quarter(here, columns, right_sources, beside, right_blocks, 3, "near_right")
            sibling, right = together(sibling, right)
        siblings.append(sibling)
        if level + 1 < levels:
            current = matmul_tn(moves[level], current) + matmul_tn(moves[levels - 1 + level], sibling)
    for step in range(1, levels):
        chain = chain if step == 1 else matmul_tn(moves[step - 1], chain)
        down.append(matmul(couples[step], chain))
    collected = matmul_tn(jnp.concatenate(down[:-1]), jnp.concatenate(siblings[:-1]))
    return add_far(collected, sibling, down[-1], left, early, late, right, basis)


def solution(mesh):
    return jax.shard_map(
        body,
        mesh=mesh,
        in_specs=(
            P(None, ("leaf", "blk")),
            P(("leaf", "blk"), None, None, None),
            P(("leaf", "blk"), None),
            P(("leaf", "blk"), None, None),
            P(),
            P(),
        ),
        out_specs=P(None, ("leaf", "blk")),
        check_vma=False,
    )
```

time: 129 us -> 48.4 us (0.38)
  local copies, waits for them, and re-layouts: 49.9 us -> 2.63 us
  matrix products: 28 us -> 6.38 us
  blocking collectives: 14.4 us -> 0 us
  Pallas kernels: 0 us -> 9.25 us
  waiting for transfers between devices: 14.6 us -> 9.84 us
    unnamed x35 -> x17, local copies, waits for them, and re-layouts: 26.3 us -> 0.13 us
    dot_general x29 -> x22, matrix products: 28 us -> 6.38 us  [the longest x15 3.72 us: matmul_tn(): lax.dot_general(left, right, TN, precision=highest, preferred_element_typ...]
    psum x1 -> x0, blocking collectives: 14.4 us -> none  [body(): moment = lax.psum(partial_value, 'blk')]
    dynamic_slice x2 -> x0, local copies, waits for them, and re-layouts: 11.8 us -> none  [pick_matrix(): lax.dynamic_index_in_dim(table, table_row, 0, keepdims=False)]
    pallas_call x0 -> x6, Pallas kernels: none -> 9.25 us  [the longest x4 5 us: near_quarter(): pl.pallas_call(kernel, in_specs=[smem, smem] + [vmem] * (2 + len(beside))...]
    gather x6 -> x0, local copies, waits for them, and re-layouts: 8.24 us -> none  [body(): picked = jnp.take(by_cluster, local_columns[:, slot], axis=0)]
    ppermute x8 -> x10, waiting for transfers between devices: 14.6 us -> 9.84 us  [the longest x8 9.83 us: xor_permute(): return lax.ppermute(value, axis, pairs)]
    reshape x2 -> x0, local copies, waits for them, and re-layouts: 3.58 us -> none  [the longest x1 1.81 us: body(): jnp.transpose(total, (1, 0, 2))]
  transfers between devices with their start and end apart: 8 -> 10, of which waited for: 4 -> 5; matrix products, arithmetic and copies ran while one was open for 50% -> 15% of each run, Pallas kernels for 0% -> 10%
where the time goes in v2:
time: 48.4 us; the launch traced here: 48.2 us
  starting transfers between devices  19.6 us (40%)
  waiting for transfers between devices  9.84 us (20%)
  Pallas kernels  9.25 us (19%)
  matrix products  6.38 us (13%)
  local copies, waits for them, and re-layouts  2.63 us (5%)
    ppermute x8, starting transfers between devices, xor_permute(): return lax.ppermute(value, axis, pairs)  12.3 us
    ppermute x8, waiting for transfers between devices, xor_permute(): return lax.ppermute(value, axis, pairs)  9.83 us
    ppermute x1, starting transfers between devices, outer_exchange(): return lax.ppermute(value, AXES, pairs + [(b, a) for a, b in pairs])  6.91 us
    pallas_call x4, Pallas kernels, near_quarter(): pl.pallas_call(kernel, in_specs=[smem, smem] + [vmem] * (2 + len(beside))...  5 us
    dot_general x15, matrix products, matmul_tn(): lax.dot_general(left, right, TN, precision=highest, preferred_element_typ...  3.72 us
    pallas_call x1, Pallas kernels, moments(): pl.pallas_call(moment_kernel, in_specs=[pl.BlockSpec(memory_space=pltpu.S...  2.18 us
    slice x4, local copies, waits for them, and re-layouts, near_quarter(): blocks[index * quarter:(index + 1) * quarter]  2.09 us
    pallas_call x1, Pallas kernels, add_far(): pl.pallas_call(far_kernel, grid=(HALVES,), in_specs=[pl.BlockSpec((rank,...  2.06 us
  transfers between devices with their start and end apart: 10, of which 5 were waited for; matrix products, arithmetic and copies ran while one was open for 15% of the time, Pallas kernels for 10%

profile of v2, /device:TPU:6, one launch (start us, length us, event | category | flops | bytes accessed | tf_op | source)
XLA Modules:
  0.0 48.2 jit_solution(4664601105937659516)
XLA Ops:
  0.0 2.2 %moments.1 = (f32[64,128]{1,0:T(8,128)S(1)}, bf16[128,512]{1,0:T(8,128)(2,1)S(1)}, bf16[128,512]{1,0:T(8,128)(2,1)S(1)}) custom-call(s32[1]{0:T(128)} %bitcast.odd_ref, bf16[128,4096]{1,0:T(8,128)(2,1)} %sources_ref.3, bf16[32,64,128]{2,1,0:T(8,128)(2,1)} %basis_ref.1), custom_call_target="tpu_custom_call" | custom-call | flops 67108864 | bytes 1572864 | tf_op jit(solution)/shard_map/moments/pallas_call | solution.py:82
  2.2 1.7 %collective-permute-start = (f32[64,128]{1,0:T(8,128)S(1)}, f32[64,128]{1,0:T(8,128)S(1)}, u32[]{:S(2)}, u32[]{:S(2)}) collective-permute-start(f32[64,128]{1,0:T(8,128)S(1)} %get-tuple-element.38), channel_id=1, source_target_pairs={{0,1},{1,0},{2,3},{3,2},{4,5},{5,4},{6,7},{7,6},{8,9},{9,8},{10,11... | collective-permute-start | bytes 98312 | tf_op jit(solution)/shard_map/ppermute | solution.py:25
  3.9 0.4 collective-permute-start.2
  4.4 0.9 %fusion.1 = f32[10,64,64]{2,0,1:T(8,128)S(1)} fusion(bf16[126,64,64]{0,2,1:T(8,128)(2,1)S(1)} %copy-done, s32[10]{0:T(128)S(1)} %pad_add_fusion), kind=kOutput, calls=%fused_computation.17 | convolution fusion | flops 10323180 | bytes 1196072 | tf_op jit(solution)/shard_map/nkj,sn->skj/dot_general | solution.py:235
  5.4 1.0 %collective-permute-done = f32[64,128]{1,0:T(8,128)S(1)} collective-permute-done((f32[64,128]{1,0:T(8,128)S(1)}, f32[64,128]{1,0:T(8,128)S(1)}, u32[]{:S(2)}, u32[]{:S(2)}) %collective-permute-start) | collective-permute-done | bytes 32800 | tf_op jit(solution)/shard_map/ppermute | solution.py:25
  6.4 3.2 %collective-permute-start.1 = (f32[64,128]{1,0:T(8,128)S(1)}, f32[64,128]{1,0:T(8,128)S(1)}, u32[]{:S(2)}, u32[]{:S(2)}) collective-permute-start(f32[64,128]{1,0:T(8,128)S(1)} %add.42), channel_id=1, source_target_pairs={{0,3},{1,2},{2,1},{3,0},{4,7},{5,6},{6,5},{7,4},{8,11},{9,10},{10,... | collective-permute-start | bytes 98312 | tf_op jit(solution)/shard_map/ppermute | solution.py:25
  9.5 0.9 %fusion.5 = f32[6,64,64]{2,0,1:T(8,128)S(1)} fusion(bf16[126,64,64]{0,2,1:T(8,128)(2,1)S(1)} %copy-done.5, s32[6]{0:T(128)S(1)} %fusion.8), kind=kOutput, calls=%fused_computation.21 | convolution fusion | flops 6193908 | bytes 1130520 | tf_op jit(solution)/shard_map/nkj,sn->skj/dot_general | solution.py:235
  10.5 0.3 fusion.9
  10.7 0.2 fusion.11
  11.0 0.2 fusion.12
  11.2 0.2 fusion.13
  11.4 0.2 fusion.20
  11.7 0.1 fusion.10
  11.9 0.1 collective-permute-start.3
  12.0 0.2 convolution_dynamic-update-slice_fusion.3
  12.2 0.2 convolution_dynamic-update-slice_fusion.2
  12.3 0.2 convolution_dynamic-update-slice_fusion.1
  12.5 0.2 convolution_dynamic-update-slice_fusion
  12.7 0.2 fusion.21.matrix_ref
  12.9 0.3 collective-permute-done.3
  13.2 0.2 fusion.14
  13.4 0.2 convolution_add_fusion.4
  13.7 0.2 fusion.15
  13.9 2.0 %collective-permute-start.4 = (f32[64,128]{1,0:T(8,128)S(1)}, f32[64,128]{1,0:T(8,128)S(1)}, u32[]{:S(2)}, u32[]{:S(2)}) collective-permute-start(f32[64,128]{1,0:T(8,128)S(1)} %convolution_add_fusion.4), channel_id=1, source_target_pairs={{0,8},{4,12},{8,0},{12,4},{16,24},{20,28},{24,16},{28,20},{32,40},... | collective-permute-start | bytes 98312 | tf_op jit(solution)/shard_map/ppermute | solution.py:25
  15.9 1.6 %slice.83.blocks_ref = bf16[8,6,128,128]{3,2,1,0:T(8,128)(2,1)S(1)} slice(bf16[32,6,128,128]{3,2,1,0:T(8,128)(2,1)} %param.7), slice={[8:16], [0:6], [0:128], [0:128]} | slice | bytes 3145728 | tf_op jit(solution)/shard_map/slice | solution.py:169
  17.6 1.2 %near_early.1.early_ref = f32[128,1024]{1,0:T(8,128)S(1)} custom-call(s32[2]{0:T(128)S(1)} %pad_add_fusion.1.place_ref, s32[6,32]{1,0:T(8,128)S(1)} %bitcast.69, bf16[128,4096]{1,0:T(8,128)(2,1)S(1)} %copy-done.1, bf16[8,6,128,128]{3,2,1,0:T(8,128)(2,1)S(1)} %slice.83.blocks_ref), custom_call_target="tpu_custom_call" | custom-call | flops 201326592 | bytes 2359296 | tf_op jit(solution)/shard_map/near_early/pallas_call | solution.py:156
  18.9 0.2 convolution_add_fusion.3
  19.1 0.2 fusion.16
  19.3 3.4 %collective-permute-start.5 = (f32[64,128]{1,0:T(8,128)S(1)}, f32[64,128]{1,0:T(8,128)S(1)}, u32[]{:S(2)}, u32[]{:S(2)}) collective-permute-start(f32[64,128]{1,0:T(8,128)S(1)} %convolution_add_fusion.3), channel_id=1, source_target_pairs={{0,16},{4,20},{8,24},{12,28},{16,0},{20,4},{24,8},{28,12},{32,48},... | collective-permute-start | bytes 98312 | tf_op jit(solution)/shard_map/ppermute | solution.py:25
  22.7 6.9 %collective-permute-start.7 = (bf16[128,512]{1,0:T(8,128)(2,1)S(1)}, bf16[128,512]{1,0:T(8,128)(2,1)S(1)}, u32[]{:S(2)}, u32[]{:S(2)}) collective-permute-start(bf16[128,512]{1,0:T(8,128)(2,1)S(1)} %get-tuple-element.55), channel_id=1, source_target_pairs={{1,2},{3,4},{5,6},{7,8},{9,10},{11,12},{13,14},{15,16},{17,18},{19... | collective-permute-start | bytes 393224 | tf_op jit(solution)/shard_map/ppermute | solution.py:36
  29.6 0.2 convolution_add_fusion.2
  29.9 0.2 fusion.17
  30.1 1.3 %collective-permute-start.6 = (f32[64,128]{1,0:T(8,128)S(1)}, f32[64,128]{1,0:T(8,128)S(1)}, u32[]{:S(2)}, u32[]{:S(2)}) collective-permute-start(f32[64,128]{1,0:T(8,128)S(1)} %convolution_add_fusion.2), channel_id=1, source_target_pairs={{0,48},{4,52},{8,56},{12,60},{16,32},{20,36},{24,40},{28,44},{32,1... | collective-permute-start | bytes 98312 | tf_op jit(solution)/shard_map/ppermute | solution.py:25
  31.4 0.2 slice.86.blocks_ref
  31.6 1.2 %near_late.1.late_ref = f32[128,1024]{1,0:T(8,128)S(1)} custom-call(s32[2]{0:T(128)S(1)} %pad_add_fusion.1.place_ref, s32[6,32]{1,0:T(8,128)S(1)} %bitcast.70, bf16[128,4096]{1,0:T(8,128)(2,1)S(1)} %copy-done.1, bf16[8,6,128,128]{3,2,1,0:T(8,128)(2,1)S(1)} %slice.86.blocks_ref), custom_call_target="tpu_custom_call" | custom-call | flops 201326592 | bytes 2359296 | tf_op jit(solution)/shard_map/near_late/pallas_call | solution.py:156
  32.8 3.4 %collective-permute-done.6 = f32[64,128]{1,0:T(8,128)S(1)} collective-permute-done((f32[64,128]{1,0:T(8,128)S(1)}, f32[64,128]{1,0:T(8,128)S(1)}, u32[]{:S(2)}, u32[]{:S(2)}) %collective-permute-start.6) | collective-permute-done | bytes 32800 | tf_op jit(solution)/shard_map/ppermute | solution.py:25
  36.2 0.2 convolution_add_fusion.1
  36.5 0.2 fusion.19
  36.7 0.6 %collective-permute-start.8 = (f32[64,128]{1,0:T(8,128)S(1)}, f32[64,128]{1,0:T(8,128)S(1)}, u32[]{:S(2)}, u32[]{:S(2)}) collective-permute-start(f32[64,128]{1,0:T(8,128)S(1)} %convolution_add_fusion.1), channel_id=1, source_target_pairs={{0,64},{4,68},{8,72},{12,76},{16,80},{20,84},{24,88},{28,92},{32,9... | collective-permute-start | bytes 98312 | tf_op jit(solution)/shard_map/ppermute | solution.py:25
  37.3 0.2 slice.88.blocks_ref
  37.5 1.3 %near_left.1.left_ref = f32[128,1024]{1,0:T(8,128)S(1)} custom-call(s32[2]{0:T(128)S(1)} %pad_add_fusion.1.place_ref, s32[6,32]{1,0:T(8,128)S(1)} %bitcast.71, bf16[128,4096]{1,0:T(8,128)(2,1)S(1)} %copy-done.1, bf16[128,512]{1,0:T(8,128)(2,1)S(1)} %collective-permute-done.2.inner_ref, bf16[128,512]{1,0:T(8,128)(2,1)S(1)} %collective-permute-done.7.outer_ref, ...), custom_call_target="tpu_custom_call" | custom-call | flops 201326592 | bytes 2359296 | tf_op jit(solution)/shard_map/near_left/pallas_call | solution.py:156
  38.8 1.9 %collective-permute-done.8 = f32[64,128]{1,0:T(8,128)S(1)} collective-permute-done((f32[64,128]{1,0:T(8,128)S(1)}, f32[64,128]{1,0:T(8,128)S(1)}, u32[]{:S(2)}, u32[]{:S(2)}) %collective-permute-start.8) | collective-permute-done | bytes 32800 | tf_op jit(solution)/shard_map/ppermute | solution.py:25
  40.7 0.2 convolution_add_fusion
  41.1 0.4 fusion.18.partial_ref
  41.5 0.2 slice.91.blocks_ref
  41.7 1.3 %near_right.1.right_ref = f32[128,1024]{1,0:T(8,128)S(1)} custom-call(s32[2]{0:T(128)S(1)} %pad_add_fusion.1.place_ref, s32[6,32]{1,0:T(8,128)S(1)} %bitcast.72, bf16[128,4096]{1,0:T(8,128)(2,1)S(1)} %copy-done.1, bf16[128,512]{1,0:T(8,128)(2,1)S(1)} %collective-permute-done.2.inner_ref, bf16[128,512]{1,0:T(8,128)(2,1)S(1)} %collective-permute-done.7.outer_ref, ...), custom_call_target="tpu_custom_call" | custom-call | flops 201326592 | bytes 2359296 | tf_op jit(solution)/shard_map/near_right/pallas_call | solution.py:156
  43.0 3.2 %collective-permute-done.9.last_ref = f32[64,128]{1,0:T(8,128)S(1)} collective-permute-done((f32[64,128]{1,0:T(8,128)S(1)}, f32[64,128]{1,0:T(8,128)S(1)}, u32[]{:S(2)}, u32[]{:S(2)}) %collective-permute-start.9) | collective-permute-done | bytes 32800 | tf_op jit(solution)/shard_map/ppermute | solution.py:25
  46.2 2.1 %add_far.1 = f32[128,4096]{1,0:T(8,128)} custom-call(f32[64,128]{1,0:T(8,128)S(1)} %fusion.18.partial_ref, f32[64,128]{1,0:T(8,128)S(1)} %collective-permute-done.9.last_ref, f32[64,64]{1,0:T(8,128)S(1)} %fusion.21.matrix_ref, f32[128,1024]{1,0:T(8,128)S(1)} %near_left.1.left_ref, f32[128,1024]{1,0:T(8,128)S(1)} %near_early.1.early_ref, ...), custom_call_target="tpu_custom_call" | custom-call | flops 67108864 | bytes 4718592 | tf_op jit(solution)/shard_map/add_far/pallas_call | solution.py:202
  (30 shorter events, 0.4 us)
Async XLA Ops:
  0.0 4.4 %copy-start = (bf16[126,64,64]{0,2,1:T(8,128)(2,1)S(1)}, bf16[126,64,64]{0,2,1:T(8,128)(2,1)}, u32[]{:S(2)}) copy-start(bf16[126,64,64]{0,2,1:T(8,128)(2,1)} %param.10) | copy-start | bytes 3096580
  0.0 9.5 %copy-start.5 = (bf16[126,64,64]{0,2,1:T(8,128)(2,1)S(1)}, bf16[126,64,64]{0,2,1:T(8,128)(2,1)}, u32[]{:S(2)}) copy-start(bf16[126,64,64]{0,2,1:T(8,128)(2,1)} %param.11) | copy-start | bytes 3096580
  2.2 4.2 %collective-permute-start = (f32[64,128]{1,0:T(8,128)S(1)}, f32[64,128]{1,0:T(8,128)S(1)}, u32[]{:S(2)}, u32[]{:S(2)}) collective-permute-start(f32[64,128]{1,0:T(8,128)S(1)} %get-tuple-element.38), channel_id=1, source_target_pairs={{0,1},{1,0},{2,3},{3,2},{4,5},{5,4},{6,7},{7,6},{8,9},{9,8},{10,11... | collective-permute-start | bytes 98312 | tf_op jit(solution)/shard_map/ppermute | solution.py:25
  3.9 7.8 %collective-permute-start.2 = (bf16[128,512]{1,0:T(8,128)(2,1)S(1)}, bf16[128,512]{1,0:T(8,128)(2,1)S(1)}, u32[]{:S(2)}, u32[]{:S(2)}) collective-permute-start(bf16[128,512]{1,0:T(8,128)(2,1)S(1)} %get-tuple-element.42), channel_id=1, source_target_pairs={{0,1},{1,0},{2,3},{3,2},{4,5},{5,4},{6,7},{7,6},{8,9},{9,8},{10,11... | collective-permute-start | bytes 393224 | tf_op jit(solution)/shard_map/ppermute | solution.py:30
  4.4 27.0 %copy-start.4 = (bf16[32,6,128,128]{3,2,1,0:T(8,128)(2,1)S(1)}, bf16[32,6,128,128]{3,2,1,0:T(8,128)(2,1)}, u32[]{:S(2)}) copy-start(bf16[32,6,128,128]{3,2,1,0:T(8,128)(2,1)} %param.7) | copy-start | bytes 18874372
  6.4 5.3 %collective-permute-start.1 = (f32[64,128]{1,0:T(8,128)S(1)}, f32[64,128]{1,0:T(8,128)S(1)}, u32[]{:S(2)}, u32[]{:S(2)}) collective-permute-start(f32[64,128]{1,0:T(8,128)S(1)} %add.42), channel_id=1, source_target_pairs={{0,3},{1,2},{2,1},{3,0},{4,7},{5,6},{6,5},{7,4},{8,11},{9,10},{10,... | collective-permute-start | bytes 98312 | tf_op jit(solution)/shard_map/ppermute | solution.py:25
  11.9 1.3 %collective-permute-start.3 = (f32[64,128]{1,0:T(8,128)S(1)}, f32[64,128]{1,0:T(8,128)S(1)}, u32[]{:S(2)}, u32[]{:S(2)}) collective-permute-start(f32[64,128]{1,0:T(8,128)S(1)} %add.43), channel_id=1, source_target_pairs={{0,4},{4,0},{8,12},{12,8},{16,20},{20,16},{24,28},{28,24},{32,36},... | collective-permute-start | bytes 98312 | tf_op jit(solution)/shard_map/ppermute | solution.py:25
  13.9 4.9 %collective-permute-start.4 = (f32[64,128]{1,0:T(8,128)S(1)}, f32[64,128]{1,0:T(8,128)S(1)}, u32[]{:S(2)}, u32[]{:S(2)}) collective-permute-start(f32[64,128]{1,0:T(8,128)S(1)} %convolution_add_fusion.4), channel_id=1, source_target_pairs={{0,8},{4,12},{8,0},{12,4},{16,24},{20,28},{24,16},{28,20},{32,40},... | collective-permute-start | bytes 98312 | tf_op jit(solution)/shard_map/ppermute | solution.py:25
  15.9 1.7 %copy-start.1 = (bf16[128,4096]{1,0:T(8,128)(2,1)S(1)}, bf16[128,4096]{1,0:T(8,128)(2,1)}, u32[]{:S(2)}) copy-start(bf16[128,4096]{1,0:T(8,128)(2,1)} %sources_ref.3) | copy-start | bytes 3145732
  15.9 1.7 %copy-start.3 = (s32[32,6]{0,1:T(8,128)S(1)}, s32[32,6]{0,1:T(8,128)}, u32[]{:S(2)}) copy-start(s32[32,6]{0,1:T(8,128)} %param.8) | copy-start | bytes 2308
  19.3 10.3 %collective-permute-start.5 = (f32[64,128]{1,0:T(8,128)S(1)}, f32[64,128]{1,0:T(8,128)S(1)}, u32[]{:S(2)}, u32[]{:S(2)}) collective-permute-start(f32[64,128]{1,0:T(8,128)S(1)} %convolution_add_fusion.3), channel_id=1, source_target_pairs={{0,16},{4,20},{8,24},{12,28},{16,0},{20,4},{24,8},{28,12},{32,48},... | collective-permute-start | bytes 98312 | tf_op jit(solution)/shard_map/ppermute | solution.py:25
  22.7 13.5 %collective-permute-start.7 = (bf16[128,512]{1,0:T(8,128)(2,1)S(1)}, bf16[128,512]{1,0:T(8,128)(2,1)S(1)}, u32[]{:S(2)}, u32[]{:S(2)}) collective-permute-start(bf16[128,512]{1,0:T(8,128)(2,1)S(1)} %get-tuple-element.55), channel_id=1, source_target_pairs={{1,2},{3,4},{5,6},{7,8},{9,10},{11,12},{13,14},{15,16},{17,18},{19... | collective-permute-start | bytes 393224 | tf_op jit(solution)/shard_map/ppermute | solution.py:36
  30.1 6.1 %collective-permute-start.6 = (f32[64,128]{1,0:T(8,128)S(1)}, f32[64,128]{1,0:T(8,128)S(1)}, u32[]{:S(2)}, u32[]{:S(2)}) collective-permute-start(f32[64,128]{1,0:T(8,128)S(1)} %convolution_add_fusion.2), channel_id=1, source_target_pairs={{0,48},{4,52},{8,56},{12,60},{16,32},{20,36},{24,40},{28,44},{32,1... | collective-permute-start | bytes 98312 | tf_op jit(solution)/shard_map/ppermute | solution.py:25
  36.7 4.0 %collective-permute-start.8 = (f32[64,128]{1,0:T(8,128)S(1)}, f32[64,128]{1,0:T(8,128)S(1)}, u32[]{:S(2)}, u32[]{:S(2)}) collective-permute-start(f32[64,128]{1,0:T(8,128)S(1)} %convolution_add_fusion.1), channel_id=1, source_target_pairs={{0,64},{4,68},{8,72},{12,76},{16,80},{20,84},{24,88},{28,92},{32,9... | collective-permute-start | bytes 98312 | tf_op jit(solution)/shard_map/ppermute | solution.py:25
  41.0 5.2 %collective-permute-start.9 = (f32[64,128]{1,0:T(8,128)S(1)}, f32[64,128]{1,0:T(8,128)S(1)}, u32[]{:S(2)}, u32[]{:S(2)}) collective-permute-start(f32[64,128]{1,0:T(8,128)S(1)} %convolution_add_fusion), channel_id=1, source_target_pairs={{0,192},{4,196},{8,200},{12,204},{16,208},{20,212},{24,216},{28,22... | collective-permute-start | bytes 98312 | tf_op jit(solution)/shard_map/ppermute | solution.py:25
  41.7 4.5 %copy-start.2 = (bf16[32,64,128]{2,1,0:T(8,128)(2,1)S(1)}, bf16[32,64,128]{2,1,0:T(8,128)(2,1)}, u32[]{:S(2)}) copy-start(bf16[32,64,128]{2,1,0:T(8,128)(2,1)} %basis_ref.1) | copy-start | bytes 1572868

commit v3 on v2

--- a/solution.py
+++ b/solution.py
@@ -2,13 +2,13 @@
 
 import jax
 import jax.numpy as jnp
+import numpy as np
 from jax import lax
 from jax.experimental import pallas as pl
 from jax.experimental.pallas import tpu as pltpu
 from jax.sharding import PartitionSpec as P
 
 REACH = 4
-HALVES = 2
 QUARTERS = 4
 VMEM_BYTES = 16 * 1024 * 1024
 NEAR_VMEM_BYTES = 16 * 1024 * 1024
@@ -143,10 +143,14 @@
     near_products(columns_ref, window, near_ref, blocks_ref, first, base)
 
 
+def take_quarter(blocks, index):
+    quarter = blocks.shape[0] // QUARTERS
+    return blocks[index * quarter : (index + 1) * quarter]
+
+
 def near_quarter(place, columns, sources, beside, blocks, index, name):
     rhs, panels = sources.shape
-    clusters, near_count, panel, _ = blocks.shape
-    quarter = clusters // QUARTERS
+    quarter, near_count, panel, _ = blocks.shape
     smem = pl.BlockSpec(memory_space=pltpu.SMEM)
     vmem = pl.BlockSpec(memory_space=pltpu.VMEM)
     kernel = functools.partial(edge_kernel if beside else middle_kernel, index * quarter)
@@ -166,60 +170,51 @@
             transcendentals=0,
         ),
         name=name,
-    )(place, columns, sources, *beside, blocks[index * quarter : (index + 1) * quarter])
-
-
-def far_kernel(
-    partial_ref, last_ref, matrix_ref, left_ref, early_ref, late_ref, right_ref, basis_ref, out_ref, leaf_local
-):
-    step = pl.program_id(0)
-
-    @pl.when(step == 0)
-    def _():
-        descended = partial_ref[...] + lax.dot_general(
-            matrix_ref[...], last_ref[...], TN, precision=highest, preferred_element_type=jnp.float32
+    )(place, columns, sources, *beside, blocks)
+
+
+def far_kernel(count, partial_ref, *refs):
+    left_ref, early_ref, late_ref, right_ref, basis_ref, out_hbm, total, sems = refs[2 * count :]
+    descended = partial_ref[...]
+    for value_ref, matrix_ref in zip(refs[:count], refs[count : 2 * count]):
+        descended += lax.dot_general(
+            matrix_ref[...], value_ref[...], TN, precision=highest, preferred_element_type=jnp.float32
         )
-        leaf_local[...] = descended.T.astype(leaf_local.dtype)
-
-    clusters, _, panel = basis_ref.shape
-    width = left_ref.shape[1]
-    flat = jnp.concatenate([basis_ref[c] for c in range(clusters)], axis=1)
-    far = jnp.dot(leaf_local[...], flat, preferred_element_type=jnp.float32)
-
-    def put(low, high):
-        out_ref[:, :width] = low[...] + far[:, :width]
-        out_ref[:, width:] = high[...] + far[:, width:]
-
-    pl.when(step == 0)(lambda: put(left_ref, early_ref))
-    pl.when(step != 0)(lambda: put(late_ref, right_ref))
-
-
-def add_far(partial, last, matrix, left, early, late, right, basis):
+    leaf_local = descended.T.astype(basis_ref.dtype)
+    clusters = basis_ref.shape[0] // QUARTERS
+    panels = left_ref.shape[1]
+    copies = []
+    for k, near_ref in enumerate((left_ref, early_ref, late_ref, right_ref)):
+        flat = jnp.concatenate([basis_ref[k * clusters + c] for c in range(clusters)], axis=1)
+        total[k] = near_ref[...] + jnp.dot(leaf_local, flat, preferred_element_type=jnp.float32)
+        copy = pltpu.make_async_copy(total.at[k], out_hbm.at[:, k * panels : (k + 1) * panels], sems.at[k])
+        copy.start()
+        copies.append(copy)
+    for copy in copies:
+        copy.wait()
+
+
+def add_far(partial, last, matrices, left, early, late, right, basis):
     rhs, quarter = left.shape
-    clusters, rank, panel = basis.shape
-    half_panels = clusters * panel // HALVES
-    whole = lambda i: (0, 0)
+    rank = basis.shape[1]
+    vmem = pl.BlockSpec(memory_space=pltpu.VMEM)
     return pl.pallas_call(
-        far_kernel,
-        grid=(HALVES,),
-        in_specs=[
-            pl.BlockSpec((rank, rhs), whole),
-            pl.BlockSpec((rank, rhs), whole),
-            pl.BlockSpec((rank, rank), whole),
-            *[pl.BlockSpec((rhs, quarter), whole)] * 4,
-            pl.BlockSpec((clusters // HALVES, rank, panel), lambda i: (i, 0, 0)),
+        functools.partial(far_kernel, len(last)),
+        in_specs=[vmem] * (6 + 2 * len(last)),
+        out_specs=pl.BlockSpec(memory_space=pltpu.HBM),
+        out_shape=jax.ShapeDtypeStruct((rhs, QUARTERS * quarter), jnp.float32),
+        scratch_shapes=[
+            pltpu.VMEM((QUARTERS, rhs, quarter), jnp.float32),
+            pltpu.SemaphoreType.DMA((QUARTERS,)),
         ],
-        out_specs=pl.BlockSpec((rhs, half_panels), lambda i: (0, i)),
-        out_shape=jax.ShapeDtypeStruct((rhs, HALVES * half_panels), jnp.float32),
-        scratch_shapes=[pltpu.VMEM((rhs, rank), jnp.bfloat16)],
         compiler_params=pltpu.CompilerParams(vmem_limit_bytes=VMEM_BYTES),
         cost_estimate=pl.CostEstimate(
-            flops=4 * rhs * half_panels * rank,
-            bytes_accessed=16 * rhs * half_panels + 4 * rank * half_panels,
+            flops=2 * rhs * QUARTERS * quarter * rank,
+            bytes_accessed=QUARTERS * (8 * rhs * quarter + 2 * rank * quarter),
             transcendentals=0,
         ),
         name="add_far",
-    )(partial, last, matrix, left, early, late, right, basis)
+    )(partial, *last, *matrices, left, early, late, right, basis)
 
 
 def matmul(left, right):
@@ -256,17 +251,20 @@
     here = place(odd, first_cluster)
     columns = near_cols.T
 
-    level_index = jnp.arange(levels, dtype=jnp.int32)
-    node = jnp.right_shift(leaf_index, level_index)
-    first_row = jnp.right_shift(leaf_count, level_index) - 2
-    mine_rows = (first_row + node).astype(jnp.int32)
-    their_rows = (first_row + (node ^ 1)).astype(jnp.int32)
+    below_top = levels - 2
+    shifts = np.array([*range(levels - 1), *range(below_top), below_top, below_top], np.int32)
+    flips = np.array([0] * (levels - 1) + [1] * below_top + [3, 2], np.int32)
+    rows = ((leaf_count >> shifts) - 2) + (jnp.right_shift(leaf_index, shifts) ^ flips)
+    rows = rows.astype(jnp.int32)
+    mine_shifts = np.arange(levels, dtype=np.int32)
+    mine_rows = ((leaf_count >> mine_shifts) - 2) + jnp.right_shift(leaf_index, mine_shifts)
+    mine_rows = mine_rows.astype(jnp.int32)
 
     moment, inner_send, outer_send = moments(odd_flag, sources, basis, REACH * panel_size)
 
     inner_clusters = inner_exchange(inner_send)
     other = xor_permute(moment, "blk", 1)
-    moves = pick_rows(transfer, jnp.concatenate([mine_rows[: levels - 1], their_rows[: levels - 1]]))
+    moves = pick_rows(transfer, rows)
     other, moves = together(other, moves)
     current = moment + other
 
@@ -276,45 +274,64 @@
     other, couples, inner_clusters = together(other, couples, inner_clusters)
     current = current + other
 
+    chains = [moves[0].T]
+    for step in range(1, levels - 1):
+        chains.append(matmul_tn(moves[step], chains[-1]))
+    down = [couples[0]]
+    for step in range(1, below_top - 1):
+        down.append(matmul(couples[step], chains[step - 1]))
+
     siblings = []
-    down = [couples[0]]
-    chain = moves[0].T
-    for level, mask in enumerate([1, 2, 4, 12, 16, 48]):
+    for level, mask in enumerate([1, 2, 4, 12]):
         if level == 1:
-            current, early_sources, early_blocks = together(current, sources, near_blocks)
-        elif level == 3:
-            current, late_sources, late_blocks = together(current, sources, near_blocks)
+            current, early_blocks = together(current, near_blocks)
         elif level == 2:
             current, outer_send = together(current, outer_send)
-        elif level == 4:
-            current, left_sources, left_blocks = together(current, sources, near_blocks)
-        elif level == 5:
-            current, right_sources, right_blocks = together(current, sources, near_blocks)
+            current, middle_sources = together(current, sources)
+        elif level == 3:
+            current, late_sources, middle_blocks = together(current, sources, near_blocks)
         sibling = xor_permute(current, "leaf", mask)
+        ready = current
+        extras = []
         if level == 1:
-            early = near_quarter(here, columns, early_sources, (), early_blocks, 1, "near_early")
-            sibling, early = together(sibling, early)
-        elif level == 3:
-            late = near_quarter(here, columns, late_sources, (), late_blocks, 2, "near_late")
-            sibling, late, outer_clusters = together(sibling, late, outer_clusters)
+            extras.append(take_quarter(early_blocks, 1))
+            ready, early_quarter, top_couples, top_chains = together(
+                current, *extras, couples[below_top - 1 :], chains[below_top - 2 :]
+            )
+            tops = [matmul(couple, top) for couple, top in zip(top_couples, top_chains)]
+            cousins = [matmul(moves[levels - 1 + below_top + k], tops[-1]) for k in range(2)]
+            extras = [early_quarter, *tops, *cousins]
         elif level == 2:
             outer_clusters = outer_exchange(outer_send)
-        elif level == 4:
+            extras.append(
+                near_quarter(here, columns, middle_sources, (), early_quarter, 1, "near_early")
+            )
+        elif level == 3:
             beside = (inner_clusters, outer_clusters)
-            left = near_quarter(here, columns, left_sources, beside, left_blocks, 0, "near_left")
-            sibling, left = together(sibling, left)
-        elif level == 5:
-            beside = (inner_clusters, outer_clusters)
-            right = near_quarter(here, columns, right_sources, beside, right_blocks, 3, "near_right")
-            sibling, right = together(sibling, right)
+            late = near_quarter(here, columns, late_sources, (), take_quarter(middle_blocks, 2), 2, "near_late")
+            extras.append(late)
+            ready, *extras = together(current, *extras)
+            left = near_quarter(here, columns, late_sources, beside, take_quarter(middle_blocks, 0), 0, "near_left")
+            extras.append(left)
+        extras.append(matmul_tn(moves[level], ready))
+        sibling, *extras = together(sibling, *extras)
+        if level == 1:
+            early_quarter = extras[0]
+            down += extras[1:4]
+            cousins = extras[4:6]
+        elif level == 2:
+            early = extras[0]
+        elif level == 3:
+            late, left = extras[:2]
         siblings.append(sibling)
-        if level + 1 < levels:
-            current = matmul_tn(moves[level], current) + matmul_tn(moves[levels - 1 + level], sibling)
-    for step in range(1, levels):
-        chain = chain if step == 1 else matmul_tn(moves[step - 1], chain)
-        down.append(matmul(couples[step], chain))
-    collected = matmul_tn(jnp.concatenate(down[:-1]), jnp.concatenate(siblings[:-1]))
-    return add_far(collected, sibling, down[-1], left, early, late, right, basis)
+        current = extras[-1] + matmul_tn(moves[levels - 1 + level], sibling)
+
+    current, last_sources, last_blocks = together(current, sources, near_blocks)
+    last = [xor_permute(current, "leaf", mask) for mask in (16, 48, 32)]
+    right = near_quarter(here, columns, last_sources, beside, take_quarter(last_blocks, 3), 3, "near_right")
+    collected = matmul_tn(jnp.concatenate(down[:below_top]), jnp.concatenate(siblings))
+    *last, right, collected = together(*last, right, collected)
+    return add_far(collected, last, [down[below_top], *cousins], left, early, late, right, basis)
 
 
 def solution(mesh):

time: 48.4 us -> 46.1 us (0.952)
  waiting for transfers between devices: 9.84 us -> 4.91 us
  starting transfers between devices: 19.6 us -> 22.5 us
    ppermute x8 -> x9, waiting for transfers between devices: 9.83 us -> 4.91 us  [xor_permute(): return lax.ppermute(value, axis, pairs)]
    ppermute x8 -> x9, starting transfers between devices: 12.3 us -> 15.2 us  [xor_permute(): return lax.ppermute(value, axis, pairs)]
    dot_general x15 -> x13, matrix products: 3.72 us -> 3.22 us  [matmul_tn(): lax.dot_general(left, right, TN, precision=highest, preferred_element_typ...]
    dot_general x5 -> x7, matrix products: 0.83 us -> 1.15 us  [matmul(): jnp.dot(left, right, precision=highest, preferred_element_type=jnp.float32)]
  transfers between devices with their start and end apart: 10 -> 11, of which waited for: 5 -> 6; matrix products, arithmetic and copies ran while one was open for 15% -> 18% of each run, Pallas kernels for 10% -> 11%
where the time goes in v3:
time: 46.1 us; the launch traced here: 46 us
  starting transfers between devices  22.5 us (49%)
  Pallas kernels  9.14 us (20%)
  matrix products  6.2 us (13%)
  waiting for transfers between devices  4.91 us (11%)
  local copies, waits for them, and re-layouts  2.72 us (6%)
  between operations  0.47 us (1%)
    ppermute x9, starting transfers between devices, xor_permute(): return lax.ppermute(value, axis, pairs)  15.2 us
    ppermute x1, starting transfers between devices, outer_exchange(): return lax.ppermute(value, AXES, pairs + [(b, a) for a, b in pairs])  6.86 us
    pallas_call x4, Pallas kernels, near_quarter(): pl.pallas_call(kernel, in_specs=[smem, smem] + [vmem] * (2 + len(beside))...  4.99 us
    ppermute x9, waiting for transfers between devices, xor_permute(): return lax.ppermute(value, axis, pairs)  4.91 us
    dot_general x13, matrix products, matmul_tn(): lax.dot_general(left, right, TN, precision=highest, preferred_element_typ...  3.22 us
    slice x3, local copies, waits for them, and re-layouts, take_quarter(): return blocks[index * quarter:(index + 1) * quarter]  2.23 us
    pallas_call x1, Pallas kernels, moments(): pl.pallas_call(moment_kernel, in_specs=[pl.BlockSpec(memory_space=pltpu.S...  2.11 us
    pallas_call x1, Pallas kernels, add_far(): pl.pallas_call(functools.partial(far_kernel, len(last)), in_specs=[vmem]...  2.03 us
  transfers between devices with their start and end apart: 11, of which 6 were waited for; matrix products, arithmetic and copies ran while one was open for 18% of the time, Pallas kernels for 11%

profile of v3, /device:TPU:6, one launch (start us, length us, event | category | flops | bytes accessed | tf_op | source)
XLA Modules:
  0.0 46.0 jit_solution(3014508784301656022)
XLA Ops:
  0.0 2.1 %moments.1 = (f32[64,128]{1,0:T(8,128)S(1)}, bf16[128,512]{1,0:T(8,128)(2,1)S(1)}, bf16[128,512]{1,0:T(8,128)(2,1)S(1)}) custom-call(s32[1]{0:T(128)} %bitcast.odd_ref, bf16[128,4096]{1,0:T(8,128)(2,1)} %sources_ref.3, bf16[32,64,128]{2,1,0:T(8,128)(2,1)} %refs_10_.1), custom_call_target="tpu_custom_call" | custom-call | flops 67108864 | bytes 1572864 | tf_op jit(solution)/shard_map/moments/pallas_call | solution.py:82
  2.2 1.7 %collective-permute-start = (f32[64,128]{1,0:T(8,128)S(1)}, f32[64,128]{1,0:T(8,128)S(1)}, u32[]{:S(2)}, u32[]{:S(2)}) collective-permute-start(f32[64,128]{1,0:T(8,128)S(1)} %get-tuple-element.56), channel_id=1, source_target_pairs={{0,1},{1,0},{2,3},{3,2},{4,5},{5,4},{6,7},{7,6},{8,9},{9,8},{10,11... | collective-permute-start | bytes 98312 | tf_op jit(solution)/shard_map/ppermute | solution.py:25
  3.9 0.4 collective-permute-start.2
  4.3 0.9 %fusion.16 = f32[11,64,64]{2,0,1:T(8,128)S(1)} fusion(bf16[126,64,64]{0,2,1:T(8,128)(2,1)S(1)} %copy-done, s32[11]{0:T(128)S(1)} %xor_add_fusion), kind=kOutput, calls=%fused_computation.17 | convolution fusion | flops 11355498 | bytes 1212460 | tf_op jit(solution)/shard_map/nkj,sn->skj/dot_general | solution.py:230
  5.3 1.0 %collective-permute-done = f32[64,128]{1,0:T(8,128)S(1)} collective-permute-done((f32[64,128]{1,0:T(8,128)S(1)}, f32[64,128]{1,0:T(8,128)S(1)}, u32[]{:S(2)}, u32[]{:S(2)}) %collective-permute-start) | collective-permute-done | bytes 32800 | tf_op jit(solution)/shard_map/ppermute | solution.py:25
  6.4 3.2 %collective-permute-start.1 = (f32[64,128]{1,0:T(8,128)S(1)}, f32[64,128]{1,0:T(8,128)S(1)}, u32[]{:S(2)}, u32[]{:S(2)}) collective-permute-start(f32[64,128]{1,0:T(8,128)S(1)} %add.29), channel_id=1, source_target_pairs={{0,3},{1,2},{2,1},{3,0},{4,7},{5,6},{6,5},{7,4},{8,11},{9,10},{10,... | collective-permute-start | bytes 98312 | tf_op jit(solution)/shard_map/ppermute | solution.py:25
  9.5 0.3 fusion.25
  9.8 0.9 %fusion.20 = f32[6,64,64]{2,0,1:T(8,128)S(1)} fusion(bf16[126,64,64]{0,2,1:T(8,128)(2,1)S(1)} %copy-done.5, s32[6]{0:T(128)S(1)} %shift-right-arithmetic_add_fusion), kind=kOutput, calls=%fused_computation.21 | convolution fusion | flops 6193908 | bytes 1130520 | tf_op jit(solution)/shard_map/nkj,sn->skj/dot_general | solution.py:230
  10.7 0.3 fusion.30
  11.0 0.2 fusion.31
  11.2 0.2 fusion.32
  11.5 0.2 fusion.33
  11.8 0.1 collective-permute-start.3
  11.9 0.2 fusion.28
  12.2 0.2 fusion.45
  12.4 0.2 fusion.46
  12.6 0.5 %collective-permute-done.3 = f32[64,128]{1,0:T(8,128)S(1)} collective-permute-done((f32[64,128]{1,0:T(8,128)S(1)}, f32[64,128]{1,0:T(8,128)S(1)}, u32[]{:S(2)}, u32[]{:S(2)}) %collective-permute-start.3) | collective-permute-done | bytes 32800 | tf_op jit(solution)/shard_map/ppermute | solution.py:25
  13.1 0.2 fusion.29
  13.3 2.0 %collective-permute-start.4 = (f32[64,128]{1,0:T(8,128)S(1)}, f32[64,128]{1,0:T(8,128)S(1)}, u32[]{:S(2)}, u32[]{:S(2)}) collective-permute-start(f32[64,128]{1,0:T(8,128)S(1)} %add.32), channel_id=1, source_target_pairs={{0,8},{4,12},{8,0},{12,4},{16,24},{20,28},{24,16},{28,20},{32,40},... | collective-permute-start | bytes 98312 | tf_op jit(solution)/shard_map/ppermute | solution.py:25
  15.3 1.7 %slice.63.blocks_ref = bf16[8,6,128,128]{3,2,1,0:T(8,128)(2,1)S(1)} slice(bf16[32,6,128,128]{3,2,1,0:T(8,128)(2,1)} %param.12), slice={[8:16], [0:6], [0:128], [0:128]} | slice | bytes 3145728 | tf_op jit(solution)/shard_map/slice | solution.py:148
  17.0 0.2 fusion.39
  17.3 0.2 fusion.36
  17.5 0.2 fusion.38.refs_5_
  17.7 0.2 fusion.37.refs_4_
  17.8 0.2 fusion.34
  18.0 0.2 fusion.35.refs_3_
  18.2 0.2 fusion.40
  18.4 3.4 %collective-permute-start.5 = (f32[64,128]{1,0:T(8,128)S(1)}, f32[64,128]{1,0:T(8,128)S(1)}, u32[]{:S(2)}, u32[]{:S(2)}) collective-permute-start(f32[64,128]{1,0:T(8,128)S(1)} %add.33), channel_id=1, source_target_pairs={{0,16},{4,20},{8,24},{12,28},{16,0},{20,4},{24,8},{28,12},{32,48},... | collective-permute-start | bytes 98312 | tf_op jit(solution)/shard_map/ppermute | solution.py:25
  21.8 0.2 fusion.41
  22.0 6.9 %collective-permute-start.7 = (bf16[128,512]{1,0:T(8,128)(2,1)S(1)}, bf16[128,512]{1,0:T(8,128)(2,1)S(1)}, u32[]{:S(2)}, u32[]{:S(2)}) collective-permute-start(bf16[128,512]{1,0:T(8,128)(2,1)S(1)} %get-tuple-element.88), channel_id=1, source_target_pairs={{1,2},{3,4},{5,6},{7,8},{9,10},{11,12},{13,14},{15,16},{17,18},{19... | collective-permute-start | bytes 393224 | tf_op jit(solution)/shard_map/ppermute | solution.py:36
  28.9 1.2 %near_early.1.refs_7_ = f32[128,1024]{1,0:T(8,128)S(1)} custom-call(s32[2]{0:T(128)S(1)} %pad_add_fusion.place_ref, s32[6,32]{1,0:T(8,128)S(1)} %bitcast.66, bf16[128,4096]{1,0:T(8,128)(2,1)S(1)} %copy-done.1, bf16[8,6,128,128]{3,2,1,0:T(8,128)(2,1)S(1)} %slice.63.blocks_ref), custom_call_target="tpu_custom_call" | custom-call | flops 201326592 | bytes 2359296 | tf_op jit(solution)/shard_map/near_early/pallas_call | solution.py:160
  30.2 0.2 fusion.42
  30.4 1.3 %collective-permute-start.6 = (f32[64,128]{1,0:T(8,128)S(1)}, f32[64,128]{1,0:T(8,128)S(1)}, u32[]{:S(2)}, u32[]{:S(2)}) collective-permute-start(f32[64,128]{1,0:T(8,128)S(1)} %add.34), channel_id=1, source_target_pairs={{0,48},{4,52},{8,56},{12,60},{16,32},{20,36},{24,40},{28,44},{32,1... | collective-permute-start | bytes 98312 | tf_op jit(solution)/shard_map/ppermute | solution.py:25
  31.7 0.4 fusion.24
  32.1 1.2 %near_late.1.refs_8_ = f32[128,1024]{1,0:T(8,128)S(1)} custom-call(s32[2]{0:T(128)S(1)} %pad_add_fusion.place_ref, s32[6,32]{1,0:T(8,128)S(1)} %bitcast.67, bf16[128,4096]{1,0:T(8,128)(2,1)S(1)} %copy-done.1, bf16[8,6,128,128]{3,2,1,0:T(8,128)(2,1)S(1)} %get-tuple-element.108.blocks_ref), custom_call_target="tpu_custom_call" | custom-call | flops 201326592 | bytes 2359296 | tf_op jit(solution)/shard_map/near_late/pallas_call | solution.py:160
  33.4 0.2 fusion.43
  33.6 1.3 %near_left.1.refs_6_ = f32[128,1024]{1,0:T(8,128)S(1)} custom-call(s32[2]{0:T(128)S(1)} %pad_add_fusion.place_ref, s32[6,32]{1,0:T(8,128)S(1)} %bitcast.68, bf16[128,4096]{1,0:T(8,128)(2,1)S(1)} %copy-done.1, bf16[128,512]{1,0:T(8,128)(2,1)S(1)} %collective-permute-done.2.inner_ref, bf16[128,512]{1,0:T(8,128)(2,1)S(1)} %collective-permute-done.7.outer_ref, ...), custom_call_target="tpu_custom_call" | custom-call | flops 201326592 | bytes 2359296 | tf_op jit(solution)/shard_map/near_left/pallas_call | solution.py:160
  34.9 1.6 %collective-permute-done.6 = f32[64,128]{1,0:T(8,128)S(1)} collective-permute-done((f32[64,128]{1,0:T(8,128)S(1)}, f32[64,128]{1,0:T(8,128)S(1)}, u32[]{:S(2)}, u32[]{:S(2)}) %collective-permute-start.6) | collective-permute-done | bytes 32800 | tf_op jit(solution)/shard_map/ppermute | solution.py:25
  36.5 0.2 fusion.44
  36.8 1.2 %collective-permute-start.10 = (f32[64,128]{1,0:T(8,128)S(1)}, f32[64,128]{1,0:T(8,128)S(1)}, u32[]{:S(2)}, u32[]{:S(2)}) collective-permute-start(f32[64,128]{1,0:T(8,128)S(1)} %add.35), channel_id=1, source_target_pairs={{0,128},{4,132},{8,136},{12,140},{16,144},{20,148},{24,152},{28,15... | collective-permute-start | bytes 98312 | tf_op jit(solution)/shard_map/ppermute | solution.py:25
  38.0 2.1 %collective-permute-start.9 = (f32[64,128]{1,0:T(8,128)S(1)}, f32[64,128]{1,0:T(8,128)S(1)}, u32[]{:S(2)}, u32[]{:S(2)}) collective-permute-start(f32[64,128]{1,0:T(8,128)S(1)} %add.35), channel_id=1, source_target_pairs={{0,192},{4,196},{8,200},{12,204},{16,208},{20,212},{24,216},{28,22... | collective-permute-start | bytes 98312 | tf_op jit(solution)/shard_map/ppermute | solution.py:25
  40.1 0.3 collective-permute-start.8
  40.4 0.4 fusion.partial_ref
  40.7 0.2 slice.76.blocks_ref
  40.9 1.3 %near_right.1.refs_9_ = f32[128,1024]{1,0:T(8,128)S(1)} custom-call(s32[2]{0:T(128)S(1)} %pad_add_fusion.place_ref, s32[6,32]{1,0:T(8,128)S(1)} %bitcast.69, bf16[128,4096]{1,0:T(8,128)(2,1)S(1)} %copy-done.1, bf16[128,512]{1,0:T(8,128)(2,1)S(1)} %collective-permute-done.2.inner_ref, bf16[128,512]{1,0:T(8,128)(2,1)S(1)} %collective-permute-done.7.outer_ref, ...), custom_call_target="tpu_custom_call" | custom-call | flops 201326592 | bytes 2359296 | tf_op jit(solution)/shard_map/near_right/pallas_call | solution.py:160
  42.3 0.8 %collective-permute-done.9.refs_1_ = f32[64,128]{1,0:T(8,128)S(1)} collective-permute-done((f32[64,128]{1,0:T(8,128)S(1)}, f32[64,128]{1,0:T(8,128)S(1)}, u32[]{:S(2)}, u32[]{:S(2)}) %collective-permute-start.9) | collective-permute-done | bytes 32800 | tf_op jit(solution)/shard_map/ppermute | solution.py:25
  43.1 0.9 %collective-permute-done.8.refs_0_ = f32[64,128]{1,0:T(8,128)S(1)} collective-permute-done((f32[64,128]{1,0:T(8,128)S(1)}, f32[64,128]{1,0:T(8,128)S(1)}, u32[]{:S(2)}, u32[]{:S(2)}) %collective-permute-start.8) | collective-permute-done | bytes 32800 | tf_op jit(solution)/shard_map/ppermute | solution.py:25
  44.0 2.0 %add_far.1 = f32[128,4096]{1,0:T(8,128)} custom-call(f32[64,128]{1,0:T(8,128)S(1)} %fusion.partial_ref, f32[64,128]{1,0:T(8,128)S(1)} %collective-permute-done.8.refs_0_, f32[64,128]{1,0:T(8,128)S(1)} %collective-permute-done.9.refs_1_, f32[64,128]{1,0:T(8,128)S(1)} %collective-permute-done.10.refs_2_, f32[64,64]{1,0:T(8,128)S(1)} %fusion.35.refs_3_, ...), custom_call_target="tpu_custom_call" | custom-call | flops 67108864 | bytes 4718592 | tf_op jit(solution)/shard_map/add_far/pallas_call | solution.py:201
  (38 shorter events, 0.5 us)
Async XLA Ops:
  0.0 4.3 %copy-start = (bf16[126,64,64]{0,2,1:T(8,128)(2,1)S(1)}, bf16[126,64,64]{0,2,1:T(8,128)(2,1)}, u32[]{:S(2)}) copy-start(bf16[126,64,64]{0,2,1:T(8,128)(2,1)} %param.15) | copy-start | bytes 3096580
  0.0 4.3 %copy-start.9 = (s32[6]{0:T(128)S(1)}, s32[6]{0:T(128)}, u32[]{:S(2)}) copy-start(s32[6]{0:T(128)} %constant.28.clone) | copy-start | bytes 76
  0.0 4.3 %copy-start.6 = (s32[11]{0:T(128)S(1)}, s32[11]{0:T(128)}, u32[]{:S(2)}) copy-start(s32[11]{0:T(128)} %constant.27.clone) | copy-start | bytes 136
  0.0 4.3 %copy-start.7 = (s32[11]{0:T(128)S(1)}, s32[11]{0:T(128)}, u32[]{:S(2)}) copy-start(s32[11]{0:T(128)} %constant.26.clone) | copy-start | bytes 136
  0.0 4.3 %copy-start.8 = (s32[11]{0:T(128)S(1)}, s32[11]{0:T(128)}, u32[]{:S(2)}) copy-start(s32[11]{0:T(128)} %constant.25.clone) | copy-start | bytes 136
  2.2 7.6 %copy-start.5 = (bf16[126,64,64]{0,2,1:T(8,128)(2,1)S(1)}, bf16[126,64,64]{0,2,1:T(8,128)(2,1)}, u32[]{:S(2)}) copy-start(bf16[126,64,64]{0,2,1:T(8,128)(2,1)} %param.16) | copy-start | bytes 3096580
  2.2 4.2 %collective-permute-start = (f32[64,128]{1,0:T(8,128)S(1)}, f32[64,128]{1,0:T(8,128)S(1)}, u32[]{:S(2)}, u32[]{:S(2)}) collective-permute-start(f32[64,128]{1,0:T(8,128)S(1)} %get-tuple-element.56), channel_id=1, source_target_pairs={{0,1},{1,0},{2,3},{3,2},{4,5},{5,4},{6,7},{7,6},{8,9},{9,8},{10,11... | collective-permute-start | bytes 98312 | tf_op jit(solution)/shard_map/ppermute | solution.py:25
  3.9 7.9 %collective-permute-start.2 = (bf16[128,512]{1,0:T(8,128)(2,1)S(1)}, bf16[128,512]{1,0:T(8,128)(2,1)S(1)}, u32[]{:S(2)}, u32[]{:S(2)}) collective-permute-start(bf16[128,512]{1,0:T(8,128)(2,1)S(1)} %get-tuple-element.60), channel_id=1, source_target_pairs={{0,1},{1,0},{2,3},{3,2},{4,5},{5,4},{6,7},{7,6},{8,9},{9,8},{10,11... | collective-permute-start | bytes 393224 | tf_op jit(solution)/shard_map/ppermute | solution.py:30
  6.4 5.4 %collective-permute-start.1 = (f32[64,128]{1,0:T(8,128)S(1)}, f32[64,128]{1,0:T(8,128)S(1)}, u32[]{:S(2)}, u32[]{:S(2)}) collective-permute-start(f32[64,128]{1,0:T(8,128)S(1)} %add.29), channel_id=1, source_target_pairs={{0,3},{1,2},{2,1},{3,0},{4,7},{5,6},{6,5},{7,4},{8,11},{9,10},{10,... | collective-permute-start | bytes 98312 | tf_op jit(solution)/shard_map/ppermute | solution.py:25
  11.8 1.3 %collective-permute-start.3 = (f32[64,128]{1,0:T(8,128)S(1)}, f32[64,128]{1,0:T(8,128)S(1)}, u32[]{:S(2)}, u32[]{:S(2)}) collective-permute-start(f32[64,128]{1,0:T(8,128)S(1)} %add.31), channel_id=1, source_target_pairs={{0,4},{4,0},{8,12},{12,8},{16,20},{20,16},{24,28},{28,24},{32,36},... | collective-permute-start | bytes 98312 | tf_op jit(solution)/shard_map/ppermute | solution.py:25
  13.3 15.6 %copy-start.1 = (bf16[128,4096]{1,0:T(8,128)(2,1)S(1)}, bf16[128,4096]{1,0:T(8,128)(2,1)}, u32[]{:S(2)}) copy-start(bf16[128,4096]{1,0:T(8,128)(2,1)} %sources_ref.3) | copy-start | bytes 3145732
  13.3 15.6 %copy-start.3 = (s32[32,6]{0,1:T(8,128)S(1)}, s32[32,6]{0,1:T(8,128)}, u32[]{:S(2)}) copy-start(s32[32,6]{0,1:T(8,128)} %param.13) | copy-start | bytes 2308
  13.3 4.8 %collective-permute-start.4 = (f32[64,128]{1,0:T(8,128)S(1)}, f32[64,128]{1,0:T(8,128)S(1)}, u32[]{:S(2)}, u32[]{:S(2)}) collective-permute-start(f32[64,128]{1,0:T(8,128)S(1)} %add.32), channel_id=1, source_target_pairs={{0,8},{4,12},{8,0},{12,4},{16,24},{20,28},{24,16},{28,20},{32,40},... | collective-permute-start | bytes 98312 | tf_op jit(solution)/shard_map/ppermute | solution.py:25
  15.3 16.4 %copy-start.4 = (bf16[32,6,128,128]{3,2,1,0:T(8,128)(2,1)S(1)}, bf16[32,6,128,128]{3,2,1,0:T(8,128)(2,1)}, u32[]{:S(2)}) copy-start(bf16[32,6,128,128]{3,2,1,0:T(8,128)(2,1)} %param.12) | copy-start | bytes 18874372
  18.4 11.7 %collective-permute-start.5 = (f32[64,128]{1,0:T(8,128)S(1)}, f32[64,128]{1,0:T(8,128)S(1)}, u32[]{:S(2)}, u32[]{:S(2)}) collective-permute-start(f32[64,128]{1,0:T(8,128)S(1)} %add.33), channel_id=1, source_target_pairs={{0,16},{4,20},{8,24},{12,28},{16,0},{20,4},{24,8},{28,12},{32,48},... | collective-permute-start | bytes 98312 | tf_op jit(solution)/shard_map/ppermute | solution.py:25
  22.0 11.6 %collective-permute-start.7 = (bf16[128,512]{1,0:T(8,128)(2,1)S(1)}, bf16[128,512]{1,0:T(8,128)(2,1)S(1)}, u32[]{:S(2)}, u32[]{:S(2)}) collective-permute-start(bf16[128,512]{1,0:T(8,128)(2,1)S(1)} %get-tuple-element.88), channel_id=1, source_target_pairs={{1,2},{3,4},{5,6},{7,8},{9,10},{11,12},{13,14},{15,16},{17,18},{19... | collective-permute-start | bytes 393224 | tf_op jit(solution)/shard_map/ppermute | solution.py:36
  30.4 6.1 %collective-permute-start.6 = (f32[64,128]{1,0:T(8,128)S(1)}, f32[64,128]{1,0:T(8,128)S(1)}, u32[]{:S(2)}, u32[]{:S(2)}) collective-permute-start(f32[64,128]{1,0:T(8,128)S(1)} %add.34), channel_id=1, source_target_pairs={{0,48},{4,52},{8,56},{12,60},{16,32},{20,36},{24,40},{28,44},{32,1... | collective-permute-start | bytes 98312 | tf_op jit(solution)/shard_map/ppermute | solution.py:25
  36.8 5.5 %collective-permute-start.10 = (f32[64,128]{1,0:T(8,128)S(1)}, f32[64,128]{1,0:T(8,128)S(1)}, u32[]{:S(2)}, u32[]{:S(2)}) collective-permute-start(f32[64,128]{1,0:T(8,128)S(1)} %add.35), channel_id=1, source_target_pairs={{0,128},{4,132},{8,136},{12,140},{16,144},{20,148},{24,152},{28,15... | collective-permute-start | bytes 98312 | tf_op jit(solution)/shard_map/ppermute | solution.py:25
  38.0 5.1 %collective-permute-start.9 = (f32[64,128]{1,0:T(8,128)S(1)}, f32[64,128]{1,0:T(8,128)S(1)}, u32[]{:S(2)}, u32[]{:S(2)}) collective-permute-start(f32[64,128]{1,0:T(8,128)S(1)} %add.35), channel_id=1, source_target_pairs={{0,192},{4,196},{8,200},{12,204},{16,208},{20,212},{24,216},{28,22... | collective-permute-start | bytes 98312 | tf_op jit(solution)/shard_map/ppermute | solution.py:25
  40.1 3.9 %collective-permute-start.8 = (f32[64,128]{1,0:T(8,128)S(1)}, f32[64,128]{1,0:T(8,128)S(1)}, u32[]{:S(2)}, u32[]{:S(2)}) collective-permute-start(f32[64,128]{1,0:T(8,128)S(1)} %add.35), channel_id=1, source_target_pairs={{0,64},{4,68},{8,72},{12,76},{16,80},{20,84},{24,88},{28,92},{32,9... | collective-permute-start | bytes 98312 | tf_op jit(solution)/shard_map/ppermute | solution.py:25
  40.9 3.1 %copy-start.2 = (bf16[32,64,128]{2,1,0:T(8,128)(2,1)S(1)}, bf16[32,64,128]{2,1,0:T(8,128)(2,1)}, u32[]{:S(2)}) copy-start(bf16[32,64,128]{2,1,0:T(8,128)(2,1)} %refs_10_.1) | copy-start | bytes 1572868

commit v4 on v3

v4 whole, which is shorter than its diff:
```python
import functools

import jax
import jax.numpy as jnp
import numpy as np
from jax import lax
from jax.experimental import pallas as pl
from jax.experimental.pallas import tpu as pltpu
from jax.sharding import PartitionSpec as P

REACH = 4
PIECES = {"left": (0, 8), "middle": (8, 16), "right": (24, 8)}
VMEM_BYTES = 16 * 1024 * 1024
NEAR_VMEM_BYTES = 16 * 1024 * 1024
MOMENT_VMEM_BYTES = 54784 * 1024

highest = lax.Precision.HIGHEST
AXES = ("leaf", "blk")
NT = (((1,), (1,)), ((), ()))
TN = (((0,), (0,)), ((), ()))


def device_index():
    return lax.axis_index("leaf") * lax.axis_size("blk") + lax.axis_index("blk")


def xor_permute(value, axis, mask):
    pairs = [(source, source ^ mask) for source in range(lax.axis_size(axis))]
    return lax.ppermute(value, axis, pairs)


def inner_exchange(value):
    count = lax.axis_size(AXES)
    return lax.ppermute(value, AXES, [(i, i ^ 1) for i in range(count)])


def outer_exchange(value):
    count = lax.axis_size(AXES)
    pairs = [(i, i + 1) for i in range(1, count - 1, 2)]
    return lax.ppermute(value, AXES, pairs + [(b, a) for a, b in pairs])


def moment_kernel(sources_hbm, basis_hbm, moment_ref, inner_ref, outer_ref, sources, basis, sems):
    chunks = sources.shape[0]
    clusters = basis.shape[0] // chunks
    panels = sources.shape[2]
    width = inner_ref.shape[1]
    copies = []
    for k in range(chunks):
        own = slice(k * clusters, (k + 1) * clusters)
        copies.append(
            (
                pltpu.make_async_copy(
                    sources_hbm.at[:, k * panels : (k + 1) * panels], sources.at[k], sems.at[2 * k]
                ),
                pltpu.make_async_copy(basis_hbm.at[own], basis.at[own], sems.at[2 * k + 1]),
            )
        )
        for copy in copies[-1]:
            copy.start()
    total = jnp.zeros(moment_ref.shape, jnp.float32)
    for k in range(chunks):
        for copy in copies[k]:
            copy.wait()
        flat = jnp.concatenate([basis[k * clusters + c] for c in range(clusters)], axis=1)
        total += lax.dot_general(flat, sources[k], NT, preferred_element_type=jnp.float32)
    moment_ref[...] = total
    odd = lax.rem(device_index(), 2)

    @pl.when(odd == 0)
    def _():
        inner_ref[...] = sources[chunks - 1, :, panels - width :]
        outer_ref[...] = sources[0, :, :width]

    @pl.when(odd != 0)
    def _():
        inner_ref[...] = sources[0, :, :width]
        outer_ref[...] = sources[chunks - 1, :, panels - width :]


def moments(sources, basis, width, chunks=4):
    rhs, panels = sources.shape
    clusters, rank, panel = basis.shape
    vmem = pl.BlockSpec(memory_space=pltpu.VMEM)
    hbm = pl.BlockSpec(memory_space=pltpu.HBM)
    return pl.pallas_call(
        moment_kernel,
        in_specs=[hbm, hbm],
        out_specs=[vmem] * 3,
        out_shape=[
            jax.ShapeDtypeStruct((rank, rhs), jnp.float32),
            jax.ShapeDtypeStruct((rhs, width), sources.dtype),
            jax.ShapeDtypeStruct((rhs, width), sources.dtype),
        ],
        scratch_shapes=[
            pltpu.VMEM((chunks, rhs, panels // chunks), sources.dtype),
            pltpu.VMEM((clusters, rank, panel), basis.dtype),
            pltpu.SemaphoreType.DMA((2 * chunks,)),
        ],
        compiler_params=pltpu.CompilerParams(vmem_limit_bytes=MOMENT_VMEM_BYTES),
        cost_estimate=pl.CostEstimate(
            flops=2 * rhs * panels * rank, bytes_accessed=2 * panels * (rhs + rank), transcendentals=0
        ),
        name="moments",
    )(sources, basis)


def near_products(columns_ref, panels_ref, near_ref, blocks_ref, first, base):
    quarter_clusters, near_count, panel, _ = blocks_ref.shape
    for c in range(quarter_clusters):
        picked = []
        for slot in range(near_count):
            column = columns_ref[slot, first + c] - base
            picked.append(panels_ref[:, pl.ds(pl.multiple_of(column * panel, panel), panel)])
        near_ref[:, c * panel : (c + 1) * panel] = jnp.dot(
            jnp.concatenate(picked, axis=1),
            blocks_ref[c].reshape(near_count * panel, panel),
            preferred_element_type=jnp.float32,
        )


def middle_kernel(first, own_clusters, columns_ref, sources_ref, blocks_ref, near_ref):
    near_products(columns_ref, sources_ref, near_ref, blocks_ref, first, device_index() * own_clusters)


def edge_kernel(
    own_clusters,
    columns_ref,
    sources_ref,
    inner_ref,
    outer_ref,
    left_blocks,
    right_blocks,
    left_ref,
    right_ref,
    left_window,
    right_window,
):
    width = inner_ref.shape[1]
    panels = sources_ref.shape[1]
    panel = left_blocks.shape[2]
    reach = left_window.shape[1] - width
    device = device_index()
    odd = lax.rem(device, 2)
    left_window[:, width:] = sources_ref[:, :reach]
    right_window[:, :reach] = sources_ref[:, panels - reach :]

    @pl.when(odd == 0)
    def _():
        left_window[:, :width] = outer_ref[...]
        right_window[:, reach:] = inner_ref[...]

    @pl.when(odd != 0)
    def _():
        left_window[:, :width] = inner_ref[...]
        right_window[:, reach:] = outer_ref[...]

    first = device * own_clusters
    near_products(columns_ref, left_window, left_ref, left_blocks, 0, first - width // panel)
    near_products(
        columns_ref,
        right_window,
        right_ref,
        right_blocks,
        PIECES["right"][0],
        first + (panels - reach) // panel,
    )


def take(blocks, piece):
    first, count = piece
    return blocks[first : first + count]


def near_pieces(columns, sources, beside, blocks, name):
    rhs, panels = sources.shape
    _, near_count, panel, _ = blocks[0].shape
    smem = pl.BlockSpec(memory_space=pltpu.SMEM)
    vmem = pl.BlockSpec(memory_space=pltpu.VMEM)
    widths = [piece.shape[0] * panel for piece in blocks]
    if beside:
        kernel = functools.partial(edge_kernel, panels // panel)
        halo = beside[0].shape[1]
        scratch = [pltpu.VMEM((rhs, width + 2 * halo), sources.dtype) for width in widths]
    else:
        kernel = functools.partial(middle_kernel, PIECES["middle"][0], panels // panel)
        scratch = []
    return pl.pallas_call(
        kernel,
        in_specs=[smem] + [vmem] * (1 + len(beside) + len(blocks)),
        out_specs=[vmem] * len(blocks),
        out_shape=[jax.ShapeDtypeStruct((rhs, width), jnp.float32) for width in widths],
        scratch_shapes=scratch,
        compiler_params=pltpu.CompilerParams(vmem_limit_bytes=NEAR_VMEM_BYTES),
        cost_estimate=pl.CostEstimate(
            flops=2 * rhs * sum(widths) * near_count * panel,
            bytes_accessed=sum(widths) * (2 * near_count * panel + 6 * rhs),
            transcendentals=0,
        ),
        name=name,
    )(columns, sources, *beside, *blocks)


def far_kernel(count, partial_ref, *refs):
    *near_refs, basis_ref, out_hbm, total, sems = refs[2 * count :]
    descended = partial_ref[...]
    for value_ref, matrix_ref in zip(refs[:count], refs[count : 2 * count]):
        descended += lax.dot_general(
            matrix_ref[...], value_ref[...], TN, precision=highest, preferred_element_type=jnp.float32
        )
    leaf_local = descended.T.astype(basis_ref.dtype)
    panel = basis_ref.shape[2]
    copies = []
    start = 0
    for k, near_ref in enumerate(near_refs):
        own = slice(start, start + near_ref.shape[1])
        start = own.stop
        flat = jnp.concatenate([basis_ref[c] for c in range(own.start // panel, own.stop // panel)], axis=1)
        total[:, own] = near_ref[...] + jnp.dot(leaf_local, flat, preferred_element_type=jnp.float32)
        copy = pltpu.make_async_copy(total.at[:, own], out_hbm.at[:, own], sems.at[k])
        copy.start()
        copies.append(copy)
    for copy in copies:
        copy.wait()


def add_far(partial, last, matrices, near, basis):
    rhs = partial.shape[1]
    clusters, rank, panel = basis.shape
    vmem = pl.BlockSpec(memory_space=pltpu.VMEM)
    return pl.pallas_call(
        functools.partial(far_kernel, len(last)),
        in_specs=[vmem] * (2 + 2 * len(last) + len(near)),
        out_specs=pl.BlockSpec(memory_space=pltpu.HBM),
        out_shape=jax.ShapeDtypeStruct((rhs, clusters * panel), jnp.float32),
        scratch_shapes=[
            pltpu.VMEM((rhs, clusters * panel), jnp.float32),
            pltpu.SemaphoreType.DMA((len(near),)),
        ],
        compiler_params=pltpu.CompilerParams(vmem_limit_bytes=VMEM_BYTES),
        cost_estimate=pl.CostEstimate(
            flops=2 * rhs * clusters * panel * rank,
            bytes_accessed=clusters * panel * (8 * rhs + 2 * rank),
            transcendentals=0,
        ),
        name="add_far",
    )(partial, *last, *matrices, *near, basis)


def matmul(left, right):
    return jnp.dot(left, right, precision=highest, preferred_element_type=jnp.float32)


def matmul_tn(left, right):
    return lax.dot_general(left, right, TN, precision=highest, preferred_element_type=jnp.float32)


def pick_rows(table, rows):
    one_hot = (rows[:, None] == jnp.arange(table.shape[0], dtype=rows.dtype)[None, :]).astype(table.dtype)
    return jnp.einsum("nkj,sn->skj", table, one_hot, preferred_element_type=jnp.float32)


def together(*values):
    return lax.optimization_barrier(values)


def body(sources, near_blocks, near_cols, basis, transfer, coupling):
    panel_size = near_blocks.shape[2]
    leaf_count = lax.axis_size("leaf")
    levels = leaf_count.bit_length() - 1
    leaf_index = lax.axis_index("leaf")
    columns = near_cols.T

    below_top = levels - 2
    shifts = np.array([*range(levels - 1), *range(below_top), below_top, below_top], np.int32)
    flips = np.array([0] * (levels - 1) + [1] * below_top + [3, 2], np.int32)
    rows = ((leaf_count >> shifts) - 2) + (jnp.right_shift(leaf_index, shifts) ^ flips)
    rows = rows.astype(jnp.int32)
    mine_shifts = np.arange(levels, dtype=np.int32)
    mine_rows = ((leaf_count >> mine_shifts) - 2) + jnp.right_shift(leaf_index, mine_shifts)
    mine_rows = mine_rows.astype(jnp.int32)

    moment, inner_send, outer_send = moments(sources, basis, REACH * panel_size)

    inner_clusters = inner_exchange(inner_send)
    other = xor_permute(moment, "blk", 1)
    moves = pick_rows(transfer, rows)
    other, moves = together(other, moves)
    current = moment + other

    current, coupling = together(current, coupling)
    other = xor_permute(current, "blk", 3)
    couples = pick_rows(coupling, mine_rows)
    other, couples, inner_clusters = together(other, couples, inner_clusters)
    current = current + other

    chains = [moves[0].T]
    for step in range(1, levels - 1):
        chains.append(matmul_tn(moves[step], chains[-1]))
    down = [couples[0]]
    for step in range(1, below_top - 1):
        down.append(matmul(couples[step], chains[step - 1]))

    siblings = []
    for level, mask in enumerate([1, 2, 4, 12]):
        if level == 1:
            current, middle_blocks = together(current, near_blocks)
        elif level == 2:
            current, middle_sources = together(current, sources)
        elif level == 3:
            current, outer_send = together(current, outer_send)
        sibling = xor_permute(current, "leaf", mask)
        ready = current
        extras = []
        if level == 1:
            mine, middle_blocks = together(matmul_tn(moves[level], current), middle_blocks)
            extras = [take(middle_blocks, PIECES["middle"]), mine]
        elif level == 2:
            (middle,) = near_pieces(columns, middle_sources, (), [middle_blocks], "near_middle")
            ready, middle, top_couples, top_chains = together(
                current, middle, couples[below_top - 1 :], chains[below_top - 2 :]
            )
            tops = [matmul(couple, top) for couple, top in zip(top_couples, top_chains)]
            cousins = [matmul(moves[levels - 1 + below_top + k], tops[-1]) for k in range(2)]
            extras = [middle, *tops, *cousins]
        elif level == 3:
            outer_clusters = outer_exchange(outer_send)
        if level != 1:
            extras.append(matmul_tn(moves[level], ready))
        sibling, *extras = together(sibling, *extras)
        if level == 1:
            middle_blocks = extras[0]
        elif level == 2:
            middle = extras[0]
            down += extras[1:4]
            cousins = extras[4:6]
        siblings.append(sibling)
        current = extras[-1] + matmul_tn(moves[levels - 1 + level], sibling)

    current, last_sources, last_blocks = together(current, sources, near_blocks)
    last = [xor_permute(current, "leaf", mask) for mask in (16, 48, 32)]
    left, right = near_pieces(
        columns,
        last_sources,
        (inner_clusters, outer_clusters),
        [take(last_blocks, PIECES["left"]), take(last_blocks, PIECES["right"])],
        "near_edges",
    )
    collected = matmul_tn(jnp.concatenate(down[:below_top]), jnp.concatenate(siblings))
    *last, left, right, collected = together(*last, left, right, collected)
    return add_far(collected, last, [down[below_top], *cousins], [left, middle, right], basis)


def solution(mesh):
    return jax.shard_map(
        body,
        mesh=mesh,
        in_specs=(
            P(None, ("leaf", "blk")),
            P(("leaf", "blk"), None, None, None),
            P(("leaf", "blk"), None),
            P(("leaf", "blk"), None, None),
            P(),
            P(),
        ),
        out_specs=P(None, ("leaf", "blk")),
        check_vma=False,
    )
```

time: 46.1 us -> 45.4 us (0.985)
  the two profiles are of different devices: /device:TPU:6 before, /device:TPU:1 now
where the time goes in v4:
time: 45.4 us; the launch traced here: 45.3 us
  starting transfers between devices  25.4 us (56%)
  Pallas kernels  7.75 us (17%)
  matrix products  6.2 us (14%)
  local copies, waits for them, and re-layouts  3.3 us (7%)
  waiting for transfers between devices  1.4 us (3%)
  other arithmetic  0.74 us (2%)
    ppermute x9, starting transfers between devices, xor_permute(): return lax.ppermute(value, axis, pairs)  19.1 us
    ppermute x1, starting transfers between devices, outer_exchange(): return lax.ppermute(value, AXES, pairs + [(b, a) for a, b in pairs])  6.23 us
    pallas_call x2, Pallas kernels, near_pieces(): pl.pallas_call(kernel, in_specs=[smem] + [vmem] * (1 + len(beside) + len(...  3.52 us
    dot_general x13, matrix products, matmul_tn(): lax.dot_general(left, right, TN, precision=highest, preferred_element_typ...  3.22 us
    slice x2, local copies, waits for them, and re-layouts, take(): return blocks[first:first + count]  2.83 us
    pallas_call x1, Pallas kernels, moments(): pl.pallas_call(moment_kernel, in_specs=[hbm, hbm], out_specs=[vmem] * 3,...  2.18 us
    pallas_call x1, Pallas kernels, add_far(): pl.pallas_call(functools.partial(far_kernel, len(last)), in_specs=[vmem]...  2.05 us
    dot_general x2, matrix products, pick_rows(): jnp.einsum('nkj,sn->skj', table, one_hot, preferred_element_type=jnp.floa...  1.83 us
  transfers between devices with their start and end apart: 11, of which 2 were waited for; matrix products, arithmetic and copies ran while one was open for 20% of the time, Pallas kernels for 8%

profile of v4, /device:TPU:1, one launch (start us, length us, event | category | flops | bytes accessed | tf_op | source)
XLA Modules:
  0.0 45.3 jit_solution(18303109353332244656)
XLA Ops:
  0.0 2.2 %moments.1 = (f32[64,128]{1,0:T(8,128)S(1)}, bf16[128,512]{1,0:T(8,128)(2,1)S(1)}, bf16[128,512]{1,0:T(8,128)(2,1)S(1)}) custom-call(bf16[128,4096]{1,0:T(8,128)(2,1)} %sources_ref.1, bf16[32,64,128]{2,1,0:T(8,128)(2,1)} %refs_9_.1), custom_call_target="tpu_custom_call" | custom-call | flops 67108864 | bytes 1572864 | tf_op jit(solution)/shard_map/moments/pallas_call | solution.py:86
  2.2 2.2 %collective-permute-start = (f32[64,128]{1,0:T(8,128)S(1)}, f32[64,128]{1,0:T(8,128)S(1)}, u32[]{:S(2)}, u32[]{:S(2)}) collective-permute-start(f32[64,128]{1,0:T(8,128)S(1)} %get-tuple-element.54), channel_id=1, source_target_pairs={{0,1},{1,0},{2,3},{3,2},{4,5},{5,4},{6,7},{7,6},{8,9},{9,8},{10,11... | collective-permute-start | bytes 98312 | tf_op jit(solution)/shard_map/ppermute | solution.py:29
  4.4 0.1 collective-permute-start.2
  4.5 0.7 %xor_add_fusion = s32[11]{0:T(128)S(1)} fusion(s32[11]{0:T(128)} %constant.18.clone, s32[11]{0:T(128)} %constant.17.clone, s32[11]{0:T(128)} %constant.16.clone, s32[]{:T(128)S(6)} %axis_index.15), kind=kLoop, calls=%fused_computation.24 | loop fusion | flops 33 | bytes 180 | tf_op jit(solution)/shard_map/add | solution.py:277
  5.2 0.9 %fusion.16 = f32[11,64,64]{2,0,1:T(8,128)S(1)} fusion(bf16[126,64,64]{0,2,1:T(8,128)(2,1)S(1)} %copy-done, s32[11]{0:T(128)S(1)} %xor_add_fusion), kind=kOutput, calls=%fused_computation.17 | convolution fusion | flops 11355498 | bytes 1212460 | tf_op jit(solution)/shard_map/nkj,sn->skj/dot_general | solution.py:260
  6.2 2.9 %collective-permute-start.1 = (f32[64,128]{1,0:T(8,128)S(1)}, f32[64,128]{1,0:T(8,128)S(1)}, u32[]{:S(2)}, u32[]{:S(2)}) collective-permute-start(f32[64,128]{1,0:T(8,128)S(1)} %add.25), channel_id=1, source_target_pairs={{0,3},{1,2},{2,1},{3,0},{4,7},{5,6},{6,5},{7,4},{8,11},{9,10},{10,... | collective-permute-start | bytes 98312 | tf_op jit(solution)/shard_map/ppermute | solution.py:29
  9.1 0.3 fusion.25
  9.4 0.0 slice-start
  9.4 0.9 %fusion.20 = f32[6,64,64]{2,0,1:T(8,128)S(1)} fusion(bf16[126,64,64]{0,2,1:T(8,128)(2,1)S(1)} %copy-done.4, s32[6]{0:T(128)S(1)} %shift-right-arithmetic_add_fusion), kind=kOutput, calls=%fused_computation.21 | convolution fusion | flops 6193908 | bytes 1130520 | tf_op jit(solution)/shard_map/nkj,sn->skj/dot_general | solution.py:260
  10.3 0.3 fusion.32
  10.6 0.2 fusion.33
  10.8 0.2 fusion.34
  11.0 0.2 fusion.35
  11.3 0.2 fusion.28
  11.6 3.3 %collective-permute-start.3 = (f32[64,128]{1,0:T(8,128)S(1)}, f32[64,128]{1,0:T(8,128)S(1)}, u32[]{:S(2)}, u32[]{:S(2)}) collective-permute-start(f32[64,128]{1,0:T(8,128)S(1)} %add.27), channel_id=1, source_target_pairs={{0,4},{4,0},{8,12},{12,8},{16,20},{20,16},{24,28},{28,24},{32,36},... | collective-permute-start | bytes 98312 | tf_op jit(solution)/shard_map/ppermute | solution.py:29
  14.9 0.1 fusion.26
  15.0 0.2 fusion.46
  15.2 0.2 fusion.45
  15.4 0.4 collective-permute-done.3
  15.8 0.2 fusion.29
  16.0 0.4 collective-permute-start.4
  16.5 0.2 fusion.30
  16.7 0.0 copy-start.1
  16.7 0.0 slice-start.1
  16.7 2.4 %slice.61.blocks_ref = bf16[16,6,128,128]{3,2,1,0:T(8,128)(2,1)S(1)} slice(bf16[32,6,128,128]{3,2,1,0:T(8,128)(2,1)} %param.12), slice={[8:24], [0:6], [0:128], [0:128]} | slice | bytes 6291456 | tf_op jit(solution)/shard_map/slice | solution.py:172
  19.2 0.2 fusion.31
  19.4 3.1 %collective-permute-start.5 = (f32[64,128]{1,0:T(8,128)S(1)}, f32[64,128]{1,0:T(8,128)S(1)}, u32[]{:S(2)}, u32[]{:S(2)}) collective-permute-start(f32[64,128]{1,0:T(8,128)S(1)} %add.29), channel_id=1, source_target_pairs={{0,16},{4,20},{8,24},{12,28},{16,0},{20,4},{24,8},{28,12},{32,48},... | collective-permute-start | bytes 98312 | tf_op jit(solution)/shard_map/ppermute | solution.py:29
  22.5 1.7 %near_middle.1.refs_7_ = f32[128,2048]{1,0:T(8,128)S(1)} custom-call(s32[6,32]{1,0:T(8,128)S(1)} %bitcast.64, bf16[128,4096]{1,0:T(8,128)(2,1)S(1)} %copy-done.1, bf16[16,6,128,128]{3,2,1,0:T(8,128)(2,1)S(1)} %slice.61.blocks_ref), custom_call_target="tpu_custom_call" | custom-call | flops 402653184 | bytes 4718592 | tf_op jit(solution)/shard_map/near_middle/pallas_call | solution.py:188
  24.3 0.2 fusion.41
  24.5 0.1 fusion.27
  24.6 0.2 fusion.38
  24.7 0.2 fusion.40.refs_5_
  24.9 0.2 fusion.39.refs_4_
  25.1 0.2 fusion.37.refs_3_
  25.2 0.2 fusion.36
  25.4 0.2 fusion.42
  25.7 3.4 %collective-permute-start.6 = (f32[64,128]{1,0:T(8,128)S(1)}, f32[64,128]{1,0:T(8,128)S(1)}, u32[]{:S(2)}, u32[]{:S(2)}) collective-permute-start(f32[64,128]{1,0:T(8,128)S(1)} %add.30), channel_id=1, source_target_pairs={{0,48},{4,52},{8,56},{12,60},{16,32},{20,36},{24,40},{28,44},{32,1... | collective-permute-start | bytes 98312 | tf_op jit(solution)/shard_map/ppermute | solution.py:29
  29.1 0.2 fusion.43
  29.3 6.2 %collective-permute-start.10 = (bf16[128,512]{1,0:T(8,128)(2,1)S(1)}, bf16[128,512]{1,0:T(8,128)(2,1)S(1)}, u32[]{:S(2)}, u32[]{:S(2)}) collective-permute-start(bf16[128,512]{1,0:T(8,128)(2,1)S(1)} %get-tuple-element.88), channel_id=1, source_target_pairs={{1,2},{3,4},{5,6},{7,8},{9,10},{11,12},{13,14},{15,16},{17,18},{19... | collective-permute-start | bytes 393224 | tf_op jit(solution)/shard_map/ppermute | solution.py:40
  35.6 0.2 fusion.44
  35.8 1.3 %collective-permute-start.7 = (f32[64,128]{1,0:T(8,128)S(1)}, f32[64,128]{1,0:T(8,128)S(1)}, u32[]{:S(2)}, u32[]{:S(2)}) collective-permute-start(f32[64,128]{1,0:T(8,128)S(1)} %add.31), channel_id=1, source_target_pairs={{0,64},{4,68},{8,72},{12,76},{16,80},{20,84},{24,88},{28,92},{32,9... | collective-permute-start | bytes 98312 | tf_op jit(solution)/shard_map/ppermute | solution.py:29
  37.1 1.8 %collective-permute-start.8 = (f32[64,128]{1,0:T(8,128)S(1)}, f32[64,128]{1,0:T(8,128)S(1)}, u32[]{:S(2)}, u32[]{:S(2)}) collective-permute-start(f32[64,128]{1,0:T(8,128)S(1)} %add.31), channel_id=1, source_target_pairs={{0,192},{4,196},{8,200},{12,204},{16,208},{20,212},{24,216},{28,22... | collective-permute-start | bytes 98312 | tf_op jit(solution)/shard_map/ppermute | solution.py:29
  38.9 0.6 %collective-permute-start.9 = (f32[64,128]{1,0:T(8,128)S(1)}, f32[64,128]{1,0:T(8,128)S(1)}, u32[]{:S(2)}, u32[]{:S(2)}) collective-permute-start(f32[64,128]{1,0:T(8,128)S(1)} %add.31), channel_id=1, source_target_pairs={{0,128},{4,132},{8,136},{12,140},{16,144},{20,148},{24,152},{28,15... | collective-permute-start | bytes 98312 | tf_op jit(solution)/shard_map/ppermute | solution.py:29
  39.6 0.4 fusion.24
  40.0 0.4 fusion.partial_ref
  40.4 1.8 %near_edges.1 = (f32[128,1024]{1,0:T(8,128)S(1)}, f32[128,1024]{1,0:T(8,128)S(1)}) custom-call(s32[6,32]{1,0:T(8,128)S(1)} %bitcast.65, bf16[128,4096]{1,0:T(8,128)(2,1)S(1)} %copy-done.1, bf16[128,512]{1,0:T(8,128)(2,1)S(1)} %collective-permute-done.2.inner_ref, bf16[128,512]{1,0:T(8,128)(2,1)S(1)} %collective-permute-done.10.outer_ref, ...), custom_call_target="tpu_custom_call" | custom-call | flops 402653184 | bytes 4718592 | tf_op jit(solution)/shard_map/near_edges/pallas_call | solution.py:188
  42.2 1.0 %collective-permute-done.9.refs_2_ = f32[64,128]{1,0:T(8,128)S(1)} collective-permute-done((f32[64,128]{1,0:T(8,128)S(1)}, f32[64,128]{1,0:T(8,128)S(1)}, u32[]{:S(2)}, u32[]{:S(2)}) %collective-permute-start.9) | collective-permute-done | bytes 32800 | tf_op jit(solution)/shard_map/ppermute | solution.py:29
  43.2 2.1 %add_far.1 = f32[128,4096]{1,0:T(8,128)} custom-call(f32[64,128]{1,0:T(8,128)S(1)} %fusion.partial_ref, f32[64,128]{1,0:T(8,128)S(1)} %collective-permute-done.7.refs_0_, f32[64,128]{1,0:T(8,128)S(1)} %collective-permute-done.8.refs_1_, f32[64,128]{1,0:T(8,128)S(1)} %collective-permute-done.9.refs_2_, f32[64,64]{1,0:T(8,128)S(1)} %fusion.37.refs_3_, ...), custom_call_target="tpu_custom_call" | custom-call | flops 67108864 | bytes 4718592 | tf_op jit(solution)/shard_map/add_far/pallas_call | solution.py:231
  (31 shorter events, 0.1 us)
Async XLA Ops:
  0.0 5.2 %copy-start = (bf16[126,64,64]{0,2,1:T(8,128)(2,1)S(1)}, bf16[126,64,64]{0,2,1:T(8,128)(2,1)}, u32[]{:S(2)}) copy-start(bf16[126,64,64]{0,2,1:T(8,128)(2,1)} %param.15) | copy-start | bytes 3096580
  0.0 6.1 %copy-start.5 = (s32[6]{0:T(128)S(1)}, s32[6]{0:T(128)}, u32[]{:S(2)}) copy-start(s32[6]{0:T(128)} %constant.19.clone) | copy-start | bytes 76
  0.0 9.4 %copy-start.4 = (bf16[126,64,64]{0,2,1:T(8,128)(2,1)S(1)}, bf16[126,64,64]{0,2,1:T(8,128)(2,1)}, u32[]{:S(2)}) copy-start(bf16[126,64,64]{0,2,1:T(8,128)(2,1)} %param.16) | copy-start | bytes 3096580
  2.2 4.0 %collective-permute-start = (f32[64,128]{1,0:T(8,128)S(1)}, f32[64,128]{1,0:T(8,128)S(1)}, u32[]{:S(2)}, u32[]{:S(2)}) collective-permute-start(f32[64,128]{1,0:T(8,128)S(1)} %get-tuple-element.54), channel_id=1, source_target_pairs={{0,1},{1,0},{2,3},{3,2},{4,5},{5,4},{6,7},{7,6},{8,9},{9,8},{10,11... | collective-permute-start | bytes 98312 | tf_op jit(solution)/shard_map/ppermute | solution.py:29
  4.4 6.9 %collective-permute-start.2 = (bf16[128,512]{1,0:T(8,128)(2,1)S(1)}, bf16[128,512]{1,0:T(8,128)(2,1)S(1)}, u32[]{:S(2)}, u32[]{:S(2)}) collective-permute-start(bf16[128,512]{1,0:T(8,128)(2,1)S(1)} %get-tuple-element.58), channel_id=1, source_target_pairs={{0,1},{1,0},{2,3},{3,2},{4,5},{5,4},{6,7},{7,6},{8,9},{9,8},{10,11... | collective-permute-start | bytes 393224 | tf_op jit(solution)/shard_map/ppermute | solution.py:34
  6.2 5.1 %collective-permute-start.1 = (f32[64,128]{1,0:T(8,128)S(1)}, f32[64,128]{1,0:T(8,128)S(1)}, u32[]{:S(2)}, u32[]{:S(2)}) collective-permute-start(f32[64,128]{1,0:T(8,128)S(1)} %add.25), channel_id=1, source_target_pairs={{0,3},{1,2},{2,1},{3,0},{4,7},{5,6},{6,5},{7,4},{8,11},{9,10},{10,... | collective-permute-start | bytes 98312 | tf_op jit(solution)/shard_map/ppermute | solution.py:29
  9.4 30.2 %slice-start = ((s8[6291456]{0:T(1024)(128)(4,1)}), s8[4194304]{0:T(1024)(128)(4,1)S(1)}, s32[]{:S(2)}) async-start(s8[6291456]{0:T(1024)(128)(4,1)} %bitcast.66), calls=%async_computation | async-start | bytes 8388608
  11.6 4.2 %collective-permute-start.3 = (f32[64,128]{1,0:T(8,128)S(1)}, f32[64,128]{1,0:T(8,128)S(1)}, u32[]{:S(2)}, u32[]{:S(2)}) collective-permute-start(f32[64,128]{1,0:T(8,128)S(1)} %add.27), channel_id=1, source_target_pairs={{0,4},{4,0},{8,12},{12,8},{16,20},{20,16},{24,28},{28,24},{32,36},... | collective-permute-start | bytes 98312 | tf_op jit(solution)/shard_map/ppermute | solution.py:29
  16.0 3.1 %collective-permute-start.4 = (f32[64,128]{1,0:T(8,128)S(1)}, f32[64,128]{1,0:T(8,128)S(1)}, u32[]{:S(2)}, u32[]{:S(2)}) collective-permute-start(f32[64,128]{1,0:T(8,128)S(1)} %add.28), channel_id=1, source_target_pairs={{0,8},{4,12},{8,0},{12,4},{16,24},{20,28},{24,16},{28,20},{32,40},... | collective-permute-start | bytes 98312 | tf_op jit(solution)/shard_map/ppermute | solution.py:29
  16.7 5.8 %copy-start.1 = (bf16[128,4096]{1,0:T(8,128)(2,1)S(1)}, bf16[128,4096]{1,0:T(8,128)(2,1)}, u32[]{:S(2)}) copy-start(bf16[128,4096]{1,0:T(8,128)(2,1)} %sources_ref.1) | copy-start | bytes 3145732
  16.7 5.8 %copy-start.3 = (s32[32,6]{0,1:T(8,128)S(1)}, s32[32,6]{0,1:T(8,128)}, u32[]{:S(2)}) copy-start(s32[32,6]{0,1:T(8,128)} %param.13) | copy-start | bytes 2308
  16.7 22.8 %slice-start.1 = ((s8[6291456]{0:T(1024)(128)(4,1)}), s8[2097152]{0:T(1024)(128)(4,1)S(1)}, s32[]{:S(2)}) async-start(s8[6291456]{0:T(1024)(128)(4,1)} %bitcast.66), calls=%async_computation.1 | async-start | bytes 4194304
  19.4 6.0 %collective-permute-start.5 = (f32[64,128]{1,0:T(8,128)S(1)}, f32[64,128]{1,0:T(8,128)S(1)}, u32[]{:S(2)}, u32[]{:S(2)}) collective-permute-start(f32[64,128]{1,0:T(8,128)S(1)} %add.29), channel_id=1, source_target_pairs={{0,16},{4,20},{8,24},{12,28},{16,0},{20,4},{24,8},{28,12},{32,48},... | collective-permute-start | bytes 98312 | tf_op jit(solution)/shard_map/ppermute | solution.py:29
  25.7 9.9 %collective-permute-start.6 = (f32[64,128]{1,0:T(8,128)S(1)}, f32[64,128]{1,0:T(8,128)S(1)}, u32[]{:S(2)}, u32[]{:S(2)}) collective-permute-start(f32[64,128]{1,0:T(8,128)S(1)} %add.30), channel_id=1, source_target_pairs={{0,48},{4,52},{8,56},{12,60},{16,32},{20,36},{24,40},{28,44},{32,1... | collective-permute-start | bytes 98312 | tf_op jit(solution)/shard_map/ppermute | solution.py:29
  29.3 11.1 %collective-permute-start.10 = (bf16[128,512]{1,0:T(8,128)(2,1)S(1)}, bf16[128,512]{1,0:T(8,128)(2,1)S(1)}, u32[]{:S(2)}, u32[]{:S(2)}) collective-permute-start(bf16[128,512]{1,0:T(8,128)(2,1)S(1)} %get-tuple-element.88), channel_id=1, source_target_pairs={{1,2},{3,4},{5,6},{7,8},{9,10},{11,12},{13,14},{15,16},{17,18},{19... | collective-permute-start | bytes 393224 | tf_op jit(solution)/shard_map/ppermute | solution.py:40
  35.8 6.4 %collective-permute-start.7 = (f32[64,128]{1,0:T(8,128)S(1)}, f32[64,128]{1,0:T(8,128)S(1)}, u32[]{:S(2)}, u32[]{:S(2)}) collective-permute-start(f32[64,128]{1,0:T(8,128)S(1)} %add.31), channel_id=1, source_target_pairs={{0,64},{4,68},{8,72},{12,76},{16,80},{20,84},{24,88},{28,92},{32,9... | collective-permute-start | bytes 98312 | tf_op jit(solution)/shard_map/ppermute | solution.py:29
  37.1 5.1 %collective-permute-start.8 = (f32[64,128]{1,0:T(8,128)S(1)}, f32[64,128]{1,0:T(8,128)S(1)}, u32[]{:S(2)}, u32[]{:S(2)}) collective-permute-start(f32[64,128]{1,0:T(8,128)S(1)} %add.31), channel_id=1, source_target_pairs={{0,192},{4,196},{8,200},{12,204},{16,208},{20,212},{24,216},{28,22... | collective-permute-start | bytes 98312 | tf_op jit(solution)/shard_map/ppermute | solution.py:29
  38.9 4.3 %collective-permute-start.9 = (f32[64,128]{1,0:T(8,128)S(1)}, f32[64,128]{1,0:T(8,128)S(1)}, u32[]{:S(2)}, u32[]{:S(2)}) collective-permute-start(f32[64,128]{1,0:T(8,128)S(1)} %add.31), channel_id=1, source_target_pairs={{0,128},{4,132},{8,136},{12,140},{16,144},{20,148},{24,152},{28,15... | collective-permute-start | bytes 98312 | tf_op jit(solution)/shard_map/ppermute | solution.py:29
  40.4 2.8 %copy-start.2 = (bf16[32,64,128]{2,1,0:T(8,128)(2,1)S(1)}, bf16[32,64,128]{2,1,0:T(8,128)(2,1)}, u32[]{:S(2)}) copy-start(bf16[32,64,128]{2,1,0:T(8,128)(2,1)} %refs_9_.1) | copy-start | bytes 1572868

commit v5 on v4

--- a/solution.py
+++ b/solution.py
@@ -78,7 +78,7 @@
         outer_ref[...] = sources[chunks - 1, :, panels - width :]
 
 
-def moments(sources, basis, width, chunks=4):
+def moments(sources, basis, width, chunks=2):
     rhs, panels = sources.shape
     clusters, rank, panel = basis.shape
     vmem = pl.BlockSpec(memory_space=pltpu.VMEM)
@@ -203,11 +203,11 @@
 
 def far_kernel(count, partial_ref, *refs):
     *near_refs, basis_ref, out_hbm, total, sems = refs[2 * count :]
-    descended = partial_ref[...]
-    for value_ref, matrix_ref in zip(refs[:count], refs[count : 2 * count]):
-        descended += lax.dot_general(
-            matrix_ref[...], value_ref[...], TN, precision=highest, preferred_element_type=jnp.float32
-        )
+    values = jnp.concatenate([ref[...] for ref in refs[:count]], axis=0)
+    matrices = jnp.concatenate([ref[...] for ref in refs[count : 2 * count]], axis=0)
+    descended = partial_ref[...] + lax.dot_general(
+        matrices, values, TN, precision=highest, preferred_element_type=jnp.float32
+    )
     leaf_local = descended.T.astype(basis_ref.dtype)
     panel = basis_ref.shape[2]
     copies = []

time: 45.4 us -> 45 us (level)
  transfers between devices with their start and end apart: 11 -> 11, of which waited for: 2 -> 2; matrix products, arithmetic and copies ran while one was open for 20% -> 21% of each run, Pallas kernels for 8% -> 8%
where the time goes in v5:
time: 45 us; the launch traced here: 44.9 us
  starting transfers between devices  25.4 us (56%)
  Pallas kernels  7.38 us (16%)
  matrix products  6.2 us (14%)
  local copies, waits for them, and re-layouts  3.3 us (7%)
  waiting for transfers between devices  1.4 us (3%)
  other arithmetic  0.74 us (2%)
    ppermute x9, starting transfers between devices, xor_permute(): return lax.ppermute(value, axis, pairs)  19.1 us
    ppermute x1, starting transfers between devices, outer_exchange(): return lax.ppermute(value, AXES, pairs + [(b, a) for a, b in pairs])  6.24 us
    pallas_call x2, Pallas kernels, near_pieces(): pl.pallas_call(kernel, in_specs=[smem] + [vmem] * (1 + len(beside) + len(...  3.51 us
    dot_general x13, matrix products, matmul_tn(): lax.dot_general(left, right, TN, precision=highest, preferred_element_typ...  3.22 us
    slice x2, local copies, waits for them, and re-layouts, take(): return blocks[first:first + count]  2.83 us
    pallas_call x1, Pallas kernels, moments(): pl.pallas_call(moment_kernel, in_specs=[hbm, hbm], out_specs=[vmem] * 3,...  2.01 us
    pallas_call x1, Pallas kernels, add_far(): pl.pallas_call(functools.partial(far_kernel, len(last)), in_specs=[vmem]...  1.87 us
    dot_general x2, matrix products, pick_rows(): jnp.einsum('nkj,sn->skj', table, one_hot, preferred_element_type=jnp.floa...  1.83 us
  transfers between devices with their start and end apart: 11, of which 2 were waited for; matrix products, arithmetic and copies ran while one was open for 21% of the time, Pallas kernels for 8%

profile of v5, /device:TPU:1, one launch (start us, length us, event | category | flops | bytes accessed | tf_op | source)
XLA Modules:
  0.0 44.9 jit_solution(7291354252790667071)
XLA Ops:
  0.0 2.0 %moments.1 = (f32[64,128]{1,0:T(8,128)S(1)}, bf16[128,512]{1,0:T(8,128)(2,1)S(1)}, bf16[128,512]{1,0:T(8,128)(2,1)S(1)}) custom-call(bf16[128,4096]{1,0:T(8,128)(2,1)} %sources_ref.1, bf16[32,64,128]{2,1,0:T(8,128)(2,1)} %refs_9_.1), custom_call_target="tpu_custom_call" | custom-call | flops 67108864 | bytes 1572864 | tf_op jit(solution)/shard_map/moments/pallas_call | solution.py:86
  2.0 2.2 %collective-permute-start = (f32[64,128]{1,0:T(8,128)S(1)}, f32[64,128]{1,0:T(8,128)S(1)}, u32[]{:S(2)}, u32[]{:S(2)}) collective-permute-start(f32[64,128]{1,0:T(8,128)S(1)} %get-tuple-element.54), channel_id=1, source_target_pairs={{0,1},{1,0},{2,3},{3,2},{4,5},{5,4},{6,7},{7,6},{8,9},{9,8},{10,11... | collective-permute-start | bytes 98312 | tf_op jit(solution)/shard_map/ppermute | solution.py:29
  4.3 0.1 collective-permute-start.2
  4.4 0.7 %xor_add_fusion = s32[11]{0:T(128)S(1)} fusion(s32[11]{0:T(128)} %constant.18.clone, s32[11]{0:T(128)} %constant.17.clone, s32[11]{0:T(128)} %constant.16.clone, s32[]{:T(128)S(6)} %axis_index.15), kind=kLoop, calls=%fused_computation.24 | loop fusion | flops 33 | bytes 180 | tf_op jit(solution)/shard_map/add | solution.py:277
  5.0 0.9 %fusion.16 = f32[11,64,64]{2,0,1:T(8,128)S(1)} fusion(bf16[126,64,64]{0,2,1:T(8,128)(2,1)S(1)} %copy-done, s32[11]{0:T(128)S(1)} %xor_add_fusion), kind=kOutput, calls=%fused_computation.17 | convolution fusion | flops 11355498 | bytes 1212460 | tf_op jit(solution)/shard_map/nkj,sn->skj/dot_general | solution.py:260
  6.0 2.9 %collective-permute-start.1 = (f32[64,128]{1,0:T(8,128)S(1)}, f32[64,128]{1,0:T(8,128)S(1)}, u32[]{:S(2)}, u32[]{:S(2)}) collective-permute-start(f32[64,128]{1,0:T(8,128)S(1)} %add.25), channel_id=1, source_target_pairs={{0,3},{1,2},{2,1},{3,0},{4,7},{5,6},{6,5},{7,4},{8,11},{9,10},{10,... | collective-permute-start | bytes 98312 | tf_op jit(solution)/shard_map/ppermute | solution.py:29
  8.9 0.3 fusion.25
  9.2 0.0 slice-start
  9.2 0.9 %fusion.20 = f32[6,64,64]{2,0,1:T(8,128)S(1)} fusion(bf16[126,64,64]{0,2,1:T(8,128)(2,1)S(1)} %copy-done.4, s32[6]{0:T(128)S(1)} %shift-right-arithmetic_add_fusion), kind=kOutput, calls=%fused_computation.21 | convolution fusion | flops 6193908 | bytes 1130520 | tf_op jit(solution)/shard_map/nkj,sn->skj/dot_general | solution.py:260
  10.1 0.3 fusion.32
  10.4 0.2 fusion.33
  10.6 0.2 fusion.34
  10.9 0.2 fusion.35
  11.2 0.2 fusion.28
  11.4 3.3 %collective-permute-start.3 = (f32[64,128]{1,0:T(8,128)S(1)}, f32[64,128]{1,0:T(8,128)S(1)}, u32[]{:S(2)}, u32[]{:S(2)}) collective-permute-start(f32[64,128]{1,0:T(8,128)S(1)} %add.27), channel_id=1, source_target_pairs={{0,4},{4,0},{8,12},{12,8},{16,20},{20,16},{24,28},{28,24},{32,36},... | collective-permute-start | bytes 98312 | tf_op jit(solution)/shard_map/ppermute | solution.py:29
  14.7 0.1 fusion.26
  14.8 0.2 fusion.46
  15.0 0.2 fusion.45
  15.2 0.4 collective-permute-done.3
  15.6 0.2 fusion.29
  15.9 0.4 collective-permute-start.4
  16.3 0.2 fusion.30
  16.5 0.0 copy-start.1
  16.5 0.0 slice-start.1
  16.6 2.4 %slice.61.blocks_ref = bf16[16,6,128,128]{3,2,1,0:T(8,128)(2,1)S(1)} slice(bf16[32,6,128,128]{3,2,1,0:T(8,128)(2,1)} %param.12), slice={[8:24], [0:6], [0:128], [0:128]} | slice | bytes 6291456 | tf_op jit(solution)/shard_map/slice | solution.py:172
  19.0 0.2 fusion.31
  19.3 3.1 %collective-permute-start.5 = (f32[64,128]{1,0:T(8,128)S(1)}, f32[64,128]{1,0:T(8,128)S(1)}, u32[]{:S(2)}, u32[]{:S(2)}) collective-permute-start(f32[64,128]{1,0:T(8,128)S(1)} %add.29), channel_id=1, source_target_pairs={{0,16},{4,20},{8,24},{12,28},{16,0},{20,4},{24,8},{28,12},{32,48},... | collective-permute-start | bytes 98312 | tf_op jit(solution)/shard_map/ppermute | solution.py:29
  22.3 1.7 %near_middle.1.refs_7_ = f32[128,2048]{1,0:T(8,128)S(1)} custom-call(s32[6,32]{1,0:T(8,128)S(1)} %bitcast.64, bf16[128,4096]{1,0:T(8,128)(2,1)S(1)} %copy-done.1, bf16[16,6,128,128]{3,2,1,0:T(8,128)(2,1)S(1)} %slice.61.blocks_ref), custom_call_target="tpu_custom_call" | custom-call | flops 402653184 | bytes 4718592 | tf_op jit(solution)/shard_map/near_middle/pallas_call | solution.py:188
  24.1 0.2 fusion.41
  24.3 0.1 fusion.27
  24.4 0.2 fusion.38
  24.6 0.2 fusion.40.refs_5_
  24.7 0.2 fusion.39.refs_4_
  24.9 0.2 fusion.37.refs_3_
  25.1 0.2 fusion.36
  25.2 0.2 fusion.42
  25.5 3.4 %collective-permute-start.6 = (f32[64,128]{1,0:T(8,128)S(1)}, f32[64,128]{1,0:T(8,128)S(1)}, u32[]{:S(2)}, u32[]{:S(2)}) collective-permute-start(f32[64,128]{1,0:T(8,128)S(1)} %add.30), channel_id=1, source_target_pairs={{0,48},{4,52},{8,56},{12,60},{16,32},{20,36},{24,40},{28,44},{32,1... | collective-permute-start | bytes 98312 | tf_op jit(solution)/shard_map/ppermute | solution.py:29
  28.9 0.2 fusion.43
  29.1 6.2 %collective-permute-start.10 = (bf16[128,512]{1,0:T(8,128)(2,1)S(1)}, bf16[128,512]{1,0:T(8,128)(2,1)S(1)}, u32[]{:S(2)}, u32[]{:S(2)}) collective-permute-start(bf16[128,512]{1,0:T(8,128)(2,1)S(1)} %get-tuple-element.88), channel_id=1, source_target_pairs={{1,2},{3,4},{5,6},{7,8},{9,10},{11,12},{13,14},{15,16},{17,18},{19... | collective-permute-start | bytes 393224 | tf_op jit(solution)/shard_map/ppermute | solution.py:40
  35.4 0.2 fusion.44
  35.6 1.3 %collective-permute-start.7 = (f32[64,128]{1,0:T(8,128)S(1)}, f32[64,128]{1,0:T(8,128)S(1)}, u32[]{:S(2)}, u32[]{:S(2)}) collective-permute-start(f32[64,128]{1,0:T(8,128)S(1)} %add.31), channel_id=1, source_target_pairs={{0,64},{4,68},{8,72},{12,76},{16,80},{20,84},{24,88},{28,92},{32,9... | collective-permute-start | bytes 98312 | tf_op jit(solution)/shard_map/ppermute | solution.py:29
  36.9 1.8 %collective-permute-start.8 = (f32[64,128]{1,0:T(8,128)S(1)}, f32[64,128]{1,0:T(8,128)S(1)}, u32[]{:S(2)}, u32[]{:S(2)}) collective-permute-start(f32[64,128]{1,0:T(8,128)S(1)} %add.31), channel_id=1, source_target_pairs={{0,192},{4,196},{8,200},{12,204},{16,208},{20,212},{24,216},{28,22... | collective-permute-start | bytes 98312 | tf_op jit(solution)/shard_map/ppermute | solution.py:29
  38.8 0.6 %collective-permute-start.9 = (f32[64,128]{1,0:T(8,128)S(1)}, f32[64,128]{1,0:T(8,128)S(1)}, u32[]{:S(2)}, u32[]{:S(2)}) collective-permute-start(f32[64,128]{1,0:T(8,128)S(1)} %add.31), channel_id=1, source_target_pairs={{0,128},{4,132},{8,136},{12,140},{16,144},{20,148},{24,152},{28,15... | collective-permute-start | bytes 98312 | tf_op jit(solution)/shard_map/ppermute | solution.py:29
  39.4 0.4 fusion.24
  39.8 0.4 fusion.partial_ref
  40.2 1.8 %near_edges.1 = (f32[128,1024]{1,0:T(8,128)S(1)}, f32[128,1024]{1,0:T(8,128)S(1)}) custom-call(s32[6,32]{1,0:T(8,128)S(1)} %bitcast.65, bf16[128,4096]{1,0:T(8,128)(2,1)S(1)} %copy-done.1, bf16[128,512]{1,0:T(8,128)(2,1)S(1)} %collective-permute-done.2.inner_ref, bf16[128,512]{1,0:T(8,128)(2,1)S(1)} %collective-permute-done.10.outer_ref, ...), custom_call_target="tpu_custom_call" | custom-call | flops 402653184 | bytes 4718592 | tf_op jit(solution)/shard_map/near_edges/pallas_call | solution.py:188
  42.0 1.0 %collective-permute-done.9.refs_2_ = f32[64,128]{1,0:T(8,128)S(1)} collective-permute-done((f32[64,128]{1,0:T(8,128)S(1)}, f32[64,128]{1,0:T(8,128)S(1)}, u32[]{:S(2)}, u32[]{:S(2)}) %collective-permute-start.9) | collective-permute-done | bytes 32800 | tf_op jit(solution)/shard_map/ppermute | solution.py:29
  43.0 1.9 %add_far.1 = f32[128,4096]{1,0:T(8,128)} custom-call(f32[64,128]{1,0:T(8,128)S(1)} %fusion.partial_ref, f32[64,128]{1,0:T(8,128)S(1)} %collective-permute-done.7.refs_0_, f32[64,128]{1,0:T(8,128)S(1)} %collective-permute-done.8.refs_1_, f32[64,128]{1,0:T(8,128)S(1)} %collective-permute-done.9.refs_2_, f32[64,64]{1,0:T(8,128)S(1)} %fusion.37.refs_3_, ...), custom_call_target="tpu_custom_call" | custom-call | flops 67108864 | bytes 4718592 | tf_op jit(solution)/shard_map/add_far/pallas_call | solution.py:231
  (31 shorter events, 0.1 us)
Async XLA Ops:
  0.0 5.0 %copy-start = (bf16[126,64,64]{0,2,1:T(8,128)(2,1)S(1)}, bf16[126,64,64]{0,2,1:T(8,128)(2,1)}, u32[]{:S(2)}) copy-start(bf16[126,64,64]{0,2,1:T(8,128)(2,1)} %param.15) | copy-start | bytes 3096580
  0.0 6.0 %copy-start.5 = (s32[6]{0:T(128)S(1)}, s32[6]{0:T(128)}, u32[]{:S(2)}) copy-start(s32[6]{0:T(128)} %constant.19.clone) | copy-start | bytes 76
  0.0 9.2 %copy-start.4 = (bf16[126,64,64]{0,2,1:T(8,128)(2,1)S(1)}, bf16[126,64,64]{0,2,1:T(8,128)(2,1)}, u32[]{:S(2)}) copy-start(bf16[126,64,64]{0,2,1:T(8,128)(2,1)} %param.16) | copy-start | bytes 3096580
  2.0 4.0 %collective-permute-start = (f32[64,128]{1,0:T(8,128)S(1)}, f32[64,128]{1,0:T(8,128)S(1)}, u32[]{:S(2)}, u32[]{:S(2)}) collective-permute-start(f32[64,128]{1,0:T(8,128)S(1)} %get-tuple-element.54), channel_id=1, source_target_pairs={{0,1},{1,0},{2,3},{3,2},{4,5},{5,4},{6,7},{7,6},{8,9},{9,8},{10,11... | collective-permute-start | bytes 98312 | tf_op jit(solution)/shard_map/ppermute | solution.py:29
  4.3 6.9 %collective-permute-start.2 = (bf16[128,512]{1,0:T(8,128)(2,1)S(1)}, bf16[128,512]{1,0:T(8,128)(2,1)S(1)}, u32[]{:S(2)}, u32[]{:S(2)}) collective-permute-start(bf16[128,512]{1,0:T(8,128)(2,1)S(1)} %get-tuple-element.58), channel_id=1, source_target_pairs={{0,1},{1,0},{2,3},{3,2},{4,5},{5,4},{6,7},{7,6},{8,9},{9,8},{10,11... | collective-permute-start | bytes 393224 | tf_op jit(solution)/shard_map/ppermute | solution.py:34
  6.0 5.1 %collective-permute-start.1 = (f32[64,128]{1,0:T(8,128)S(1)}, f32[64,128]{1,0:T(8,128)S(1)}, u32[]{:S(2)}, u32[]{:S(2)}) collective-permute-start(f32[64,128]{1,0:T(8,128)S(1)} %add.25), channel_id=1, source_target_pairs={{0,3},{1,2},{2,1},{3,0},{4,7},{5,6},{6,5},{7,4},{8,11},{9,10},{10,... | collective-permute-start | bytes 98312 | tf_op jit(solution)/shard_map/ppermute | solution.py:29
  9.2 30.2 %slice-start = ((s8[6291456]{0:T(1024)(128)(4,1)}), s8[4194304]{0:T(1024)(128)(4,1)S(1)}, s32[]{:S(2)}) async-start(s8[6291456]{0:T(1024)(128)(4,1)} %bitcast.66), calls=%async_computation | async-start | bytes 8388608
  11.4 4.2 %collective-permute-start.3 = (f32[64,128]{1,0:T(8,128)S(1)}, f32[64,128]{1,0:T(8,128)S(1)}, u32[]{:S(2)}, u32[]{:S(2)}) collective-permute-start(f32[64,128]{1,0:T(8,128)S(1)} %add.27), channel_id=1, source_target_pairs={{0,4},{4,0},{8,12},{12,8},{16,20},{20,16},{24,28},{28,24},{32,36},... | collective-permute-start | bytes 98312 | tf_op jit(solution)/shard_map/ppermute | solution.py:29
  15.9 3.1 %collective-permute-start.4 = (f32[64,128]{1,0:T(8,128)S(1)}, f32[64,128]{1,0:T(8,128)S(1)}, u32[]{:S(2)}, u32[]{:S(2)}) collective-permute-start(f32[64,128]{1,0:T(8,128)S(1)} %add.28), channel_id=1, source_target_pairs={{0,8},{4,12},{8,0},{12,4},{16,24},{20,28},{24,16},{28,20},{32,40},... | collective-permute-start | bytes 98312 | tf_op jit(solution)/shard_map/ppermute | solution.py:29
  16.5 5.8 %copy-start.1 = (bf16[128,4096]{1,0:T(8,128)(2,1)S(1)}, bf16[128,4096]{1,0:T(8,128)(2,1)}, u32[]{:S(2)}) copy-start(bf16[128,4096]{1,0:T(8,128)(2,1)} %sources_ref.1) | copy-start | bytes 3145732
  16.5 5.8 %copy-start.3 = (s32[32,6]{0,1:T(8,128)S(1)}, s32[32,6]{0,1:T(8,128)}, u32[]{:S(2)}) copy-start(s32[32,6]{0,1:T(8,128)} %param.13) | copy-start | bytes 2308
  16.5 22.9 %slice-start.1 = ((s8[6291456]{0:T(1024)(128)(4,1)}), s8[2097152]{0:T(1024)(128)(4,1)S(1)}, s32[]{:S(2)}) async-start(s8[6291456]{0:T(1024)(128)(4,1)} %bitcast.66), calls=%async_computation.1 | async-start | bytes 4194304
  19.3 6.0 %collective-permute-start.5 = (f32[64,128]{1,0:T(8,128)S(1)}, f32[64,128]{1,0:T(8,128)S(1)}, u32[]{:S(2)}, u32[]{:S(2)}) collective-permute-start(f32[64,128]{1,0:T(8,128)S(1)} %add.29), channel_id=1, source_target_pairs={{0,16},{4,20},{8,24},{12,28},{16,0},{20,4},{24,8},{28,12},{32,48},... | collective-permute-start | bytes 98312 | tf_op jit(solution)/shard_map/ppermute | solution.py:29
  25.5 9.9 %collective-permute-start.6 = (f32[64,128]{1,0:T(8,128)S(1)}, f32[64,128]{1,0:T(8,128)S(1)}, u32[]{:S(2)}, u32[]{:S(2)}) collective-permute-start(f32[64,128]{1,0:T(8,128)S(1)} %add.30), channel_id=1, source_target_pairs={{0,48},{4,52},{8,56},{12,60},{16,32},{20,36},{24,40},{28,44},{32,1... | collective-permute-start | bytes 98312 | tf_op jit(solution)/shard_map/ppermute | solution.py:29
  29.1 11.1 %collective-permute-start.10 = (bf16[128,512]{1,0:T(8,128)(2,1)S(1)}, bf16[128,512]{1,0:T(8,128)(2,1)S(1)}, u32[]{:S(2)}, u32[]{:S(2)}) collective-permute-start(bf16[128,512]{1,0:T(8,128)(2,1)S(1)} %get-tuple-element.88), channel_id=1, source_target_pairs={{1,2},{3,4},{5,6},{7,8},{9,10},{11,12},{13,14},{15,16},{17,18},{19... | collective-permute-start | bytes 393224 | tf_op jit(solution)/shard_map/ppermute | solution.py:40
  35.6 6.4 %collective-permute-start.7 = (f32[64,128]{1,0:T(8,128)S(1)}, f32[64,128]{1,0:T(8,128)S(1)}, u32[]{:S(2)}, u32[]{:S(2)}) collective-permute-start(f32[64,128]{1,0:T(8,128)S(1)} %add.31), channel_id=1, source_target_pairs={{0,64},{4,68},{8,72},{12,76},{16,80},{20,84},{24,88},{28,92},{32,9... | collective-permute-start | bytes 98312 | tf_op jit(solution)/shard_map/ppermute | solution.py:29
  36.9 5.1 %collective-permute-start.8 = (f32[64,128]{1,0:T(8,128)S(1)}, f32[64,128]{1,0:T(8,128)S(1)}, u32[]{:S(2)}, u32[]{:S(2)}) collective-permute-start(f32[64,128]{1,0:T(8,128)S(1)} %add.31), channel_id=1, source_target_pairs={{0,192},{4,196},{8,200},{12,204},{16,208},{20,212},{24,216},{28,22... | collective-permute-start | bytes 98312 | tf_op jit(solution)/shard_map/ppermute | solution.py:29
  38.8 4.3 %collective-permute-start.9 = (f32[64,128]{1,0:T(8,128)S(1)}, f32[64,128]{1,0:T(8,128)S(1)}, u32[]{:S(2)}, u32[]{:S(2)}) collective-permute-start(f32[64,128]{1,0:T(8,128)S(1)} %add.31), channel_id=1, source_target_pairs={{0,128},{4,132},{8,136},{12,140},{16,144},{20,148},{24,152},{28,15... | collective-permute-start | bytes 98312 | tf_op jit(solution)/shard_map/ppermute | solution.py:29
  40.2 2.8 %copy-start.2 = (bf16[32,64,128]{2,1,0:T(8,128)(2,1)S(1)}, bf16[32,64,128]{2,1,0:T(8,128)(2,1)}, u32[]{:S(2)}) copy-start(bf16[32,64,128]{2,1,0:T(8,128)(2,1)} %refs_9_.1) | copy-start | bytes 1572868

commit v6 on v5

--- a/solution.py
+++ b/solution.py
@@ -302,7 +302,7 @@
         down.append(matmul(couples[step], chains[step - 1]))
 
     siblings = []
-    for level, mask in enumerate([1, 2, 4, 12]):
+    for level, mask in enumerate([1, 2, 4, 14]):
         if level == 1:
             current, middle_blocks = together(current, near_blocks)
         elif level == 2:

time: 45 us -> 44.6 us (level)
  no operation moved by 1% of the time
where the time goes in v6:
time: 44.6 us; the launch traced here: 44.5 us
  starting transfers between devices  25 us (56%)
  Pallas kernels  7.4 us (17%)
  matrix products  6.2 us (14%)
  local copies, waits for them, and re-layouts  3.3 us (7%)
  waiting for transfers between devices  1.39 us (3%)
  other arithmetic  0.74 us (2%)
    ppermute x9, starting transfers between devices, xor_permute(): return lax.ppermute(value, axis, pairs)  18.6 us
    ppermute x1, starting transfers between devices, outer_exchange(): return lax.ppermute(value, AXES, pairs + [(b, a) for a, b in pairs])  6.23 us
    pallas_call x2, Pallas kernels, near_pieces(): pl.pallas_call(kernel, in_specs=[smem] + [vmem] * (1 + len(beside) + len(...  3.52 us
    dot_general x13, matrix products, matmul_tn(): lax.dot_general(left, right, TN, precision=highest, preferred_element_typ...  3.22 us
    slice x2, local copies, waits for them, and re-layouts, take(): return blocks[first:first + count]  2.83 us
    pallas_call x1, Pallas kernels, moments(): pl.pallas_call(moment_kernel, in_specs=[hbm, hbm], out_specs=[vmem] * 3,...  2.01 us
    pallas_call x1, Pallas kernels, add_far(): pl.pallas_call(functools.partial(far_kernel, len(last)), in_specs=[vmem]...  1.87 us
    dot_general x2, matrix products, pick_rows(): jnp.einsum('nkj,sn->skj', table, one_hot, preferred_element_type=jnp.floa...  1.83 us
  transfers between devices with their start and end apart: 11, of which 2 were waited for; matrix products, arithmetic and copies ran while one was open for 21% of the time, Pallas kernels for 8%

profile of v6, /device:TPU:1, one launch (start us, length us, event | category | flops | bytes accessed | tf_op | source)
XLA Modules:
  0.0 44.5 jit_solution(872783751333223795)
XLA Ops:
  0.0 2.0 %moments.1 = (f32[64,128]{1,0:T(8,128)S(1)}, bf16[128,512]{1,0:T(8,128)(2,1)S(1)}, bf16[128,512]{1,0:T(8,128)(2,1)S(1)}) custom-call(bf16[128,4096]{1,0:T(8,128)(2,1)} %sources_ref.1, bf16[32,64,128]{2,1,0:T(8,128)(2,1)} %refs_9_.1), custom_call_target="tpu_custom_call" | custom-call | flops 67108864 | bytes 1572864 | tf_op jit(solution)/shard_map/moments/pallas_call | solution.py:86
  2.0 2.2 %collective-permute-start = (f32[64,128]{1,0:T(8,128)S(1)}, f32[64,128]{1,0:T(8,128)S(1)}, u32[]{:S(2)}, u32[]{:S(2)}) collective-permute-start(f32[64,128]{1,0:T(8,128)S(1)} %get-tuple-element.54), channel_id=1, source_target_pairs={{0,1},{1,0},{2,3},{3,2},{4,5},{5,4},{6,7},{7,6},{8,9},{9,8},{10,11... | collective-permute-start | bytes 98312 | tf_op jit(solution)/shard_map/ppermute | solution.py:29
  4.3 0.1 collective-permute-start.2
  4.4 0.7 %xor_add_fusion = s32[11]{0:T(128)S(1)} fusion(s32[11]{0:T(128)} %constant.18.clone, s32[11]{0:T(128)} %constant.17.clone, s32[11]{0:T(128)} %constant.16.clone, s32[]{:T(128)S(6)} %axis_index.15), kind=kLoop, calls=%fused_computation.24 | loop fusion | flops 33 | bytes 180 | tf_op jit(solution)/shard_map/add | solution.py:277
  5.0 0.9 %fusion.16 = f32[11,64,64]{2,0,1:T(8,128)S(1)} fusion(bf16[126,64,64]{0,2,1:T(8,128)(2,1)S(1)} %copy-done, s32[11]{0:T(128)S(1)} %xor_add_fusion), kind=kOutput, calls=%fused_computation.17 | convolution fusion | flops 11355498 | bytes 1212460 | tf_op jit(solution)/shard_map/nkj,sn->skj/dot_general | solution.py:260
  6.0 2.9 %collective-permute-start.1 = (f32[64,128]{1,0:T(8,128)S(1)}, f32[64,128]{1,0:T(8,128)S(1)}, u32[]{:S(2)}, u32[]{:S(2)}) collective-permute-start(f32[64,128]{1,0:T(8,128)S(1)} %add.25), channel_id=1, source_target_pairs={{0,3},{1,2},{2,1},{3,0},{4,7},{5,6},{6,5},{7,4},{8,11},{9,10},{10,... | collective-permute-start | bytes 98312 | tf_op jit(solution)/shard_map/ppermute | solution.py:29
  8.9 0.3 fusion.25
  9.2 0.0 slice-start
  9.2 0.9 %fusion.20 = f32[6,64,64]{2,0,1:T(8,128)S(1)} fusion(bf16[126,64,64]{0,2,1:T(8,128)(2,1)S(1)} %copy-done.4, s32[6]{0:T(128)S(1)} %shift-right-arithmetic_add_fusion), kind=kOutput, calls=%fused_computation.21 | convolution fusion | flops 6193908 | bytes 1130520 | tf_op jit(solution)/shard_map/nkj,sn->skj/dot_general | solution.py:260
  10.1 0.3 fusion.32
  10.4 0.2 fusion.33
  10.6 0.2 fusion.34
  10.9 0.2 fusion.35
  11.2 0.2 fusion.28
  11.4 3.3 %collective-permute-start.3 = (f32[64,128]{1,0:T(8,128)S(1)}, f32[64,128]{1,0:T(8,128)S(1)}, u32[]{:S(2)}, u32[]{:S(2)}) collective-permute-start(f32[64,128]{1,0:T(8,128)S(1)} %add.27), channel_id=1, source_target_pairs={{0,4},{4,0},{8,12},{12,8},{16,20},{20,16},{24,28},{28,24},{32,36},... | collective-permute-start | bytes 98312 | tf_op jit(solution)/shard_map/ppermute | solution.py:29
  14.7 0.1 fusion.26
  14.8 0.2 fusion.46
  15.0 0.2 fusion.45
  15.2 0.4 collective-permute-done.3
  15.6 0.2 fusion.29
  15.9 0.4 collective-permute-start.4
  16.3 0.2 fusion.30
  16.5 0.0 copy-start.1
  16.5 0.0 slice-start.1
  16.6 2.4 %slice.61.blocks_ref = bf16[16,6,128,128]{3,2,1,0:T(8,128)(2,1)S(1)} slice(bf16[32,6,128,128]{3,2,1,0:T(8,128)(2,1)} %param.12), slice={[8:24], [0:6], [0:128], [0:128]} | slice | bytes 6291456 | tf_op jit(solution)/shard_map/slice | solution.py:172
  19.0 0.2 fusion.31
  19.3 3.1 %collective-permute-start.5 = (f32[64,128]{1,0:T(8,128)S(1)}, f32[64,128]{1,0:T(8,128)S(1)}, u32[]{:S(2)}, u32[]{:S(2)}) collective-permute-start(f32[64,128]{1,0:T(8,128)S(1)} %add.29), channel_id=1, source_target_pairs={{0,16},{4,20},{8,24},{12,28},{16,0},{20,4},{24,8},{28,12},{32,48},... | collective-permute-start | bytes 98312 | tf_op jit(solution)/shard_map/ppermute | solution.py:29
  22.3 1.7 %near_middle.1.refs_7_ = f32[128,2048]{1,0:T(8,128)S(1)} custom-call(s32[6,32]{1,0:T(8,128)S(1)} %bitcast.64, bf16[128,4096]{1,0:T(8,128)(2,1)S(1)} %copy-done.1, bf16[16,6,128,128]{3,2,1,0:T(8,128)(2,1)S(1)} %slice.61.blocks_ref), custom_call_target="tpu_custom_call" | custom-call | flops 402653184 | bytes 4718592 | tf_op jit(solution)/shard_map/near_middle/pallas_call | solution.py:188
  24.1 0.2 fusion.41
  24.3 0.1 fusion.27
  24.4 0.2 fusion.38
  24.6 0.2 fusion.40.refs_5_
  24.7 0.2 fusion.39.refs_4_
  24.9 0.2 fusion.37.refs_3_
  25.1 0.2 fusion.36
  25.2 0.2 fusion.42
  25.5 2.9 %collective-permute-start.6 = (f32[64,128]{1,0:T(8,128)S(1)}, f32[64,128]{1,0:T(8,128)S(1)}, u32[]{:S(2)}, u32[]{:S(2)}) collective-permute-start(f32[64,128]{1,0:T(8,128)S(1)} %add.30), channel_id=1, source_target_pairs={{0,56},{4,60},{8,48},{12,52},{16,40},{20,44},{24,32},{28,36},{32,2... | collective-permute-start | bytes 98312 | tf_op jit(solution)/shard_map/ppermute | solution.py:29
  28.4 0.2 fusion.43
  28.7 6.2 %collective-permute-start.10 = (bf16[128,512]{1,0:T(8,128)(2,1)S(1)}, bf16[128,512]{1,0:T(8,128)(2,1)S(1)}, u32[]{:S(2)}, u32[]{:S(2)}) collective-permute-start(bf16[128,512]{1,0:T(8,128)(2,1)S(1)} %get-tuple-element.88), channel_id=1, source_target_pairs={{1,2},{3,4},{5,6},{7,8},{9,10},{11,12},{13,14},{15,16},{17,18},{19... | collective-permute-start | bytes 393224 | tf_op jit(solution)/shard_map/ppermute | solution.py:40
  34.9 0.2 fusion.44
  35.2 1.3 %collective-permute-start.7 = (f32[64,128]{1,0:T(8,128)S(1)}, f32[64,128]{1,0:T(8,128)S(1)}, u32[]{:S(2)}, u32[]{:S(2)}) collective-permute-start(f32[64,128]{1,0:T(8,128)S(1)} %add.31), channel_id=1, source_target_pairs={{0,64},{4,68},{8,72},{12,76},{16,80},{20,84},{24,88},{28,92},{32,9... | collective-permute-start | bytes 98312 | tf_op jit(solution)/shard_map/ppermute | solution.py:29
  36.5 1.8 %collective-permute-start.8 = (f32[64,128]{1,0:T(8,128)S(1)}, f32[64,128]{1,0:T(8,128)S(1)}, u32[]{:S(2)}, u32[]{:S(2)}) collective-permute-start(f32[64,128]{1,0:T(8,128)S(1)} %add.31), channel_id=1, source_target_pairs={{0,192},{4,196},{8,200},{12,204},{16,208},{20,212},{24,216},{28,22... | collective-permute-start | bytes 98312 | tf_op jit(solution)/shard_map/ppermute | solution.py:29
  38.3 0.6 %collective-permute-start.9 = (f32[64,128]{1,0:T(8,128)S(1)}, f32[64,128]{1,0:T(8,128)S(1)}, u32[]{:S(2)}, u32[]{:S(2)}) collective-permute-start(f32[64,128]{1,0:T(8,128)S(1)} %add.31), channel_id=1, source_target_pairs={{0,128},{4,132},{8,136},{12,140},{16,144},{20,148},{24,152},{28,15... | collective-permute-start | bytes 98312 | tf_op jit(solution)/shard_map/ppermute | solution.py:29
  38.9 0.4 fusion.24
  39.4 0.4 fusion.partial_ref
  39.8 1.8 %near_edges.1 = (f32[128,1024]{1,0:T(8,128)S(1)}, f32[128,1024]{1,0:T(8,128)S(1)}) custom-call(s32[6,32]{1,0:T(8,128)S(1)} %bitcast.65, bf16[128,4096]{1,0:T(8,128)(2,1)S(1)} %copy-done.1, bf16[128,512]{1,0:T(8,128)(2,1)S(1)} %collective-permute-done.2.inner_ref, bf16[128,512]{1,0:T(8,128)(2,1)S(1)} %collective-permute-done.10.outer_ref, ...), custom_call_target="tpu_custom_call" | custom-call | flops 402653184 | bytes 4718592 | tf_op jit(solution)/shard_map/near_edges/pallas_call | solution.py:188
  41.6 1.0 %collective-permute-done.9.refs_2_ = f32[64,128]{1,0:T(8,128)S(1)} collective-permute-done((f32[64,128]{1,0:T(8,128)S(1)}, f32[64,128]{1,0:T(8,128)S(1)}, u32[]{:S(2)}, u32[]{:S(2)}) %collective-permute-start.9) | collective-permute-done | bytes 32800 | tf_op jit(solution)/shard_map/ppermute | solution.py:29
  42.6 1.9 %add_far.1 = f32[128,4096]{1,0:T(8,128)} custom-call(f32[64,128]{1,0:T(8,128)S(1)} %fusion.partial_ref, f32[64,128]{1,0:T(8,128)S(1)} %collective-permute-done.7.refs_0_, f32[64,128]{1,0:T(8,128)S(1)} %collective-permute-done.8.refs_1_, f32[64,128]{1,0:T(8,128)S(1)} %collective-permute-done.9.refs_2_, f32[64,64]{1,0:T(8,128)S(1)} %fusion.37.refs_3_, ...), custom_call_target="tpu_custom_call" | custom-call | flops 67108864 | bytes 4718592 | tf_op jit(solution)/shard_map/add_far/pallas_call | solution.py:231
  (31 shorter events, 0.1 us)
Async XLA Ops:
  0.0 5.0 %copy-start = (bf16[126,64,64]{0,2,1:T(8,128)(2,1)S(1)}, bf16[126,64,64]{0,2,1:T(8,128)(2,1)}, u32[]{:S(2)}) copy-start(bf16[126,64,64]{0,2,1:T(8,128)(2,1)} %param.15) | copy-start | bytes 3096580
  0.0 6.0 %copy-start.5 = (s32[6]{0:T(128)S(1)}, s32[6]{0:T(128)}, u32[]{:S(2)}) copy-start(s32[6]{0:T(128)} %constant.19.clone) | copy-start | bytes 76
  0.0 9.2 %copy-start.4 = (bf16[126,64,64]{0,2,1:T(8,128)(2,1)S(1)}, bf16[126,64,64]{0,2,1:T(8,128)(2,1)}, u32[]{:S(2)}) copy-start(bf16[126,64,64]{0,2,1:T(8,128)(2,1)} %param.16) | copy-start | bytes 3096580
  2.0 4.0 %collective-permute-start = (f32[64,128]{1,0:T(8,128)S(1)}, f32[64,128]{1,0:T(8,128)S(1)}, u32[]{:S(2)}, u32[]{:S(2)}) collective-permute-start(f32[64,128]{1,0:T(8,128)S(1)} %get-tuple-element.54), channel_id=1, source_target_pairs={{0,1},{1,0},{2,3},{3,2},{4,5},{5,4},{6,7},{7,6},{8,9},{9,8},{10,11... | collective-permute-start | bytes 98312 | tf_op jit(solution)/shard_map/ppermute | solution.py:29
  4.3 6.9 %collective-permute-start.2 = (bf16[128,512]{1,0:T(8,128)(2,1)S(1)}, bf16[128,512]{1,0:T(8,128)(2,1)S(1)}, u32[]{:S(2)}, u32[]{:S(2)}) collective-permute-start(bf16[128,512]{1,0:T(8,128)(2,1)S(1)} %get-tuple-element.58), channel_id=1, source_target_pairs={{0,1},{1,0},{2,3},{3,2},{4,5},{5,4},{6,7},{7,6},{8,9},{9,8},{10,11... | collective-permute-start | bytes 393224 | tf_op jit(solution)/shard_map/ppermute | solution.py:34
  6.0 5.1 %collective-permute-start.1 = (f32[64,128]{1,0:T(8,128)S(1)}, f32[64,128]{1,0:T(8,128)S(1)}, u32[]{:S(2)}, u32[]{:S(2)}) collective-permute-start(f32[64,128]{1,0:T(8,128)S(1)} %add.25), channel_id=1, source_target_pairs={{0,3},{1,2},{2,1},{3,0},{4,7},{5,6},{6,5},{7,4},{8,11},{9,10},{10,... | collective-permute-start | bytes 98312 | tf_op jit(solution)/shard_map/ppermute | solution.py:29
  9.2 29.7 %slice-start = ((s8[6291456]{0:T(1024)(128)(4,1)}), s8[4194304]{0:T(1024)(128)(4,1)S(1)}, s32[]{:S(2)}) async-start(s8[6291456]{0:T(1024)(128)(4,1)} %bitcast.66), calls=%async_computation | async-start | bytes 8388608
  11.4 4.2 %collective-permute-start.3 = (f32[64,128]{1,0:T(8,128)S(1)}, f32[64,128]{1,0:T(8,128)S(1)}, u32[]{:S(2)}, u32[]{:S(2)}) collective-permute-start(f32[64,128]{1,0:T(8,128)S(1)} %add.27), channel_id=1, source_target_pairs={{0,4},{4,0},{8,12},{12,8},{16,20},{20,16},{24,28},{28,24},{32,36},... | collective-permute-start | bytes 98312 | tf_op jit(solution)/shard_map/ppermute | solution.py:29
  15.9 3.1 %collective-permute-start.4 = (f32[64,128]{1,0:T(8,128)S(1)}, f32[64,128]{1,0:T(8,128)S(1)}, u32[]{:S(2)}, u32[]{:S(2)}) collective-permute-start(f32[64,128]{1,0:T(8,128)S(1)} %add.28), channel_id=1, source_target_pairs={{0,8},{4,12},{8,0},{12,4},{16,24},{20,28},{24,16},{28,20},{32,40},... | collective-permute-start | bytes 98312 | tf_op jit(solution)/shard_map/ppermute | solution.py:29
  16.5 5.8 %copy-start.1 = (bf16[128,4096]{1,0:T(8,128)(2,1)S(1)}, bf16[128,4096]{1,0:T(8,128)(2,1)}, u32[]{:S(2)}) copy-start(bf16[128,4096]{1,0:T(8,128)(2,1)} %sources_ref.1) | copy-start | bytes 3145732
  16.5 5.8 %copy-start.3 = (s32[32,6]{0,1:T(8,128)S(1)}, s32[32,6]{0,1:T(8,128)}, u32[]{:S(2)}) copy-start(s32[32,6]{0,1:T(8,128)} %param.13) | copy-start | bytes 2308
  16.5 22.4 %slice-start.1 = ((s8[6291456]{0:T(1024)(128)(4,1)}), s8[2097152]{0:T(1024)(128)(4,1)S(1)}, s32[]{:S(2)}) async-start(s8[6291456]{0:T(1024)(128)(4,1)} %bitcast.66), calls=%async_computation.1 | async-start | bytes 4194304
  19.3 6.0 %collective-permute-start.5 = (f32[64,128]{1,0:T(8,128)S(1)}, f32[64,128]{1,0:T(8,128)S(1)}, u32[]{:S(2)}, u32[]{:S(2)}) collective-permute-start(f32[64,128]{1,0:T(8,128)S(1)} %add.29), channel_id=1, source_target_pairs={{0,16},{4,20},{8,24},{12,28},{16,0},{20,4},{24,8},{28,12},{32,48},... | collective-permute-start | bytes 98312 | tf_op jit(solution)/shard_map/ppermute | solution.py:29
  25.5 9.4 %collective-permute-start.6 = (f32[64,128]{1,0:T(8,128)S(1)}, f32[64,128]{1,0:T(8,128)S(1)}, u32[]{:S(2)}, u32[]{:S(2)}) collective-permute-start(f32[64,128]{1,0:T(8,128)S(1)} %add.30), channel_id=1, source_target_pairs={{0,56},{4,60},{8,48},{12,52},{16,40},{20,44},{24,32},{28,36},{32,2... | collective-permute-start | bytes 98312 | tf_op jit(solution)/shard_map/ppermute | solution.py:29
  28.7 11.1 %collective-permute-start.10 = (bf16[128,512]{1,0:T(8,128)(2,1)S(1)}, bf16[128,512]{1,0:T(8,128)(2,1)S(1)}, u32[]{:S(2)}, u32[]{:S(2)}) collective-permute-start(bf16[128,512]{1,0:T(8,128)(2,1)S(1)} %get-tuple-element.88), channel_id=1, source_target_pairs={{1,2},{3,4},{5,6},{7,8},{9,10},{11,12},{13,14},{15,16},{17,18},{19... | collective-permute-start | bytes 393224 | tf_op jit(solution)/shard_map/ppermute | solution.py:40
  35.2 6.4 %collective-permute-start.7 = (f32[64,128]{1,0:T(8,128)S(1)}, f32[64,128]{1,0:T(8,128)S(1)}, u32[]{:S(2)}, u32[]{:S(2)}) collective-permute-start(f32[64,128]{1,0:T(8,128)S(1)} %add.31), channel_id=1, source_target_pairs={{0,64},{4,68},{8,72},{12,76},{16,80},{20,84},{24,88},{28,92},{32,9... | collective-permute-start | bytes 98312 | tf_op jit(solution)/shard_map/ppermute | solution.py:29
  36.5 5.1 %collective-permute-start.8 = (f32[64,128]{1,0:T(8,128)S(1)}, f32[64,128]{1,0:T(8,128)S(1)}, u32[]{:S(2)}, u32[]{:S(2)}) collective-permute-start(f32[64,128]{1,0:T(8,128)S(1)} %add.31), channel_id=1, source_target_pairs={{0,192},{4,196},{8,200},{12,204},{16,208},{20,212},{24,216},{28,22... | collective-permute-start | bytes 98312 | tf_op jit(solution)/shard_map/ppermute | solution.py:29
  38.3 4.3 %collective-permute-start.9 = (f32[64,128]{1,0:T(8,128)S(1)}, f32[64,128]{1,0:T(8,128)S(1)}, u32[]{:S(2)}, u32[]{:S(2)}) collective-permute-start(f32[64,128]{1,0:T(8,128)S(1)} %add.31), channel_id=1, source_target_pairs={{0,128},{4,132},{8,136},{12,140},{16,144},{20,148},{24,152},{28,15... | collective-permute-start | bytes 98312 | tf_op jit(solution)/shard_map/ppermute | solution.py:29
  39.8 2.8 %copy-start.2 = (bf16[32,64,128]{2,1,0:T(8,128)(2,1)S(1)}, bf16[32,64,128]{2,1,0:T(8,128)(2,1)}, u32[]{:S(2)}) copy-start(bf16[32,64,128]{2,1,0:T(8,128)(2,1)} %refs_9_.1) | copy-start | bytes 1572868
